TPU v7x, 32 devices: a whole 2x2x4 slice. The times are simulated.
32 devices in a mesh: groups: 2 (over y), seq: 4 (over x, core), role: 4 (over z).
Axes of the slice: x: 2, y: 2, z: 4, core: 2. Of those that a mesh axis runs over, the one named last changes fastest.
Arguments:
- query_rows: bfloat16 [8, 256, 4096], P('groups', 'seq', 'role'), parts along dimension 0, may hold values from -6 to 6
- encoded_key_rows: bfloat16 [8, 256, 512], P('groups', ('seq', 'role')), parts along dimension 0, may hold values from -6 to 6
- value_matrix_rows: bfloat16 [8, 256, 512], P('groups', ('seq', 'role')), parts along dimension 0, may hold values from -6 to 6
- output_weight: bfloat16 [4096, 2048], P('role', 'seq'), may hold values from -0.09375 to 0.09375
- residual: bfloat16 [8, 256, 2048], P(('groups', 'role'), 'seq'), parts along dimension 0, may hold values from -7.5 to 7.5
- norm_gain: float32 [2048], replicated, may hold values from 0.5 to 1.5
- route_experts: int32 [8, 256, 8], P(('groups', 'role'), 'seq'), parts along dimension 0, may hold values from 0 to 15, all different within a row; in each aligned block of 64 rows (0 to 63, 64 to 127, ..., all dimensions but the last counted through in order) at most 33 rows name the same one
- route_gates: float32 [8, 256, 8], P(('groups', 'role'), 'seq'), parts along dimension 0, may hold values from 0.05 to 0.3
- gate_weight: bfloat16 [16, 2048, 768], P(('seq', 'role')), may hold values from -0.125 to 0.125
- up_weight: bfloat16 [16, 2048, 768], P(('seq', 'role')), may hold values from -0.125 to 0.125
- down_weight: bfloat16 [16, 768, 2048], P(('seq', 'role')), may hold values from -0.21875 to 0.21875
Outputs:
- layer_output: bfloat16 [8, 256, 2048], P(('groups', 'role'), 'seq'), parts along dimension 0
There are 2 independent parts, one for each index of `groups`. A program takes and returns all parts, laid end to end along the dimension named above; an argument that names none is the same for every part. Nothing has to cross between parts.
Inputs may be any that keep to these rules, and one draw needn't show every extreme that they name: `route_experts`: each token names 8 different experts. Within the 64 positions of one sequence that one index of seq holds, no expert is named by more than 33 routes, and in every draw some expert is named by exactly 33 routes in some such block.
All inputs are finite; a program needn't handle non-finite values.
Results may differ from a plain program's by a relative error of at most 0.014.
Values may be sent and summed in bfloat16 or wider, within the bound.
No kernel may reach another device: no remote copies, remote signals or barrier semaphores. Data moves between devices by JAX's collectives and lax.ppermute only.
A program may use at most 128 MiB of HBM per device.

v0:
```python
from functools import partial

import jax
import jax.numpy as jnp
from jax import lax
from jax.experimental import pallas as pl
from jax.experimental.pallas import tpu as pltpu
from jax.sharding import PartitionSpec as P

D = 2048
QUERY_HEADS = 32
KEY_VALUE_HEADS = 4
HEAD_WIDTH = 128
TOPK = 8


epsilon = 1e-06
masked_score = -1e30
EXPERT_VMEM = 16 * 2**20
SMALL_VMEM = 12 * 2**20
COPY_VMEM = 4 * 2**20
GATE_COLUMNS = 128
LOG2_E = 1.4426950408889634
NOTHING = pl.CostEstimate(flops=1, bytes_accessed=1, transcendentals=0)
SHORT = pl.CostEstimate(flops=2 * 10**9, bytes_accessed=4 * 2**20, transcendentals=0)
LONG = pl.CostEstimate(flops=10**10, bytes_accessed=1, transcendentals=0)


def score_block(queries, every_key, query_position, block_start, block_width, score_scale):
    keys_part = lax.slice_in_dim(every_key, block_start, block_start + block_width, axis=0)
    raw_scores = (
        jnp.einsum("qhd,kd->hqk", queries, keys_part, preferred_element_type=jnp.float32)
        * score_scale
    )
    key_position = block_start + jnp.arange(block_width, dtype=jnp.int32)
    return jnp.where(
        key_position[None, None, :] <= query_position[None, :, None], raw_scores, masked_score
    )


def value_block(rounded, every_value, block_start, block_width):
    prob_block = lax.slice_in_dim(rounded, block_start, block_start + block_width, axis=2)
    values_part = lax.slice_in_dim(every_value, block_start, block_start + block_width, axis=0)
    return jnp.einsum("hqk,kd->qhd", prob_block, values_part, preferred_element_type=jnp.float32)


def routed_shards(
    query_rows,
    encoded_key_rows,
    value_matrix_rows,
    output_weight,
    residual,
    norm_gain,
    route_experts,
    route_gates,
    gate_weight,
    up_weight,
    down_weight,
):
    seq_count = lax.axis_size("seq")
    role_count = lax.axis_size("role")
    seq_index = lax.axis_index("seq")
    role_index = lax.axis_index("role")
    batch_count = query_rows.shape[0]
    local_length = query_rows.shape[1]
    local_heads = query_rows.shape[2] // HEAD_WIDTH
    full_length = local_length * seq_count
    query_group_width = QUERY_HEADS // KEY_VALUE_HEADS
    head_pick = role_index * local_heads // query_group_width
    role_keys, role_values = (
        lax.all_gather(encoded_key_rows, "role", axis=1, tiled=True),
        lax.all_gather(value_matrix_rows, "role", axis=1, tiled=True),
    )
    head_keys = lax.dynamic_slice_in_dim(role_keys, head_pick * HEAD_WIDTH, HEAD_WIDTH, 2)
    head_values = lax.dynamic_slice_in_dim(role_values, head_pick * HEAD_WIDTH, HEAD_WIDTH, 2)
    whole_keys, whole_values, whole_proj = (
        lax.all_gather(head_keys, "seq", axis=1, tiled=True),
        lax.all_gather(head_values, "seq", axis=1, tiled=True),
        lax.all_gather(output_weight, "seq", axis=1, tiled=True),
    )
    key_width = full_length // 8
    score_scale = HEAD_WIDTH ** (-0.5)
    query_position = seq_index * local_length + jnp.arange(local_length, dtype=jnp.int32)
    last_needed = (seq_index + 1) * local_length

    def one_sequence(operands):
        own_queries, every_key, every_value = operands
        queries = own_queries.reshape(local_length, local_heads, HEAD_WIDTH)
        pieces = []
        for number in range(8):
            block_start = number * key_width
            compute = partial(
                score_block, queries, every_key, query_position, block_start, key_width, score_scale
            )
            skipped = partial(
                jnp.full, (local_heads, local_length, key_width), masked_score, jnp.float32
            )
            pieces.append(lax.cond(block_start < last_needed, compute, skipped))
        scores = jnp.concatenate(pieces, axis=2)
        row_peak = jnp.max(scores, axis=2, keepdims=True)
        weights = jnp.exp(scores - row_peak)
        totals = jnp.sum(weights, axis=2, keepdims=True)
        rounded = weights.astype(jnp.bfloat16)
        mixed_rows = jnp.zeros((local_length, local_heads, HEAD_WIDTH), jnp.float32)
        for number in range(8):
            block_start = number * key_width
            product = partial(value_block, rounded, every_value, block_start, key_width)
            nothing = partial(jnp.zeros, (local_length, local_heads, HEAD_WIDTH), jnp.float32)
            mixed_rows = mixed_rows + lax.cond(block_start < last_needed, product, nothing)
        attended = (mixed_rows / totals.transpose(1, 0, 2)).astype(jnp.bfloat16)
        return attended.reshape(local_length, local_heads * HEAD_WIDTH)

    attended = lax.map(one_sequence, (query_rows, whole_keys, whole_values))
    flat_attended = attended.reshape(batch_count * local_length, local_heads * HEAD_WIDTH)
    projected = lax.psum_scatter(
        jnp.dot(flat_attended, whole_proj, preferred_element_type=jnp.float32).astype(jnp.bfloat16),
        "role",
        scatter_dimension=0,
        tiled=True,
    ).astype(jnp.float32)
    hidden = residual[0].astype(jnp.float32) + projected
    variance = jnp.mean(hidden * hidden, axis=-1, keepdims=True)
    normed = (hidden * lax.rsqrt(variance + epsilon) * norm_gain).astype(jnp.bfloat16)
    expert_ids = route_experts.reshape(-1)
    gate_values = route_gates.reshape(-1)
    experts_local = gate_weight.shape[0]
    device_count = seq_count * role_count
    expert_count = experts_local * device_count
    assign = expert_ids.shape[0]
    capacity = assign // expert_count + 1
    onehot = (expert_ids[:, None] == jnp.arange(expert_count, dtype=jnp.int32)[None, :]).astype(
        jnp.int32
    )
    earlier = jnp.cumsum(onehot, axis=0) - onehot
    slot_rank = jnp.sum(earlier * onehot, axis=1)
    slot_index = expert_ids * capacity + slot_rank
    source_token = jnp.arange(assign, dtype=jnp.int32) // TOPK
    slot_token = jnp.zeros((expert_count * capacity,), jnp.int32).at[slot_index].set(source_token)
    slot_used = jnp.zeros((expert_count * capacity,), jnp.bfloat16).at[slot_index].set(1.0)
    outgoing = (normed[slot_token] * slot_used[:, None]).reshape(
        device_count, experts_local, capacity, D
    )
    incoming = lax.all_to_all(outgoing, ("seq", "role"), split_axis=0, concat_axis=0, tiled=True)
    gate_hidden = jnp.einsum(
        "sjcd,jdf->sjcf", incoming, gate_weight, preferred_element_type=jnp.float32
    )
    up_hidden = jnp.einsum(
        "sjcd,jdf->sjcf", incoming, up_weight, preferred_element_type=jnp.float32
    )
    activated = (jax.nn.silu(gate_hidden) * up_hidden).astype(jnp.bfloat16)
    returned = lax.all_to_all(
        jnp.einsum(
            "sjcf,jfd->sjcd", activated, down_weight, preferred_element_type=jnp.float32
        ).astype(jnp.bfloat16),
        ("seq", "role"),
        split_axis=0,
        concat_axis=0,
        tiled=True,
    )
    gathered = returned.reshape(expert_count * capacity, D)[slot_index]
    weighted = gathered.astype(jnp.float32) * gate_values[:, None]
    expert_sum = jnp.sum(weighted.reshape(-1, TOPK, D), axis=1)
    return (hidden + expert_sum).astype(jnp.bfloat16).reshape(residual.shape)


def in_hbm(*arrays):
    return [pltpu.with_memory_space_constraint(array, pltpu.HBM) for array in arrays]


def hbm_specs(count):
    return [pl.BlockSpec(memory_space=pltpu.HBM)] * count


def fetch_scratch(*arrays):
    return [pltpu.VMEM(array.shape, array.dtype) for array in arrays] + [
        pltpu.SemaphoreType.DMA((len(arrays),))
    ]


def start_fetch(from_refs, scratch):
    *buffers, sems = scratch
    copies = [
        pltpu.make_async_copy(from_ref, buffer, sems.at[n])
        for n, (from_ref, buffer) in enumerate(zip(from_refs, buffers))
    ]
    for copy in copies:
        copy.start()
    return copies, buffers


def in_vmem(count):
    return [pl.BlockSpec(memory_space=pltpu.VMEM)] * count


def attend_kernel(seq_count, role_count, slots, groups, at_ref, *refs):
    last_block, *refs = refs
    count = seq_count + 2
    attended_ref, *partial_refs = refs[count : count + 1 + len(groups)]
    copies, (query_ref, *buffers) = start_fetch(refs[:count], refs[count + 1 + len(groups) :])
    blocks, proj_refs = buffers[: seq_count - 1] + [last_block], buffers[seq_count - 1 :]
    seq_index, role_index = at_ref[0], at_ref[1]
    local_length = query_ref.shape[1]
    local_heads = query_ref.shape[2] // HEAD_WIDTH
    per_role = local_length // role_count
    rows = local_heads * local_length
    keys_all = seq_count * local_length
    slot = lax.broadcasted_iota(jnp.int32, (rows, keys_all), 1)
    block_number, within = slot // local_length, slot % local_length
    key_position = (
        (seq_index ^ block_number) * local_length
        + (role_index ^ (within // per_role)) * per_role
        + within % per_role
    )
    query_position = (
        seq_index * local_length
        + lax.broadcasted_iota(jnp.int32, (rows, keys_all), 0) % local_length
    )
    seen = key_position <= query_position
    scale = HEAD_WIDTH ** (-0.5) * LOG2_E
    for copy in copies[:seq_count]:
        copy.wait()
    for n, k in enumerate(slots):
        b = role_index ^ k
        own = query_ref[b]
        queries = jnp.concatenate(
            [own[:, h * HEAD_WIDTH : (h + 1) * HEAD_WIDTH] for h in range(local_heads)], axis=0
        )
        key_value = jnp.concatenate([block[b] for block in blocks], axis=0)
        keys, values = key_value[:, :HEAD_WIDTH], key_value[:, HEAD_WIDTH:]
        scores = lax.dot_general(
            queries, keys, (((1,), (1,)), ((), ())), preferred_element_type=jnp.float32
        )
        scores = jnp.where(seen, scores * scale, masked_score)
        weights = jnp.exp2(scores - jnp.max(scores, axis=1, keepdims=True))
        totals = jnp.sum(weights, axis=1, keepdims=True)
        mixed = jnp.dot(weights.astype(jnp.bfloat16), values, preferred_element_type=jnp.float32)
        attended = (mixed * (1.0 / totals)).astype(jnp.bfloat16)
        for h in range(local_heads):
            attended_ref[
                n * local_length : (n + 1) * local_length, h * HEAD_WIDTH : (h + 1) * HEAD_WIDTH
            ] = attended[h * local_length : (h + 1) * local_length]
    for copy in copies[seq_count:]:
        copy.wait()
    project_into(slots, groups, attended_ref, proj_refs, partial_refs)


def join_kernel(*refs):
    *piece_refs, out_ref = refs
    at = 0
    for ref in piece_refs:
        size = ref.shape[1]
        out_ref[:, at : at + size, :] = ref[...]
        at += size


def role_groups(role_count):
    last = role_count // 2
    bits = [1 << n for n in range(last.bit_length() - 1)]
    return [[k for k in range(role_count) if k & -k == bit] for bit in bits] + [[0, last]]


def project_into(slots, groups, attended_ref, proj_refs, partial_refs):
    slots = list(slots)
    rows = attended_ref.shape[0] // len(slots)
    at = 0
    for proj_ref in proj_refs:
        width = proj_ref.shape[1]
        product = jnp.dot(
            attended_ref[...], proj_ref[...], preferred_element_type=jnp.float32
        ).astype(jnp.bfloat16)
        for group, partial_ref in zip(groups, partial_refs):
            for n, k in enumerate(group):
                start = slots.index(k) * rows
                partial_ref[n * rows : (n + 1) * rows, at : at + width] = product[
                    start : start + rows
                ]
        at += width


def project_kernel(slots, groups, attended_ref, order_ref, *refs):
    count = (len(refs) - len(groups) - 1) // 2
    copies, proj_refs = start_fetch(refs[:count], refs[count + len(groups) :])
    for copy in copies:
        copy.wait()
    project_into(slots, groups, attended_ref, proj_refs, refs[count : count + len(groups)])


def partial_shapes(groups, rows, width):
    return [jax.ShapeDtypeStruct((rows * len(group), width), jnp.bfloat16) for group in groups]


def near_sum_kernel(route_ref, other_route_ref, came_ref, sent_any, *refs):
    out_refs, both_ref = refs[:2], refs[2]
    copies, (sent,) = start_fetch([sent_any], refs[3:])
    rows, width = sent.shape[0] // 2, sent.shape[1]
    lane = lax.broadcasted_iota(jnp.int32, (rows, GATE_COLUMNS), 1)
    half = GATE_COLUMNS // 2
    expert = (lane % half).astype(jnp.float32)
    for p, routes in enumerate((route_ref, other_route_ref)):
        shares = jnp.zeros((rows, GATE_COLUMNS), jnp.float32)
        routed = routes.shape[1] // 2
        for k in range(routed):
            named, weight = routes[:, k : k + 1], routes[:, routed + k : routed + k + 1]
            shares = shares + jnp.where(expert == named, weight, 0.0)
        first = shares.astype(jnp.bfloat16).astype(jnp.float32)
        terms = jnp.where(lane < half, first, shares - first).astype(jnp.bfloat16)
        out_refs[p][:, width:] = terms
        both_ref[p * rows : (p + 1) * rows, width:] = terms
    copies[0].wait()
    for p in range(2):
        total = sent[p * rows : (p + 1) * rows].astype(jnp.float32)
        total = total + came_ref[(1 - p) * rows : (2 - p) * rows].astype(jnp.float32)
        out_refs[p][:, :width] = total.astype(jnp.bfloat16)
        both_ref[p * rows : (p + 1) * rows, :width] = total.astype(jnp.bfloat16)


def far_sum_kernel(rows, order_count, *refs):
    refs = refs[order_count:]
    chips = (len(refs) - 4) // 3
    came_refs, sent_any = refs[:chips], refs[chips : 2 * chips]
    own_ref, other_ref, both_ref = refs[2 * chips : 2 * chips + 3]
    copies, sent_refs = start_fetch(sent_any, refs[2 * chips + 3 :])
    for copy in copies:
        copy.wait()
    size = chips * rows
    for n, (sent, came) in enumerate(zip(sent_refs, came_refs)):
        to = slice(n * rows, (n + 1) * rows)
        for p, out_ref in enumerate((own_ref, other_ref)):
            total = sent[p * rows : (p + 1) * rows].astype(jnp.float32)
            total = total + came[(1 - p) * rows : (2 - p) * rows].astype(jnp.float32)
            out_ref[to] = total.astype(jnp.bfloat16)
            both_ref[p * size + n * rows : p * size + (n + 1) * rows] = total.astype(jnp.bfloat16)


def norm_kernel(chips, near_row, far_row, at_ref, gain_ref, *refs):
    parts, (normed_ref, *hidden_refs, whole_ref) = refs[: 2 * chips], refs[2 * chips :]
    seq_index = at_ref[0]
    features = whole_ref.shape[1]
    rows = whole_ref.shape[0] // chips
    width = features // chips // 2
    for n in range(chips):
        near, far = parts[2 * n : 2 * n + 2]
        for m in range(chips):
            part = far if m else near
            first = ((far_row if m else near_row) if n else 0) + (m - 1 if m else 0) * rows
            to = slice((n ^ m) * rows, ((n ^ m) + 1) * rows)
            for j in range(2):
                start = pl.multiple_of((seq_index ^ (2 * n + j)) * width, width)
                whole_ref[to, pl.ds(start, width)] = part[
                    first : first + rows, j * width : (j + 1) * width
                ].astype(jnp.float32)
        first = near_row if n else 0
        normed_ref[n * rows : (n + 1) * rows, features:] = near[first : first + rows, 2 * width :]
    hidden = whole_ref[...]
    variance = jnp.mean(hidden * hidden, axis=1, keepdims=True)
    normed = hidden * lax.rsqrt(variance + epsilon) * gain_ref[...]
    normed_ref[:, :features] = normed.astype(jnp.bfloat16)
    for hidden_ref in hidden_refs:
        hidden_ref[...] = hidden[:rows]


def expert_kernel(token_count, at_ref, *refs):
    token_refs = refs[:token_count]
    gate_ref, up_ref, down_ref, keep_ref, send_ref, activated_ref = refs[token_count:]
    features, units = gate_ref.shape[1:]
    tokens = jnp.concatenate([ref[:, :features] for ref in token_refs], axis=0)
    gates = jnp.concatenate([ref[:, features:] for ref in token_refs], axis=0)
    lane = lax.broadcasted_iota(jnp.int32, gates.shape, 1)
    mine = lane % (GATE_COLUMNS // 2) == at_ref[2]
    share = jnp.sum(jnp.where(mine, gates.astype(jnp.float32), 0.0), axis=1, keepdims=True)
    block = units
    for f in range(0, units, block):
        gate_hidden = jnp.dot(
            tokens, gate_ref[0, :, f : f + block], preferred_element_type=jnp.float32
        )
        up_hidden = jnp.dot(tokens, up_ref[0, :, f : f + block], preferred_element_type=jnp.float32)
        activated_ref[:, f : f + block] = (
            gate_hidden / (1.0 + jnp.exp(-gate_hidden)) * up_hidden
        ).astype(jnp.bfloat16)
    kept = keep_ref.shape[0]
    block = 1024 if features % 1024 == 0 else features
    for c in range(0, features, block):
        product = jnp.dot(
            activated_ref[...], down_ref[0, :, c : c + block], preferred_element_type=jnp.float32
        )
        product = (product * share).astype(jnp.bfloat16)
        keep_ref[:, c : c + block] = product[:kept]
        send_ref[:, c : c + block] = product[kept:]


def run_expert(at, tokens, gate_weight, up_weight, down_weight):
    units = gate_weight.shape[2]
    width = gate_weight.shape[1]
    rows = sum(part.shape[0] for part in tokens)
    half = jax.ShapeDtypeStruct((rows // 2, width), jnp.bfloat16)
    return pl.pallas_call(
        partial(expert_kernel, len(tokens)),
        in_specs=[pl.BlockSpec(memory_space=pltpu.SMEM)] + in_vmem(len(tokens) + 3),
        out_specs=in_vmem(2),
        out_shape=[half, half],
        scratch_shapes=[pltpu.VMEM((rows, units), jnp.bfloat16)],
        compiler_params=pltpu.CompilerParams(vmem_limit_bytes=EXPERT_VMEM),
        cost_estimate=NOTHING,
    )(at, *tokens, gate_weight, up_weight, down_weight)


def after(array, *others):
    return lax.optimization_barrier((array, *others))[0]


def added(terms):
    total = terms[0].astype(jnp.float32)
    for term in terms[1:]:
        total = total + term.astype(jnp.float32)
    return total


def gathered_shards(
    query_rows,
    encoded_key_rows,
    value_matrix_rows,
    output_weight,
    residual,
    norm_gain,
    route_experts,
    route_gates,
    gate_weight,
    up_weight,
    down_weight,
):
    seq_count = lax.axis_size("seq")
    role_count = lax.axis_size("role")
    seq_index = lax.axis_index("seq")
    role_index = lax.axis_index("role")
    batch_count, local_length, query_width = query_rows.shape
    local_heads = query_width // HEAD_WIDTH
    group_width = QUERY_HEADS // KEY_VALUE_HEADS
    role_bits = [1 << n for n in range(role_count.bit_length() - 1)]
    at = jnp.stack([seq_index, role_index, seq_index * role_count + role_index]).astype(jnp.int32)

    def over_role(array, k):
        return lax.ppermute(array, "role", [(i, i ^ k) for i in range(role_count)])

    def over_seq(array, j):
        return lax.ppermute(array, "seq", [(i, i ^ j) for i in range(seq_count)])

    beside_proj = over_seq(output_weight, 1)
    block_width = output_weight.shape[1]
    across_steps = range(2, seq_count, 2)

    pieces = []
    for k in range(role_count):
        head = ((role_index ^ k) * local_heads // group_width) * HEAD_WIDTH
        piece = jnp.concatenate(
            [
                lax.dynamic_slice_in_dim(encoded_key_rows, head, HEAD_WIDTH, 2),
                lax.dynamic_slice_in_dim(value_matrix_rows, head, HEAD_WIDTH, 2),
            ],
            axis=2,
        )
        pieces.append(piece)
    pieces[1] = after(pieces[1], beside_proj)
    pieces = [piece if k == 0 else over_role(piece, k) for k, piece in enumerate(pieces)]
    block = pl.pallas_call(
        join_kernel,
        in_specs=in_vmem(len(pieces)),
        out_specs=pl.BlockSpec(memory_space=pltpu.VMEM),
        out_shape=jax.ShapeDtypeStruct(
            (batch_count, local_length, 2 * HEAD_WIDTH), jnp.bfloat16
        ),
        compiler_params=pltpu.CompilerParams(vmem_limit_bytes=COPY_VMEM),
        cost_estimate=SHORT,
    )(*pieces)
    same_core = [block] + [over_seq(block, j) for j in across_steps]
    blocks = []
    for part in same_core:
        blocks += [part, over_seq(part, 1)]
    last = role_count // 2
    routes = jnp.concatenate([route_experts[0].astype(jnp.float32), route_gates[0]], axis=1)
    residual_blocks = [
        lax.dynamic_slice_in_dim(residual[0], (seq_index ^ j) * block_width, block_width, 1)
        for j in range(seq_count)
    ]
    residuals = [
        jnp.concatenate(residual_blocks[j : j + 2], axis=1) for j in range(0, seq_count, 2)
    ]

    rows = batch_count * local_length
    near_width = 2 * output_weight.shape[1]
    groups = role_groups(role_count)
    attend_args = in_hbm(query_rows, *blocks[:-1], output_weight, beside_proj)
    slot_sets = [(range(1, role_count, 2), groups[:1]), (range(0, role_count, 2), groups[1:])]
    attended, near = [], []
    for slots, parts in slot_sets:
        half_rows = jax.ShapeDtypeStruct((rows // 2, query_width), jnp.bfloat16)
        half, *partials = pl.pallas_call(
            partial(attend_kernel, seq_count, role_count, slots, parts),
            in_specs=[pl.BlockSpec(memory_space=pltpu.SMEM)]
            + in_vmem(1)
            + hbm_specs(len(attend_args)),
            out_specs=in_vmem(1 + len(parts)),
            out_shape=[half_rows] + partial_shapes(parts, local_length, near_width),
            scratch_shapes=fetch_scratch(*attend_args),
            compiler_params=pltpu.CompilerParams(vmem_limit_bytes=SMALL_VMEM),
            cost_estimate=SHORT,
        )(at, blocks[-1], *attend_args)
        attended.append(half)
        near += partials

    for j in across_steps:
        residuals[j // 2] = over_seq(after(residuals[j // 2], attended[1]), j)
    other_routes = over_role(routes, last)

    def summed_over_role(parts, extra, *before):
        terms = [[part] for part in parts]
        for n, group in enumerate(groups[:-1]):
            bit = 1 << n
            leaving = terms[n][0] if len(terms[n]) == 1 else added(terms[n]).astype(jnp.bfloat16)
            came = over_role(leaving, bit)
            for m in range(n + 1, len(groups)):
                at_rows = [group.index(k ^ bit) for k in groups[m]]
                if at_rows == list(range(len(group))):
                    terms[m].append(came)
                else:
                    split = [came[i * local_length : (i + 1) * local_length] for i in at_rows]
                    terms[m].append(jnp.concatenate(split, axis=0))
        extra = jnp.pad(after(extra, *before) if before else extra, ((0, local_length), (0, 0)))
        sent = added(terms[-1] + [extra]).astype(jnp.bfloat16)
        return sent

    near_sent = summed_over_role(near, residuals[0])
    near_came = over_role(near_sent, last)
    near_args = in_hbm(near_sent)
    own_shape, both_shape = [
        jax.ShapeDtypeStruct((size, near_width + GATE_COLUMNS), jnp.bfloat16)
        for size in (local_length, 2 * local_length)
    ]
    near_halves = pl.pallas_call(
        near_sum_kernel,
        in_specs=in_vmem(3) + hbm_specs(1),
        out_specs=in_vmem(3),
        out_shape=[own_shape, own_shape, both_shape],
        scratch_shapes=fetch_scratch(*near_args),
        compiler_params=pltpu.CompilerParams(vmem_limit_bytes=SMALL_VMEM),
        cost_estimate=LONG,
    )(routes, other_routes, near_came, *near_args)

    def walk(k, bits):
        found = [k]
        for n, bit in enumerate(bits):
            found += walk(k | bit, bits[n + 1 :])
        return found

    lower_bits = role_bits[:-1][::-1]
    order = walk(last, lower_bits) + walk(0, lower_bits)
    far_plane, final = order[1], order[-1]

    def across(part):
        return [over_seq(part, j) for j in across_steps]

    def spread(own, other, both, ordered):
        planes, crossed = {0: own, last: other}, {}
        both_across = across(both)
        size = own.shape[0]
        for k in order:
            if k not in planes:
                bit = k & -k
                held = planes[k ^ bit]
                wait = ordered and k < last
                planes[k] = over_role(after(held, planes[far_plane]) if wait else held, bit)
            if k in (0, last):
                crossed[k] = both_across
            elif k < last:
                source = k ^ (k & -k)
                came = [part[:size] for part in crossed[source]] if source == 0 else crossed[source]
                crossed[k] = [over_role(part, k & -k) for part in came]
            else:
                crossed[k] = across(after(planes[k], *both_across))
        return planes, crossed

    near_planes, near_crossed = spread(*near_halves, False)

    sent, came = [], []
    for n, j in enumerate(across_steps, 1):
        far = []
        for half, (slots, parts) in zip(attended, slot_sets):
            far += pl.pallas_call(
                partial(project_kernel, slots, parts),
                in_specs=in_vmem(1) + [pl.BlockSpec(memory_space=pl.ANY)] + hbm_specs(2),
                out_specs=in_vmem(len(parts)),
                out_shape=partial_shapes(parts, local_length, near_width),
                scratch_shapes=fetch_scratch(output_weight, beside_proj),
                compiler_params=pltpu.CompilerParams(vmem_limit_bytes=SMALL_VMEM),
                cost_estimate=SHORT,
            )(over_seq(half, j), other_routes, *in_hbm(output_weight, beside_proj))
        sent.append(summed_over_role(far, residuals[n], near_halves[0]))
        came.append(over_role(sent[-1], last))

    chips = 1 + len(across_steps)
    far_args = in_hbm(*sent)
    far_rows = (chips - 1) * local_length
    far_shape, far_both_shape = [
        jax.ShapeDtypeStruct((size, near_width), jnp.bfloat16) for size in (far_rows, 2 * far_rows)
    ]
    first_come = [*near_crossed[0], near_planes[far_plane], *near_crossed[far_plane]]
    first_come.append(near_planes[final])
    far_halves = pl.pallas_call(
        partial(far_sum_kernel, local_length, len(first_come)),
        in_specs=[pl.BlockSpec(memory_space=pl.ANY)] * len(first_come)
        + in_vmem(len(came))
        + hbm_specs(len(far_args)),
        out_specs=in_vmem(3),
        out_shape=[far_shape, far_shape, far_both_shape],
        scratch_shapes=fetch_scratch(*far_args),
        compiler_params=pltpu.CompilerParams(vmem_limit_bytes=SMALL_VMEM),
        cost_estimate=SHORT,
    )(*first_come, *came, *far_args)
    far_own, far_other, far_both = far_halves
    far_other = after(far_other, *near_crossed[final])
    far_planes, far_crossed = spread(far_own, far_other, far_both, True)

    width = residual.shape[2]
    gain = norm_gain.reshape(1, width)

    def normed_rows(parts, second, *hidden_shape):
        rows = chips * local_length
        firsts = (local_length, far_rows) if second else (0, 0)
        return pl.pallas_call(
            partial(norm_kernel, chips, *firsts),
            in_specs=[pl.BlockSpec(memory_space=pltpu.SMEM)] + in_vmem(1 + 2 * chips),
            out_specs=in_vmem(1 + len(hidden_shape)),
            out_shape=[
                jax.ShapeDtypeStruct((rows, width + GATE_COLUMNS), jnp.bfloat16),
                *hidden_shape,
            ],
            scratch_shapes=[pltpu.VMEM((rows, width), jnp.float32)],
            compiler_params=pltpu.CompilerParams(vmem_limit_bytes=SMALL_VMEM),
            cost_estimate=NOTHING,
        )(at, gain, *parts)

    keep, send, slots, leaving, passed = {}, {}, {}, {}, {}

    hidden_shape = jax.ShapeDtypeStruct((local_length, width), jnp.float32)
    hidden = []

    hidden_shape = jax.ShapeDtypeStruct((local_length, width), jnp.float32)
    hidden = []

    def prepared(k, *first):
        late = far_crossed[k]
        if first:
            late = [after(part, *first) for part in late]
        parts = [near_planes[k], far_planes[k]]
        for pair in zip(near_crossed[k], late):
            parts += pair
        normed, *own = normed_rows(parts, k == last, *([] if k else [hidden_shape]))
        hidden.extend(own)
        return [normed, over_seq(normed, 1)]

    def expert(tokens, *others):
        if others:
            tokens = lax.optimization_barrier((*tokens, *others))[: len(tokens)]
        return run_expert(at, tokens, gate_weight, up_weight, down_weight)

    def combine(k, *before):
        came = over_seq(after(send[k], *before) if before else send[k], 1)
        sums = []
        for n in range(len(across_steps)):
            chunk = slice((n + 1) * local_length, (n + 2) * local_length)
            sums.append(added([keep[k][chunk], came[chunk]]).astype(jnp.bfloat16))
        return [keep[k][:local_length], came[:local_length]], sums

    def pass_on(k):
        passed[k] = [over_seq(part, j) for part, j in zip(leaving[k], across_steps)]
        slots[k] += passed[k]

    ready = {far_plane: prepared(far_plane, far_planes[final], *far_crossed[final])}
    ready[final] = prepared(final)
    keep[far_plane], send[far_plane] = expert(ready[far_plane], ready[final][0])
    ready |= {k: prepared(k, keep[far_plane]) for k in (last, 0)}
    slots[far_plane], leaving[far_plane] = combine(far_plane)
    leaving[far_plane] = [after(part, ready[last][0], ready[0][0]) for part in leaving[far_plane]]
    pass_on(far_plane)
    keep[last], send[last] = expert(ready[last], keep[far_plane], *leaving[far_plane])
    slots[last], leaving[last] = combine(last)
    leaving[last] = [after(part, *passed[far_plane]) for part in leaving[last]]
    pass_on(last)
    keep[final], send[final] = expert(ready[final], keep[last])
    slots[far_plane] = [added(slots[far_plane]).astype(jnp.bfloat16)]
    slots[final], leaving[final] = combine(final, *passed[far_plane])
    leaving[final] = [after(part, *leaving[last]) for part in leaving[final]]
    pass_on(final)
    keep[0], send[0] = expert(ready[0], keep[final], *leaving[last])
    slots[0], leaving[0] = combine(0, *passed[last])
    leaving[0] = [after(part, *leaving[final]) for part in leaving[0]]
    pass_on(0)
    for bit in role_bits:
        for k in [k for k in sorted(slots, reverse=True) if k & bit]:
            going = added(slots.pop(k)).astype(jnp.bfloat16)
            if k == last:
                going = after(going, *leaving[final])
            slots[k ^ bit].append(over_role(going, bit))
    return added(hidden + slots[0]).astype(jnp.bfloat16).reshape(residual.shape)


def solution(mesh):
    placed = (
        P("groups", "seq", "role"),
        P("groups", ("seq", "role"), None),
        P("groups", ("seq", "role"), None),
        P("role", "seq"),
        P(("groups", "role"), "seq", None),
        P(),
        P(("groups", "role"), "seq", None),
        P(("groups", "role"), "seq", None),
        P(("seq", "role"), None, None),
        P(("seq", "role"), None, None),
        P(("seq", "role"), None, None),
    )
    experts = mesh.shape["seq"] * mesh.shape["role"]
    return jax.shard_map(
        gathered_shards if experts <= 2 * TOPK else routed_shards,
        mesh=mesh,
        in_specs=placed,
        out_specs=P(("groups", "role"), "seq", None),
        check_vma=False,
    )
```

profile of v0, /device:TPU:0, one launch (start us, length us, event | category | flops | bytes accessed | tf_op | source)
XLA Modules:
  0.0 121.4 jit_solution(14514736271328517534)
XLA Ops:
  1.3 3.7 %collective-permute-start.3 = (bf16[4,16,256]{2,1,0:T(8,128)(2,1)S(1)}, bf16[4,16,256]{2,1,0:T(8,128)(2,1)S(1)}, u32[]{:S(2)}, u32[]{:S(2)}) collective-permute-start(bf16[4,16,256]{2,1,0:T(8,128)(2,1)S(1)} %pad_maximum_fusion.3), channel_id=1, source_target_pairs={{0,2},{1,3},{2,0},{3,1},{4,6},{5,7},{6,4},{7,5},{8,10},{9,11},{10,... | collective-permute-start | bytes 98312 | tf_op jit(solution)/shard_map/ppermute | solution.py:442
  5.0 1.3 %collective-permute-start.4 = (bf16[4,16,256]{2,1,0:T(8,128)(2,1)S(1)}, bf16[4,16,256]{2,1,0:T(8,128)(2,1)S(1)}, u32[]{:S(2)}, u32[]{:S(2)}) collective-permute-start(bf16[4,16,256]{2,1,0:T(8,128)(2,1)S(1)} %pad_maximum_fusion.4), channel_id=1, source_target_pairs={{0,3},{1,2},{2,1},{3,0},{4,7},{5,6},{6,5},{7,4},{8,11},{9,10},{10,... | collective-permute-start | bytes 98312 | tf_op jit(solution)/shard_map/ppermute | solution.py:442
  7.0 3.7 %collective-permute-done.4.refs_3_ = bf16[4,16,256]{2,1,0:T(8,128)(2,1)S(1)} collective-permute-done((bf16[4,16,256]{2,1,0:T(8,128)(2,1)S(1)}, bf16[4,16,256]{2,1,0:T(8,128)(2,1)S(1)}, u32[]{:S(2)}, u32[]{:S(2)}) %collective-permute-start.4) | collective-permute-done | bytes 32800 | tf_op jit(solution)/shard_map/ppermute | solution.py:442
  10.8 1.6 %collective-permute-start.5 = (bf16[4,64,256]{2,1,0:T(8,128)(2,1)S(1)}, bf16[4,64,256]{2,1,0:T(8,128)(2,1)S(1)}, u32[]{:S(2)}, u32[]{:S(2)}) collective-permute-start(bf16[4,64,256]{2,1,0:T(8,128)(2,1)S(1)} %shard_map.109.refs_2_), channel_id=1, source_target_pairs={{0,8},{4,12},{8,0},{12,4},{1,9},{5,13},{9,1},{13,5},{2,10},{6,14},... | collective-permute-start | bytes 393224 | tf_op jit(solution)/shard_map/ppermute | solution.py:445
  12.5 1.3 %collective-permute-start = (f32[64,16]{1,0:T(8,128)S(1)}, f32[64,16]{1,0:T(8,128)S(1)}, u32[]{:S(2)}, u32[]{:S(2)}) collective-permute-start(f32[64,16]{1,0:T(8,128)S(1)} %copy.15.route_ref), channel_id=1, source_target_pairs={{0,2},{1,3},{2,0},{3,1},{4,6},{5,7},{6,4},{7,5},{8,10},{9,11},{10,... | collective-permute-start | bytes 12296 | tf_op jit(solution)/shard_map/ppermute | solution.py:442
  13.7 2.1 %collective-permute-done.5.refs_4_ = bf16[4,64,256]{2,1,0:T(8,128)(2,1)S(1)} collective-permute-done((bf16[4,64,256]{2,1,0:T(8,128)(2,1)S(1)}, bf16[4,64,256]{2,1,0:T(8,128)(2,1)S(1)}, u32[]{:S(2)}, u32[]{:S(2)}) %collective-permute-start.5) | collective-permute-done | bytes 131104 | tf_op jit(solution)/shard_map/ppermute | solution.py:445
  16.0 1.2 %collective-permute-done.6.refs_0_ = bf16[4,64,256]{2,1,0:T(8,128)(2,1)S(1)} collective-permute-done((bf16[4,64,256]{2,1,0:T(8,128)(2,1)S(1)}, bf16[4,64,256]{2,1,0:T(8,128)(2,1)S(1)}, u32[]{:S(2)}, u32[]{:S(2)}) %collective-permute-start.6) | collective-permute-done | bytes 131104 | tf_op jit(solution)/shard_map/ppermute | solution.py:445
  17.2 2.9 %shard_map.111 = (bf16[128,1024]{1,0:T(8,128)(2,1)S(1)}, bf16[128,1024]{1,0:T(8,128)(2,1)S(1)}) custom-call(s32[3]{0:T(128)S(1)} %pad_add_fusion.at_ref, bf16[4,64,256]{2,1,0:T(8,128)(2,1)S(1)} %collective-permute-done.6.refs_0_, bf16[4,64,1024]{2,1,0:T(8,128)(2,1)} %refs_1_.3, bf16[4,64,256]{2,1,0:T(8,128)(2,1)} %copy-done.4, ...), custom_call_target="tpu_custom_call" | custom-call | flops 2000000000 | bytes 4194304 | tf_op jit(solution)/shard_map/pallas_call | solution.py:496
  20.2 1.6 %collective-permute-start.15 = (bf16[128,1024]{1,0:T(8,128)(2,1)S(1)}, bf16[128,1024]{1,0:T(8,128)(2,1)S(1)}, u32[]{:S(2)}, u32[]{:S(2)}) collective-permute-start(bf16[128,1024]{1,0:T(8,128)(2,1)S(1)} %get-tuple-element.57), channel_id=1, source_target_pairs={{0,8},{4,12},{8,0},{12,4},{1,9},{5,13},{9,1},{13,5},{2,10},{6,14},... | collective-permute-start | bytes 786440 | tf_op jit(solution)/shard_map/ppermute | solution.py:445
  21.8 2.9 %shard_map.110 = (bf16[128,1024]{1,0:T(8,128)(2,1)S(1)}, bf16[128,1024]{1,0:T(8,128)(2,1)S(1)}) custom-call(s32[3]{0:T(128)S(1)} %pad_add_fusion.at_ref, bf16[4,64,256]{2,1,0:T(8,128)(2,1)S(1)} %collective-permute-done.6.refs_0_, bf16[4,64,1024]{2,1,0:T(8,128)(2,1)} %refs_1_.3, bf16[4,64,256]{2,1,0:T(8,128)(2,1)} %copy-done.4, ...), custom_call_target="tpu_custom_call" | custom-call | flops 2000000000 | bytes 4194304 | tf_op jit(solution)/shard_map/pallas_call | solution.py:496
  25.3 1.5 %collective-permute-start.17 = (bf16[64,1024]{1,0:T(8,128)(2,1)S(1)}, bf16[64,1024]{1,0:T(8,128)(2,1)S(1)}, u32[]{:S(2)}, u32[]{:S(2)}) collective-permute-start(bf16[64,1024]{1,0:T(8,128)(2,1)S(1)} %pad_maximum_fusion), channel_id=1, source_target_pairs={{0,8},{4,12},{8,0},{12,4},{1,9},{5,13},{9,1},{13,5},{2,10},{6,14},... | collective-permute-start | bytes 393224 | tf_op jit(solution)/shard_map/ppermute | solution.py:445
  26.8 1.8 %collective-permute-done.8 = bf16[128,1024]{1,0:T(8,128)(2,1)S(1)} collective-permute-done((bf16[128,1024]{1,0:T(8,128)(2,1)S(1)}, bf16[128,1024]{1,0:T(8,128)(2,1)S(1)}, u32[]{:S(2)}, u32[]{:S(2)}) %collective-permute-start.8) | collective-permute-done | bytes 262176 | tf_op jit(solution)/shard_map/ppermute | solution.py:442
  28.6 1.5 %collective-permute-start.9 = (bf16[128,1024]{1,0:T(8,128)(2,1)S(1)}, bf16[128,1024]{1,0:T(8,128)(2,1)S(1)}, u32[]{:S(2)}, u32[]{:S(2)}) collective-permute-start(bf16[128,1024]{1,0:T(8,128)(2,1)S(1)} %add_convert_fusion.9.sent_any), channel_id=1, source_target_pairs={{0,2},{1,3},{2,0},{3,1},{4,6},{5,7},{6,4},{7,5},{8,10},{9,11},{10,... | collective-permute-start | bytes 786440 | tf_op jit(solution)/shard_map/ppermute | solution.py:442
  30.1 2.0 %shard_map.114 = bf16[128,1024]{1,0:T(8,128)(2,1)S(1)} custom-call(bf16[128,1024]{1,0:T(8,128)(2,1)S(1)} %collective-permute-done.15.attended_ref, f32[64,16]{1,0:T(8,128)S(1)} %collective-permute-done.other_route_ref.order_ref, bf16[1024,512]{1,0:T(8,128)(2,1)} %refs_0_.3, bf16[1024,512]{1,0:T(8,128)(2,1)} %copy-done.10), custom_call_target="tpu_custom_call" | custom-call | flops 2000000000 | bytes 4194304 | tf_op jit(solution)/shard_map/pallas_call | solution.py:587
  32.2 1.4 %collective-permute-start.16 = (bf16[128,1024]{1,0:T(8,128)(2,1)S(1)}, bf16[128,1024]{1,0:T(8,128)(2,1)S(1)}, u32[]{:S(2)}, u32[]{:S(2)}) collective-permute-start(bf16[128,1024]{1,0:T(8,128)(2,1)S(1)} %shard_map.114), channel_id=1, source_target_pairs={{0,1},{1,0},{2,3},{3,2},{4,5},{5,4},{6,7},{7,6},{8,9},{9,8},{10,11... | collective-permute-start | bytes 786440 | tf_op jit(solution)/shard_map/ppermute | solution.py:442
  33.6 1.5 %collective-permute-done.14.attended_ref = bf16[128,1024]{1,0:T(8,128)(2,1)S(1)} collective-permute-done((bf16[128,1024]{1,0:T(8,128)(2,1)S(1)}, bf16[128,1024]{1,0:T(8,128)(2,1)S(1)}, u32[]{:S(2)}, u32[]{:S(2)}) %collective-permute-start.14) | collective-permute-done | bytes 262176 | tf_op jit(solution)/shard_map/ppermute | solution.py:445
  35.1 2.0 %shard_map.113 = bf16[128,1024]{1,0:T(8,128)(2,1)S(1)} custom-call(bf16[128,1024]{1,0:T(8,128)(2,1)S(1)} %collective-permute-done.14.attended_ref, f32[64,16]{1,0:T(8,128)S(1)} %collective-permute-done.other_route_ref.order_ref, bf16[1024,512]{1,0:T(8,128)(2,1)} %refs_0_.3, bf16[1024,512]{1,0:T(8,128)(2,1)} %copy-done.10), custom_call_target="tpu_custom_call" | custom-call | flops 2000000000 | bytes 4194304 | tf_op jit(solution)/shard_map/pallas_call | solution.py:587
  37.1 5.7 %collective-permute-done.9.came_ref = bf16[128,1024]{1,0:T(8,128)(2,1)S(1)} collective-permute-done((bf16[128,1024]{1,0:T(8,128)(2,1)S(1)}, bf16[128,1024]{1,0:T(8,128)(2,1)S(1)}, u32[]{:S(2)}, u32[]{:S(2)}) %collective-permute-start.9) | collective-permute-done | bytes 262176 | tf_op jit(solution)/shard_map/ppermute | solution.py:442
  42.9 1.3 %shard_map.112 = (bf16[64,1152]{1,0:T(8,128)(2,1)S(1)}, bf16[64,1152]{1,0:T(8,128)(2,1)S(1)}, bf16[128,1152]{1,0:T(8,128)(2,1)S(1)}) custom-call(f32[64,16]{1,0:T(8,128)S(1)} %copy.15.route_ref, f32[64,16]{1,0:T(8,128)S(1)} %collective-permute-done.other_route_ref.order_ref, bf16[128,1024]{1,0:T(8,128)(2,1)S(1)} %collective-permute-done.9.came_ref, ...), custom_call_target="tpu_custom_call" | custom-call | flops 10000000000 | bytes 1 | tf_op jit(solution)/shard_map/pallas_call | solution.py:538
  44.3 1.5 %collective-permute-start.10 = (bf16[128,1152]{1,0:T(8,128)(2,1)S(1)}, bf16[128,1152]{1,0:T(8,128)(2,1)S(1)}, u32[]{:S(2)}, u32[]{:S(2)}) collective-permute-start(bf16[128,1152]{1,0:T(8,128)(2,1)S(1)} %get-tuple-element.53), channel_id=1, source_target_pairs={{0,8},{4,12},{8,0},{12,4},{1,9},{5,13},{9,1},{13,5},{2,10},{6,14},... | collective-permute-start | bytes 884744 | tf_op jit(solution)/shard_map/ppermute | solution.py:445
  45.9 2.6 %collective-permute-start.18 = (bf16[128,1024]{1,0:T(8,128)(2,1)S(1)}, bf16[128,1024]{1,0:T(8,128)(2,1)S(1)}, u32[]{:S(2)}, u32[]{:S(2)}) collective-permute-start(bf16[128,1024]{1,0:T(8,128)(2,1)S(1)} %add_convert_fusion.8.refs_5_), channel_id=1, source_target_pairs={{0,2},{1,3},{2,0},{3,1},{4,6},{5,7},{6,4},{7,5},{8,10},{9,11},{10,... | collective-permute-start | bytes 786440 | tf_op jit(solution)/shard_map/ppermute | solution.py:442
  48.6 3.2 %collective-permute-done.11.refs_1_.refs_0_ = bf16[64,1152]{1,0:T(8,128)(2,1)S(1)} collective-permute-done((bf16[64,1152]{1,0:T(8,128)(2,1)S(1)}, bf16[64,1152]{1,0:T(8,128)(2,1)S(1)}, u32[]{:S(2)}, u32[]{:S(2)}) %collective-permute-start.11) | collective-permute-done | bytes 147488 | tf_op jit(solution)/shard_map/ppermute | solution.py:442
  51.8 1.4 %collective-permute-done.10.refs_0_.refs_2_ = bf16[128,1152]{1,0:T(8,128)(2,1)S(1)} collective-permute-done((bf16[128,1152]{1,0:T(8,128)(2,1)S(1)}, bf16[128,1152]{1,0:T(8,128)(2,1)S(1)}, u32[]{:S(2)}, u32[]{:S(2)}) %collective-permute-start.10) | collective-permute-done | bytes 294944 | tf_op jit(solution)/shard_map/ppermute | solution.py:445
  53.2 1.5 %collective-permute-start.12 = (bf16[64,1152]{1,0:T(8,128)(2,1)S(1)}, bf16[64,1152]{1,0:T(8,128)(2,1)S(1)}, u32[]{:S(2)}, u32[]{:S(2)}) collective-permute-start(bf16[64,1152]{1,0:T(8,128)(2,1)S(1)} %collective-permute-done.11.refs_1_.refs_0_), channel_id=1, source_target_pairs={{0,8},{4,12},{8,0},{12,4},{1,9},{5,13},{9,1},{13,5},{2,10},{6,14},... | collective-permute-start | bytes 442376 | tf_op jit(solution)/shard_map/ppermute | solution.py:445
  54.7 1.7 %collective-permute-start.20 = (bf16[64,1152]{1,0:T(8,128)(2,1)S(1)}, bf16[64,1152]{1,0:T(8,128)(2,1)S(1)}, u32[]{:S(2)}, u32[]{:S(2)}) collective-permute-start(bf16[64,1152]{1,0:T(8,128)(2,1)S(1)} %slice.72), channel_id=1, source_target_pairs={{0,1},{1,0},{2,3},{3,2},{4,5},{5,4},{6,7},{7,6},{8,9},{9,8},{10,11... | collective-permute-start | bytes 442376 | tf_op jit(solution)/shard_map/ppermute | solution.py:442
  56.5 1.6 %collective-permute-done.13.refs_3_.refs_0_ = bf16[64,1152]{1,0:T(8,128)(2,1)S(1)} collective-permute-done((bf16[64,1152]{1,0:T(8,128)(2,1)S(1)}, bf16[64,1152]{1,0:T(8,128)(2,1)S(1)}, u32[]{:S(2)}, u32[]{:S(2)}) %collective-permute-start.13) | collective-permute-done | bytes 147488 | tf_op jit(solution)/shard_map/ppermute | solution.py:442
  58.1 2.5 %collective-permute-done.18.refs_4_ = bf16[128,1024]{1,0:T(8,128)(2,1)S(1)} collective-permute-done((bf16[128,1024]{1,0:T(8,128)(2,1)S(1)}, bf16[128,1024]{1,0:T(8,128)(2,1)S(1)}, u32[]{:S(2)}, u32[]{:S(2)}) %collective-permute-start.18) | collective-permute-done | bytes 262176 | tf_op jit(solution)/shard_map/ppermute | solution.py:442
  60.6 1.0 shard_map.115
  62.9 5.0 %collective-permute-done.21.refs_1_ = bf16[64,1024]{1,0:T(8,128)(2,1)S(1)} collective-permute-done((bf16[64,1024]{1,0:T(8,128)(2,1)S(1)}, bf16[64,1024]{1,0:T(8,128)(2,1)S(1)}, u32[]{:S(2)}, u32[]{:S(2)}) %collective-permute-start.21) | collective-permute-done | bytes 131104 | tf_op jit(solution)/shard_map/ppermute | solution.py:442
  69.2 1.6 %collective-permute-start.24 = (bf16[64,1024]{1,0:T(8,128)(2,1)S(1)}, bf16[64,1024]{1,0:T(8,128)(2,1)S(1)}, u32[]{:S(2)}, u32[]{:S(2)}) collective-permute-start(bf16[64,1024]{1,0:T(8,128)(2,1)S(1)} %slice.73), channel_id=1, source_target_pairs={{0,1},{1,0},{2,3},{3,2},{4,5},{5,4},{6,7},{7,6},{8,9},{9,8},{10,11... | collective-permute-start | bytes 393224 | tf_op jit(solution)/shard_map/ppermute | solution.py:442
  70.8 2.4 %collective-permute-done.23.refs_1_ = bf16[64,1024]{1,0:T(8,128)(2,1)S(1)} collective-permute-done((bf16[64,1024]{1,0:T(8,128)(2,1)S(1)}, bf16[64,1024]{1,0:T(8,128)(2,1)S(1)}, u32[]{:S(2)}, u32[]{:S(2)}) %collective-permute-start.23) | collective-permute-done | bytes 131104 | tf_op jit(solution)/shard_map/ppermute | solution.py:442
  76.4 1.1 collective-permute-done.25.refs_1_
  77.4 3.2 %shard_map.118 = (bf16[128,2048]{1,0:T(8,128)(2,1)S(1)}, bf16[128,2048]{1,0:T(8,128)(2,1)S(1)}) custom-call(s32[3]{0:T(128)S(1)} %pad_add_fusion.at_ref, bf16[128,2176]{1,0:T(8,128)(2,1)S(1)} %shard_map.116.refs_0_, bf16[128,2176]{1,0:T(8,128)(2,1)S(1)} %collective-permute-done.25.refs_1_, bf16[1,2048,768]{2,1,0:T(8,128)(2,1)S(1)} %copy-done, ...), custom_call_target="tpu_custom_call" | custom-call | flops 1 | bytes 1 | tf_op jit(solution)/shard_map/pallas_call | solution.py:396
  82.3 0.9 shard_map.119
  83.2 1.3 %collective-permute-start.31 = (bf16[64,2048]{1,0:T(8,128)(2,1)S(1)}, bf16[64,2048]{1,0:T(8,128)(2,1)S(1)}, u32[]{:S(2)}, u32[]{:S(2)}) collective-permute-start(bf16[64,2048]{1,0:T(8,128)(2,1)S(1)} %add_convert_fusion.7), channel_id=1, source_target_pairs={{0,8},{4,12},{8,0},{12,4},{1,9},{5,13},{9,1},{13,5},{2,10},{6,14},... | collective-permute-start | bytes 786440 | tf_op jit(solution)/shard_map/ppermute | solution.py:445
  84.6 3.2 %shard_map.121 = (bf16[128,2048]{1,0:T(8,128)(2,1)S(1)}, bf16[128,2048]{1,0:T(8,128)(2,1)S(1)}) custom-call(s32[3]{0:T(128)S(1)} %pad_add_fusion.at_ref, bf16[128,2176]{1,0:T(8,128)(2,1)S(1)} %shard_map.120.refs_0_, bf16[128,2176]{1,0:T(8,128)(2,1)S(1)} %collective-permute-done.28.refs_1_, bf16[1,2048,768]{2,1,0:T(8,128)(2,1)S(1)} %copy-done, ...), custom_call_target="tpu_custom_call" | custom-call | flops 1 | bytes 1 | tf_op jit(solution)/shard_map/pallas_call | solution.py:396
  88.3 3.4 %shard_map.122 = (bf16[128,2048]{1,0:T(8,128)(2,1)S(1)}, bf16[128,2048]{1,0:T(8,128)(2,1)S(1)}) custom-call(s32[3]{0:T(128)S(1)} %pad_add_fusion.at_ref, bf16[128,2176]{1,0:T(8,128)(2,1)S(1)} %shard_map.117.refs_0_, bf16[128,2176]{1,0:T(8,128)(2,1)S(1)} %collective-permute-done.27.refs_1_, bf16[1,2048,768]{2,1,0:T(8,128)(2,1)S(1)} %copy-done, ...), custom_call_target="tpu_custom_call" | custom-call | flops 1 | bytes 1 | tf_op jit(solution)/shard_map/pallas_call | solution.py:396
  92.0 1.3 %collective-permute-start.38 = (bf16[64,2048]{1,0:T(8,128)(2,1)S(1)}, bf16[64,2048]{1,0:T(8,128)(2,1)S(1)}, u32[]{:S(2)}, u32[]{:S(2)}) collective-permute-start(bf16[64,2048]{1,0:T(8,128)(2,1)S(1)} %add_convert_fusion.2), channel_id=1, source_target_pairs={{0,1},{1,0},{2,3},{3,2},{4,5},{5,4},{6,7},{7,6},{8,9},{9,8},{10,11... | collective-permute-start | bytes 786440 | tf_op jit(solution)/shard_map/ppermute | solution.py:442
  93.3 1.3 %collective-permute-start.32 = (bf16[64,2048]{1,0:T(8,128)(2,1)S(1)}, bf16[64,2048]{1,0:T(8,128)(2,1)S(1)}, u32[]{:S(2)}, u32[]{:S(2)}) collective-permute-start(bf16[64,2048]{1,0:T(8,128)(2,1)S(1)} %add_convert_fusion.6), channel_id=1, source_target_pairs={{0,8},{4,12},{8,0},{12,4},{1,9},{5,13},{9,1},{13,5},{2,10},{6,14},... | collective-permute-start | bytes 786440 | tf_op jit(solution)/shard_map/ppermute | solution.py:445
  94.7 3.2 %shard_map.123 = (bf16[128,2048]{1,0:T(8,128)(2,1)S(1)}, bf16[128,2048]{1,0:T(8,128)(2,1)S(1)}) custom-call(s32[3]{0:T(128)S(1)} %pad_add_fusion.at_ref, bf16[128,2176]{1,0:T(8,128)(2,1)S(1)} %get-tuple-element.83.refs_0_, bf16[128,2176]{1,0:T(8,128)(2,1)S(1)} %collective-permute-done.26.refs_1_, bf16[1,2048,768]{2,1,0:T(8,128)(2,1)S(1)} %copy-done, ...), custom_call_target="tpu_custom_call" | custom-call | flops 1 | bytes 1 | tf_op jit(solution)/shard_map/pallas_call | solution.py:396
  98.8 3.8 %collective-permute-done.32 = bf16[64,2048]{1,0:T(8,128)(2,1)S(1)} collective-permute-done((bf16[64,2048]{1,0:T(8,128)(2,1)S(1)}, bf16[64,2048]{1,0:T(8,128)(2,1)S(1)}, u32[]{:S(2)}, u32[]{:S(2)}) %collective-permute-start.32) | collective-permute-done | bytes 262176 | tf_op jit(solution)/shard_map/ppermute | solution.py:445
  102.7 0.9 collective-permute-start.39
  103.6 3.8 %collective-permute-done.36 = bf16[64,2048]{1,0:T(8,128)(2,1)S(1)} collective-permute-done((bf16[64,2048]{1,0:T(8,128)(2,1)S(1)}, bf16[64,2048]{1,0:T(8,128)(2,1)S(1)}, u32[]{:S(2)}, u32[]{:S(2)}) %collective-permute-start.36) | collective-permute-done | bytes 262176 | tf_op jit(solution)/shard_map/ppermute | solution.py:445
  107.5 0.9 collective-permute-start.37
  108.5 1.3 %collective-permute-start.35 = (bf16[64,2048]{1,0:T(8,128)(2,1)S(1)}, bf16[64,2048]{1,0:T(8,128)(2,1)S(1)}, u32[]{:S(2)}, u32[]{:S(2)}) collective-permute-start(bf16[64,2048]{1,0:T(8,128)(2,1)S(1)} %add_convert_fusion.5), channel_id=1, source_target_pairs={{0,8},{4,12},{8,0},{12,4},{1,9},{5,13},{9,1},{13,5},{2,10},{6,14},... | collective-permute-start | bytes 786440 | tf_op jit(solution)/shard_map/ppermute | solution.py:445
  109.8 8.3 %collective-permute-done.39 = bf16[64,2048]{1,0:T(8,128)(2,1)S(1)} collective-permute-done((bf16[64,2048]{1,0:T(8,128)(2,1)S(1)}, bf16[64,2048]{1,0:T(8,128)(2,1)S(1)}, u32[]{:S(2)}, u32[]{:S(2)}) %collective-permute-start.39) | collective-permute-done | bytes 262176 | tf_op jit(solution)/shard_map/ppermute | solution.py:442
  118.1 2.4 %collective-permute-done.37 = bf16[64,2048]{1,0:T(8,128)(2,1)S(1)} collective-permute-done((bf16[64,2048]{1,0:T(8,128)(2,1)S(1)}, bf16[64,2048]{1,0:T(8,128)(2,1)S(1)}, u32[]{:S(2)}, u32[]{:S(2)}) %collective-permute-start.37) | collective-permute-done | bytes 262176 | tf_op jit(solution)/shard_map/ppermute | solution.py:442
  120.5 0.9 fusion.2
  (96 shorter events, 13.0 us)
Async XLA Ops:
  0.0 6.3 %collective-permute-start.1 = (bf16[1024,512]{1,0:T(8,128)(2,1)}, bf16[1024,512]{1,0:T(8,128)(2,1)S(1)}, u32[]{:S(2)}, u32[]{:S(2)}) collective-permute-start(bf16[1024,512]{1,0:T(8,128)(2,1)} %refs_0_.3), channel_id=1, source_target_pairs={{0,4},{4,0},{8,12},{12,8},{1,5},{5,1},{9,13},{13,9},{2,6},{6,2},{1... | collective-permute-start | bytes 3145736 | tf_op jit(solution)/shard_map/ppermute | solution.py:445
  1.3 5.7 %collective-permute-start.3 = (bf16[4,16,256]{2,1,0:T(8,128)(2,1)S(1)}, bf16[4,16,256]{2,1,0:T(8,128)(2,1)S(1)}, u32[]{:S(2)}, u32[]{:S(2)}) collective-permute-start(bf16[4,16,256]{2,1,0:T(8,128)(2,1)S(1)} %pad_maximum_fusion.3), channel_id=1, source_target_pairs={{0,2},{1,3},{2,0},{3,1},{4,6},{5,7},{6,4},{7,5},{8,10},{9,11},{10,... | collective-permute-start | bytes 98312 | tf_op jit(solution)/shard_map/ppermute | solution.py:442
  5.0 5.8 %collective-permute-start.4 = (bf16[4,16,256]{2,1,0:T(8,128)(2,1)S(1)}, bf16[4,16,256]{2,1,0:T(8,128)(2,1)S(1)}, u32[]{:S(2)}, u32[]{:S(2)}) collective-permute-start(bf16[4,16,256]{2,1,0:T(8,128)(2,1)S(1)} %pad_maximum_fusion.4), channel_id=1, source_target_pairs={{0,3},{1,2},{2,1},{3,0},{4,7},{5,6},{6,5},{7,4},{8,11},{9,10},{10,... | collective-permute-start | bytes 98312 | tf_op jit(solution)/shard_map/ppermute | solution.py:442
  6.3 4.4 %collective-permute-start.2 = (bf16[4,16,256]{2,1,0:T(8,128)(2,1)S(1)}, bf16[4,16,256]{2,1,0:T(8,128)(2,1)S(1)}, u32[]{:S(2)}, u32[]{:S(2)}) collective-permute-start(bf16[4,16,256]{2,1,0:T(8,128)(2,1)S(1)} %pad_maximum_fusion.2), channel_id=1, source_target_pairs={{0,1},{1,0},{2,3},{3,2},{4,5},{5,4},{6,7},{7,6},{8,9},{9,8},{10,11... | collective-permute-start | bytes 98312 | tf_op jit(solution)/shard_map/ppermute | solution.py:442
  6.7 5.7 %copy-start.9 = (f32[1,64,8]{1,2,0:T(8,128)S(1)}, f32[1,64,8]{1,2,0:T(8,128)}, u32[]{:S(2)}) copy-start(f32[1,64,8]{1,2,0:T(8,128)} %param.18) | copy-start | bytes 6148
  6.7 9.3 %copy-start.7 = (bf16[1,64,2048]{2,1,0:T(8,128)(2,1)S(1)}, bf16[1,64,2048]{2,1,0:T(8,128)(2,1)}, u32[]{:S(2)}) copy-start(bf16[1,64,2048]{2,1,0:T(8,128)(2,1)} %param.15) | copy-start | bytes 786436
  10.8 6.4 %copy-start.4 = (bf16[4,64,256]{2,1,0:T(8,128)(2,1)}, bf16[4,64,256]{2,1,0:T(8,128)(2,1)S(1)}, u32[]{:S(2)}) copy-start(bf16[4,64,256]{2,1,0:T(8,128)(2,1)S(1)} %shard_map.109.refs_2_) | copy-start | bytes 393220
  10.8 5.0 %collective-permute-start.5 = (bf16[4,64,256]{2,1,0:T(8,128)(2,1)S(1)}, bf16[4,64,256]{2,1,0:T(8,128)(2,1)S(1)}, u32[]{:S(2)}, u32[]{:S(2)}) collective-permute-start(bf16[4,64,256]{2,1,0:T(8,128)(2,1)S(1)} %shard_map.109.refs_2_), channel_id=1, source_target_pairs={{0,8},{4,12},{8,0},{12,4},{1,9},{5,13},{9,1},{13,5},{2,10},{6,14},... | collective-permute-start | bytes 393224 | tf_op jit(solution)/shard_map/ppermute | solution.py:445
  12.5 17.7 %collective-permute-start = (f32[64,16]{1,0:T(8,128)S(1)}, f32[64,16]{1,0:T(8,128)S(1)}, u32[]{:S(2)}, u32[]{:S(2)}) collective-permute-start(f32[64,16]{1,0:T(8,128)S(1)} %copy.15.route_ref), channel_id=1, source_target_pairs={{0,2},{1,3},{2,0},{3,1},{4,6},{5,7},{6,4},{7,5},{8,10},{9,11},{10,... | collective-permute-start | bytes 12296 | tf_op jit(solution)/shard_map/ppermute | solution.py:442
  13.7 2.2 %collective-permute-start.7 = (bf16[4,64,256]{2,1,0:T(8,128)(2,1)S(1)}, bf16[4,64,256]{2,1,0:T(8,128)(2,1)S(1)}, u32[]{:S(2)}, u32[]{:S(2)}) collective-permute-start(bf16[4,64,256]{2,1,0:T(8,128)(2,1)S(1)} %shard_map.109.refs_2_), channel_id=1, source_target_pairs={{0,4},{4,0},{8,12},{12,8},{1,5},{5,1},{9,13},{13,9},{2,6},{6,2},{1... | collective-permute-start | bytes 393224 | tf_op jit(solution)/shard_map/ppermute | solution.py:445
  15.9 1.3 %collective-permute-start.6 = (bf16[4,64,256]{2,1,0:T(8,128)(2,1)S(1)}, bf16[4,64,256]{2,1,0:T(8,128)(2,1)S(1)}, u32[]{:S(2)}, u32[]{:S(2)}) collective-permute-start(bf16[4,64,256]{2,1,0:T(8,128)(2,1)S(1)} %collective-permute-done.5.refs_4_), channel_id=1, source_target_pairs={{0,4},{4,0},{8,12},{12,8},{1,5},{5,1},{9,13},{13,9},{2,6},{6,2},{1... | collective-permute-start | bytes 393224 | tf_op jit(solution)/shard_map/ppermute | solution.py:445
  20.1 8.4 %collective-permute-start.8 = (bf16[128,1024]{1,0:T(8,128)(2,1)S(1)}, bf16[128,1024]{1,0:T(8,128)(2,1)S(1)}, u32[]{:S(2)}, u32[]{:S(2)}) collective-permute-start(bf16[128,1024]{1,0:T(8,128)(2,1)S(1)} %get-tuple-element.51), channel_id=1, source_target_pairs={{0,1},{1,0},{2,3},{3,2},{4,5},{5,4},{6,7},{7,6},{8,9},{9,8},{10,11... | collective-permute-start | bytes 786440 | tf_op jit(solution)/shard_map/ppermute | solution.py:442
  20.2 9.9 %collective-permute-start.15 = (bf16[128,1024]{1,0:T(8,128)(2,1)S(1)}, bf16[128,1024]{1,0:T(8,128)(2,1)S(1)}, u32[]{:S(2)}, u32[]{:S(2)}) collective-permute-start(bf16[128,1024]{1,0:T(8,128)(2,1)S(1)} %get-tuple-element.57), channel_id=1, source_target_pairs={{0,8},{4,12},{8,0},{12,4},{1,9},{5,13},{9,1},{13,5},{2,10},{6,14},... | collective-permute-start | bytes 786440 | tf_op jit(solution)/shard_map/ppermute | solution.py:445
  24.7 10.4 %collective-permute-start.14 = (bf16[128,1024]{1,0:T(8,128)(2,1)S(1)}, bf16[128,1024]{1,0:T(8,128)(2,1)S(1)}, u32[]{:S(2)}, u32[]{:S(2)}) collective-permute-start(bf16[128,1024]{1,0:T(8,128)(2,1)S(1)} %get-tuple-element.56), channel_id=1, source_target_pairs={{0,8},{4,12},{8,0},{12,4},{1,9},{5,13},{9,1},{13,5},{2,10},{6,14},... | collective-permute-start | bytes 786440 | tf_op jit(solution)/shard_map/ppermute | solution.py:445
  25.3 20.5 %collective-permute-start.17 = (bf16[64,1024]{1,0:T(8,128)(2,1)S(1)}, bf16[64,1024]{1,0:T(8,128)(2,1)S(1)}, u32[]{:S(2)}, u32[]{:S(2)}) collective-permute-start(bf16[64,1024]{1,0:T(8,128)(2,1)S(1)} %pad_maximum_fusion), channel_id=1, source_target_pairs={{0,8},{4,12},{8,0},{12,4},{1,9},{5,13},{9,1},{13,5},{2,10},{6,14},... | collective-permute-start | bytes 393224 | tf_op jit(solution)/shard_map/ppermute | solution.py:445
  28.6 14.2 %collective-permute-start.9 = (bf16[128,1024]{1,0:T(8,128)(2,1)S(1)}, bf16[128,1024]{1,0:T(8,128)(2,1)S(1)}, u32[]{:S(2)}, u32[]{:S(2)}) collective-permute-start(bf16[128,1024]{1,0:T(8,128)(2,1)S(1)} %add_convert_fusion.9.sent_any), channel_id=1, source_target_pairs={{0,2},{1,3},{2,0},{3,1},{4,6},{5,7},{6,4},{7,5},{8,10},{9,11},{10,... | collective-permute-start | bytes 786440 | tf_op jit(solution)/shard_map/ppermute | solution.py:442
  32.2 13.6 %collective-permute-start.16 = (bf16[128,1024]{1,0:T(8,128)(2,1)S(1)}, bf16[128,1024]{1,0:T(8,128)(2,1)S(1)}, u32[]{:S(2)}, u32[]{:S(2)}) collective-permute-start(bf16[128,1024]{1,0:T(8,128)(2,1)S(1)} %shard_map.114), channel_id=1, source_target_pairs={{0,1},{1,0},{2,3},{3,2},{4,5},{5,4},{6,7},{7,6},{8,9},{9,8},{10,11... | collective-permute-start | bytes 786440 | tf_op jit(solution)/shard_map/ppermute | solution.py:442
  44.2 7.6 %collective-permute-start.11 = (bf16[64,1152]{1,0:T(8,128)(2,1)S(1)}, bf16[64,1152]{1,0:T(8,128)(2,1)S(1)}, u32[]{:S(2)}, u32[]{:S(2)}) collective-permute-start(bf16[64,1152]{1,0:T(8,128)(2,1)S(1)} %get-tuple-element.54.refs_0_), channel_id=1, source_target_pairs={{0,1},{1,0},{2,3},{3,2},{4,5},{5,4},{6,7},{7,6},{8,9},{9,8},{10,11... | collective-permute-start | bytes 442376 | tf_op jit(solution)/shard_map/ppermute | solution.py:442
  44.3 8.9 %collective-permute-start.10 = (bf16[128,1152]{1,0:T(8,128)(2,1)S(1)}, bf16[128,1152]{1,0:T(8,128)(2,1)S(1)}, u32[]{:S(2)}, u32[]{:S(2)}) collective-permute-start(bf16[128,1152]{1,0:T(8,128)(2,1)S(1)} %get-tuple-element.53), channel_id=1, source_target_pairs={{0,8},{4,12},{8,0},{12,4},{1,9},{5,13},{9,1},{13,5},{2,10},{6,14},... | collective-permute-start | bytes 884744 | tf_op jit(solution)/shard_map/ppermute | solution.py:445
  45.9 14.6 %copy-start.5 = (bf16[128,1024]{1,0:T(8,128)(2,1)}, bf16[128,1024]{1,0:T(8,128)(2,1)S(1)}, u32[]{:S(2)}) copy-start(bf16[128,1024]{1,0:T(8,128)(2,1)S(1)} %add_convert_fusion.8.refs_5_) | copy-start | bytes 786436
  45.9 14.6 %collective-permute-start.18 = (bf16[128,1024]{1,0:T(8,128)(2,1)S(1)}, bf16[128,1024]{1,0:T(8,128)(2,1)S(1)}, u32[]{:S(2)}, u32[]{:S(2)}) collective-permute-start(bf16[128,1024]{1,0:T(8,128)(2,1)S(1)} %add_convert_fusion.8.refs_5_), channel_id=1, source_target_pairs={{0,2},{1,3},{2,0},{3,1},{4,6},{5,7},{6,4},{7,5},{8,10},{9,11},{10,... | collective-permute-start | bytes 786440 | tf_op jit(solution)/shard_map/ppermute | solution.py:442
  48.5 9.5 %collective-permute-start.13 = (bf16[64,1152]{1,0:T(8,128)(2,1)S(1)}, bf16[64,1152]{1,0:T(8,128)(2,1)S(1)}, u32[]{:S(2)}, u32[]{:S(2)}) collective-permute-start(bf16[64,1152]{1,0:T(8,128)(2,1)S(1)} %get-tuple-element.52.refs_0_), channel_id=1, source_target_pairs={{0,1},{1,0},{2,3},{3,2},{4,5},{5,4},{6,7},{7,6},{8,9},{9,8},{10,11... | collective-permute-start | bytes 442376 | tf_op jit(solution)/shard_map/ppermute | solution.py:442
  53.2 7.3 %collective-permute-start.12 = (bf16[64,1152]{1,0:T(8,128)(2,1)S(1)}, bf16[64,1152]{1,0:T(8,128)(2,1)S(1)}, u32[]{:S(2)}, u32[]{:S(2)}) collective-permute-start(bf16[64,1152]{1,0:T(8,128)(2,1)S(1)} %collective-permute-done.11.refs_1_.refs_0_), channel_id=1, source_target_pairs={{0,8},{4,12},{8,0},{12,4},{1,9},{5,13},{9,1},{13,5},{2,10},{6,14},... | collective-permute-start | bytes 442376 | tf_op jit(solution)/shard_map/ppermute | solution.py:445
  54.7 19.9 %copy-start.3 = (f32[2048]{0:T(1024)S(1)}, f32[2048]{0:T(1024)}, u32[]{:S(2)}) copy-start(f32[2048]{0:T(1024)} %param.16) | copy-start | bytes 24580
  54.7 22.7 %copy-start = (bf16[1,2048,768]{2,1,0:T(8,128)(2,1)S(1)}, bf16[1,2048,768]{2,1,0:T(8,128)(2,1)}, u32[]{:S(2)}) copy-start(bf16[1,2048,768]{2,1,0:T(8,128)(2,1)} %refs_2_.7) | copy-start | bytes 9437188
  54.7 22.7 %copy-start.1 = (bf16[1,2048,768]{2,1,0:T(8,128)(2,1)S(1)}, bf16[1,2048,768]{2,1,0:T(8,128)(2,1)}, u32[]{:S(2)}) copy-start(bf16[1,2048,768]{2,1,0:T(8,128)(2,1)} %refs_3_.7) | copy-start | bytes 9437188
  54.7 22.7 %copy-start.2 = (bf16[1,768,2048]{2,1,0:T(8,128)(2,1)S(1)}, bf16[1,768,2048]{2,1,0:T(8,128)(2,1)}, u32[]{:S(2)}) copy-start(bf16[1,768,2048]{2,1,0:T(8,128)(2,1)} %refs_4_.7) | copy-start | bytes 9437188
  54.7 8.2 %collective-permute-start.20 = (bf16[64,1152]{1,0:T(8,128)(2,1)S(1)}, bf16[64,1152]{1,0:T(8,128)(2,1)S(1)}, u32[]{:S(2)}, u32[]{:S(2)}) collective-permute-start(bf16[64,1152]{1,0:T(8,128)(2,1)S(1)} %slice.72), channel_id=1, source_target_pairs={{0,1},{1,0},{2,3},{3,2},{4,5},{5,4},{6,7},{7,6},{8,9},{9,8},{10,11... | collective-permute-start | bytes 442376 | tf_op jit(solution)/shard_map/ppermute | solution.py:442
  61.6 7.1 %collective-permute-start.19 = (bf16[128,1024]{1,0:T(8,128)(2,1)S(1)}, bf16[128,1024]{1,0:T(8,128)(2,1)S(1)}, u32[]{:S(2)}, u32[]{:S(2)}) collective-permute-start(bf16[128,1024]{1,0:T(8,128)(2,1)S(1)} %get-tuple-element.61), channel_id=1, source_target_pairs={{0,8},{4,12},{8,0},{12,4},{1,9},{5,13},{9,1},{13,5},{2,10},{6,14},... | collective-permute-start | bytes 786440 | tf_op jit(solution)/shard_map/ppermute | solution.py:445
  62.9 5.0 %collective-permute-start.21 = (bf16[64,1024]{1,0:T(8,128)(2,1)S(1)}, bf16[64,1024]{1,0:T(8,128)(2,1)S(1)}, u32[]{:S(2)}, u32[]{:S(2)}) collective-permute-start(bf16[64,1024]{1,0:T(8,128)(2,1)S(1)} %get-tuple-element.63.refs_1_), channel_id=1, source_target_pairs={{0,1},{1,0},{2,3},{3,2},{4,5},{5,4},{6,7},{7,6},{8,9},{9,8},{10,11... | collective-permute-start | bytes 393224 | tf_op jit(solution)/shard_map/ppermute | solution.py:442
  67.9 5.2 %collective-permute-start.23 = (bf16[64,1024]{1,0:T(8,128)(2,1)S(1)}, bf16[64,1024]{1,0:T(8,128)(2,1)S(1)}, u32[]{:S(2)}, u32[]{:S(2)}) collective-permute-start(bf16[64,1024]{1,0:T(8,128)(2,1)S(1)} %get-tuple-element.65.refs_1_), channel_id=1, source_target_pairs={{0,1},{1,0},{2,3},{3,2},{4,5},{5,4},{6,7},{7,6},{8,9},{9,8},{10,11... | collective-permute-start | bytes 393224 | tf_op jit(solution)/shard_map/ppermute | solution.py:442
  68.7 5.0 %collective-permute-start.22 = (bf16[64,1024]{1,0:T(8,128)(2,1)S(1)}, bf16[64,1024]{1,0:T(8,128)(2,1)S(1)}, u32[]{:S(2)}, u32[]{:S(2)}) collective-permute-start(bf16[64,1024]{1,0:T(8,128)(2,1)S(1)} %collective-permute-done.21.refs_1_), channel_id=1, source_target_pairs={{0,8},{4,12},{8,0},{12,4},{1,9},{5,13},{9,1},{13,5},{2,10},{6,14},... | collective-permute-start | bytes 393224 | tf_op jit(solution)/shard_map/ppermute | solution.py:445
  69.2 5.4 %collective-permute-start.24 = (bf16[64,1024]{1,0:T(8,128)(2,1)S(1)}, bf16[64,1024]{1,0:T(8,128)(2,1)S(1)}, u32[]{:S(2)}, u32[]{:S(2)}) collective-permute-start(bf16[64,1024]{1,0:T(8,128)(2,1)S(1)} %slice.73), channel_id=1, source_target_pairs={{0,1},{1,0},{2,3},{3,2},{4,5},{5,4},{6,7},{7,6},{8,9},{9,8},{10,11... | collective-permute-start | bytes 393224 | tf_op jit(solution)/shard_map/ppermute | solution.py:442
  75.4 2.0 %collective-permute-start.25 = (bf16[128,2176]{1,0:T(8,128)(2,1)S(1)}, bf16[128,2176]{1,0:T(8,128)(2,1)S(1)}, u32[]{:S(2)}, u32[]{:S(2)}) collective-permute-start(bf16[128,2176]{1,0:T(8,128)(2,1)S(1)} %shard_map.116.refs_0_), channel_id=1, source_target_pairs={{0,4},{4,0},{8,12},{12,8},{1,5},{5,1},{9,13},{13,9},{2,6},{6,2},{1... | collective-permute-start | bytes 1671176 | tf_op jit(solution)/shard_map/ppermute | solution.py:445
  80.6 2.5 %collective-permute-start.29 = (bf16[128,2048]{1,0:T(8,128)(2,1)S(1)}, bf16[128,2048]{1,0:T(8,128)(2,1)S(1)}, u32[]{:S(2)}, u32[]{:S(2)}) collective-permute-start(bf16[128,2048]{1,0:T(8,128)(2,1)S(1)} %get-tuple-element.73), channel_id=1, source_target_pairs={{0,4},{4,0},{8,12},{12,8},{1,5},{5,1},{9,13},{13,9},{2,6},{6,2},{1... | collective-permute-start | bytes 1572872 | tf_op jit(solution)/shard_map/ppermute | solution.py:445
  80.8 7.5 %collective-permute-start.27 = (bf16[128,2176]{1,0:T(8,128)(2,1)S(1)}, bf16[128,2176]{1,0:T(8,128)(2,1)S(1)}, u32[]{:S(2)}, u32[]{:S(2)}) collective-permute-start(bf16[128,2176]{1,0:T(8,128)(2,1)S(1)} %shard_map.117.refs_0_), channel_id=1, source_target_pairs={{0,4},{4,0},{8,12},{12,8},{1,5},{5,1},{9,13},{13,9},{2,6},{6,2},{1... | collective-permute-start | bytes 1671176 | tf_op jit(solution)/shard_map/ppermute | solution.py:445
  82.1 2.5 %collective-permute-start.28 = (bf16[128,2176]{1,0:T(8,128)(2,1)S(1)}, bf16[128,2176]{1,0:T(8,128)(2,1)S(1)}, u32[]{:S(2)}, u32[]{:S(2)}) collective-permute-start(bf16[128,2176]{1,0:T(8,128)(2,1)S(1)} %shard_map.120.refs_0_), channel_id=1, source_target_pairs={{0,4},{4,0},{8,12},{12,8},{1,5},{5,1},{9,13},{13,9},{2,6},{6,2},{1... | collective-permute-start | bytes 1671176 | tf_op jit(solution)/shard_map/ppermute | solution.py:445
  83.2 8.7 %collective-permute-start.31 = (bf16[64,2048]{1,0:T(8,128)(2,1)S(1)}, bf16[64,2048]{1,0:T(8,128)(2,1)S(1)}, u32[]{:S(2)}, u32[]{:S(2)}) collective-permute-start(bf16[64,2048]{1,0:T(8,128)(2,1)S(1)} %add_convert_fusion.7), channel_id=1, source_target_pairs={{0,8},{4,12},{8,0},{12,4},{1,9},{5,13},{9,1},{13,5},{2,10},{6,14},... | collective-permute-start | bytes 786440 | tf_op jit(solution)/shard_map/ppermute | solution.py:445
  87.7 5.5 %collective-permute-start.30 = (bf16[128,2048]{1,0:T(8,128)(2,1)S(1)}, bf16[128,2048]{1,0:T(8,128)(2,1)S(1)}, u32[]{:S(2)}, u32[]{:S(2)}) collective-permute-start(bf16[128,2048]{1,0:T(8,128)(2,1)S(1)} %get-tuple-element.81), channel_id=1, source_target_pairs={{0,4},{4,0},{8,12},{12,8},{1,5},{5,1},{9,13},{13,9},{2,6},{6,2},{1... | collective-permute-start | bytes 1572872 | tf_op jit(solution)/shard_map/ppermute | solution.py:445
  87.9 6.8 %collective-permute-start.26 = (bf16[128,2176]{1,0:T(8,128)(2,1)S(1)}, bf16[128,2176]{1,0:T(8,128)(2,1)S(1)}, u32[]{:S(2)}, u32[]{:S(2)}) collective-permute-start(bf16[128,2176]{1,0:T(8,128)(2,1)S(1)} %get-tuple-element.83.refs_0_), channel_id=1, source_target_pairs={{0,4},{4,0},{8,12},{12,8},{1,5},{5,1},{9,13},{13,9},{2,6},{6,2},{1... | collective-permute-start | bytes 1671176 | tf_op jit(solution)/shard_map/ppermute | solution.py:445
  91.9 6.0 %collective-permute-start.34 = (bf16[128,2048]{1,0:T(8,128)(2,1)S(1)}, bf16[128,2048]{1,0:T(8,128)(2,1)S(1)}, u32[]{:S(2)}, u32[]{:S(2)}) collective-permute-start(bf16[128,2048]{1,0:T(8,128)(2,1)S(1)} %get-tuple-element.89), channel_id=1, source_target_pairs={{0,4},{4,0},{8,12},{12,8},{1,5},{5,1},{9,13},{13,9},{2,6},{6,2},{1... | collective-permute-start | bytes 1572872 | tf_op jit(solution)/shard_map/ppermute | solution.py:445
  92.0 10.6 %collective-permute-start.38 = (bf16[64,2048]{1,0:T(8,128)(2,1)S(1)}, bf16[64,2048]{1,0:T(8,128)(2,1)S(1)}, u32[]{:S(2)}, u32[]{:S(2)}) collective-permute-start(bf16[64,2048]{1,0:T(8,128)(2,1)S(1)} %add_convert_fusion.2), channel_id=1, source_target_pairs={{0,1},{1,0},{2,3},{3,2},{4,5},{5,4},{6,7},{7,6},{8,9},{9,8},{10,11... | collective-permute-start | bytes 786440 | tf_op jit(solution)/shard_map/ppermute | solution.py:442
  93.3 9.2 %collective-permute-start.32 = (bf16[64,2048]{1,0:T(8,128)(2,1)S(1)}, bf16[64,2048]{1,0:T(8,128)(2,1)S(1)}, u32[]{:S(2)}, u32[]{:S(2)}) collective-permute-start(bf16[64,2048]{1,0:T(8,128)(2,1)S(1)} %add_convert_fusion.6), channel_id=1, source_target_pairs={{0,8},{4,12},{8,0},{12,4},{1,9},{5,13},{9,1},{13,5},{2,10},{6,14},... | collective-permute-start | bytes 786440 | tf_op jit(solution)/shard_map/ppermute | solution.py:445
  97.9 9.5 %collective-permute-start.36 = (bf16[64,2048]{1,0:T(8,128)(2,1)S(1)}, bf16[64,2048]{1,0:T(8,128)(2,1)S(1)}, u32[]{:S(2)}, u32[]{:S(2)}) collective-permute-start(bf16[64,2048]{1,0:T(8,128)(2,1)S(1)} %add_convert_fusion.4), channel_id=1, source_target_pairs={{0,8},{4,12},{8,0},{12,4},{1,9},{5,13},{9,1},{13,5},{2,10},{6,14},... | collective-permute-start | bytes 786440 | tf_op jit(solution)/shard_map/ppermute | solution.py:445
  102.5 5.9 %collective-permute-start.33 = (bf16[128,2048]{1,0:T(8,128)(2,1)S(1)}, bf16[128,2048]{1,0:T(8,128)(2,1)S(1)}, u32[]{:S(2)}, u32[]{:S(2)}) collective-permute-start(bf16[128,2048]{1,0:T(8,128)(2,1)S(1)} %get-tuple-element.87), channel_id=1, source_target_pairs={{0,4},{4,0},{8,12},{12,8},{1,5},{5,1},{9,13},{13,9},{2,6},{6,2},{1... | collective-permute-start | bytes 1572872 | tf_op jit(solution)/shard_map/ppermute | solution.py:445
  102.7 15.4 %collective-permute-start.39 = (bf16[64,2048]{1,0:T(8,128)(2,1)S(1)}, bf16[64,2048]{1,0:T(8,128)(2,1)S(1)}, u32[]{:S(2)}, u32[]{:S(2)}) collective-permute-start(bf16[64,2048]{1,0:T(8,128)(2,1)S(1)} %add_convert_fusion.1), channel_id=1, source_target_pairs={{0,2},{1,3},{2,0},{3,1},{4,6},{5,7},{6,4},{7,5},{8,10},{9,11},{10,... | collective-permute-start | bytes 786440 | tf_op jit(solution)/shard_map/ppermute | solution.py:442
  107.5 12.9 %collective-permute-start.37 = (bf16[64,2048]{1,0:T(8,128)(2,1)S(1)}, bf16[64,2048]{1,0:T(8,128)(2,1)S(1)}, u32[]{:S(2)}, u32[]{:S(2)}) collective-permute-start(bf16[64,2048]{1,0:T(8,128)(2,1)S(1)} %add_convert_fusion.3), channel_id=1, source_target_pairs={{0,1},{1,0},{2,3},{3,2},{4,5},{5,4},{6,7},{7,6},{8,9},{9,8},{10,11... | collective-permute-start | bytes 786440 | tf_op jit(solution)/shard_map/ppermute | solution.py:442
  108.5 11.9 %collective-permute-start.35 = (bf16[64,2048]{1,0:T(8,128)(2,1)S(1)}, bf16[64,2048]{1,0:T(8,128)(2,1)S(1)}, u32[]{:S(2)}, u32[]{:S(2)}) collective-permute-start(bf16[64,2048]{1,0:T(8,128)(2,1)S(1)} %add_convert_fusion.5), channel_id=1, source_target_pairs={{0,8},{4,12},{8,0},{12,4},{1,9},{5,13},{9,1},{13,5},{2,10},{6,14},... | collective-permute-start | bytes 786440 | tf_op jit(solution)/shard_map/ppermute | solution.py:445
  (5 other events, 16.3 us)
where the time goes:
time: 122 us; the launch traced here: 121 us
  waiting for transfers between devices  54.9 us (45%)
  starting transfers between devices  34.7 us (28%)
  Pallas kernels  28.6 us (23%)
  other arithmetic  1.78 us (1%)
    ppermute x17, waiting for transfers between devices, over_role(): return lax.ppermute(array, 'role', [(i, i ^ k) for i in range(role_count)])  38.4 us
    ppermute x17, starting transfers between devices, over_role(): return lax.ppermute(array, 'role', [(i, i ^ k) for i in range(role_count)])  18.7 us
    ppermute x23, waiting for transfers between devices, over_seq(): return lax.ppermute(array, 'seq', [(i, i ^ j) for i in range(seq_count)])  16.4 us
    ppermute x23, starting transfers between devices, over_seq(): return lax.ppermute(array, 'seq', [(i, i ^ j) for i in range(seq_count)])  16 us
    pallas_call x4, Pallas kernels, run_expert(): pl.pallas_call(partial(expert_kernel, len(tokens)), in_specs=[pl.BlockSpe...  12.9 us
    pallas_call x2, Pallas kernels, gathered_shards(): pl.pallas_call(partial(attend_kernel, seq_count, role_count, slots, parts...  5.79 us
    pallas_call x2, Pallas kernels, gathered_shards(): pl.pallas_call(partial(project_kernel, slots, parts), in_specs=in_vmem(1)...  4.08 us
    pallas_call x4, Pallas kernels, normed_rows(): pl.pallas_call(partial(norm_kernel, chips, *firsts), in_specs=[pl.BlockSp...  3.44 us
  transfers between devices with their start and end apart: 40, of which 23 were waited for; matrix products, arithmetic and copies ran while one was open for 2% of the time, Pallas kernels for 20%

commit v1 on v0

--- a/solution.py
+++ b/solution.py
@@ -289,9 +289,8 @@
     return [jax.ShapeDtypeStruct((rows * len(group), width), jnp.bfloat16) for group in groups]
 
 
-def near_sum_kernel(route_ref, other_route_ref, came_ref, sent_any, *refs):
+def near_sum_kernel(route_ref, other_route_ref, came_ref, sent, *refs):
     out_refs, both_ref = refs[:2], refs[2]
-    copies, (sent,) = start_fetch([sent_any], refs[3:])
     rows, width = sent.shape[0] // 2, sent.shape[1]
     lane = lax.broadcasted_iota(jnp.int32, (rows, GATE_COLUMNS), 1)
     half = GATE_COLUMNS // 2
@@ -306,7 +305,6 @@
         terms = jnp.where(lane < half, first, shares - first).astype(jnp.bfloat16)
         out_refs[p][:, width:] = terms
         both_ref[p * rows : (p + 1) * rows, width:] = terms
-    copies[0].wait()
     for p in range(2):
         total = sent[p * rows : (p + 1) * rows].astype(jnp.float32)
         total = total + came_ref[(1 - p) * rows : (2 - p) * rows].astype(jnp.float32)
@@ -316,12 +314,9 @@
 
 def far_sum_kernel(rows, order_count, *refs):
     refs = refs[order_count:]
-    chips = (len(refs) - 4) // 3
-    came_refs, sent_any = refs[:chips], refs[chips : 2 * chips]
+    chips = (len(refs) - 3) // 2
+    came_refs, sent_refs = refs[:chips], refs[chips : 2 * chips]
     own_ref, other_ref, both_ref = refs[2 * chips : 2 * chips + 3]
-    copies, sent_refs = start_fetch(sent_any, refs[2 * chips + 3 :])
-    for copy in copies:
-        copy.wait()
     size = chips * rows
     for n, (sent, came) in enumerate(zip(sent_refs, came_refs)):
         to = slice(n * rows, (n + 1) * rows)
@@ -333,30 +328,37 @@
 
 
 def norm_kernel(chips, near_row, far_row, at_ref, gain_ref, *refs):
-    parts, (normed_ref, *hidden_refs, whole_ref) = refs[: 2 * chips], refs[2 * chips :]
+    parts, (normed_ref, *hidden_refs) = refs[: 2 * chips], refs[2 * chips :]
     seq_index = at_ref[0]
-    features = whole_ref.shape[1]
-    rows = whole_ref.shape[0] // chips
+    rows = normed_ref.shape[0] // chips
+    features = gain_ref.shape[1]
     width = features // chips // 2
-    for n in range(chips):
-        near, far = parts[2 * n : 2 * n + 2]
-        for m in range(chips):
-            part = far if m else near
+
+    def pieces(to):
+        for n in range(chips):
+            m = n ^ to
+            part = parts[2 * n + (1 if m else 0)]
             first = ((far_row if m else near_row) if n else 0) + (m - 1 if m else 0) * rows
-            to = slice((n ^ m) * rows, ((n ^ m) + 1) * rows)
             for j in range(2):
-                start = pl.multiple_of((seq_index ^ (2 * n + j)) * width, width)
-                whole_ref[to, pl.ds(start, width)] = part[
-                    first : first + rows, j * width : (j + 1) * width
-                ].astype(jnp.float32)
-        first = near_row if n else 0
-        normed_ref[n * rows : (n + 1) * rows, features:] = near[first : first + rows, 2 * width :]
-    hidden = whole_ref[...]
-    variance = jnp.mean(hidden * hidden, axis=1, keepdims=True)
-    normed = hidden * lax.rsqrt(variance + epsilon) * gain_ref[...]
-    normed_ref[:, :features] = normed.astype(jnp.bfloat16)
-    for hidden_ref in hidden_refs:
-        hidden_ref[...] = hidden[:rows]
+                values = part[first : first + rows, j * width : (j + 1) * width]
+                yield seq_index ^ (2 * n + j), values.astype(jnp.float32)
+
+    for to in range(chips):
+        squares = sum(
+            jnp.sum(values * values, axis=1, keepdims=True) for _, values in pieces(to)
+        )
+        factor = lax.rsqrt(squares * (1.0 / features) + epsilon)
+        to_rows = slice(to * rows, (to + 1) * rows)
+        for block, values in pieces(to):
+            columns = pl.ds(pl.multiple_of(block * width, width), width)
+            normed_ref[to_rows, columns] = (values * factor * gain_ref[:, columns]).astype(
+                jnp.bfloat16
+            )
+            if to == 0:
+                for hidden_ref in hidden_refs:
+                    hidden_ref[:, columns] = values
+        near, first = parts[2 * to], near_row if to else 0
+        normed_ref[to_rows, features:] = near[first : first + rows, 2 * width :]
 
 
 def expert_kernel(token_count, at_ref, *refs):
@@ -530,20 +532,18 @@
 
     near_sent = summed_over_role(near, residuals[0])
     near_came = over_role(near_sent, last)
-    near_args = in_hbm(near_sent)
     own_shape, both_shape = [
         jax.ShapeDtypeStruct((size, near_width + GATE_COLUMNS), jnp.bfloat16)
         for size in (local_length, 2 * local_length)
     ]
     near_halves = pl.pallas_call(
         near_sum_kernel,
-        in_specs=in_vmem(3) + hbm_specs(1),
+        in_specs=in_vmem(4),
         out_specs=in_vmem(3),
         out_shape=[own_shape, own_shape, both_shape],
-        scratch_shapes=fetch_scratch(*near_args),
         compiler_params=pltpu.CompilerParams(vmem_limit_bytes=SMALL_VMEM),
         cost_estimate=LONG,
-    )(routes, other_routes, near_came, *near_args)
+    )(routes, other_routes, near_came, near_sent)
 
     def walk(k, bits):
         found = [k]
@@ -597,7 +597,6 @@
         came.append(over_role(sent[-1], last))
 
     chips = 1 + len(across_steps)
-    far_args = in_hbm(*sent)
     far_rows = (chips - 1) * local_length
     far_shape, far_both_shape = [
         jax.ShapeDtypeStruct((size, near_width), jnp.bfloat16) for size in (far_rows, 2 * far_rows)
@@ -607,14 +606,12 @@
     far_halves = pl.pallas_call(
         partial(far_sum_kernel, local_length, len(first_come)),
         in_specs=[pl.BlockSpec(memory_space=pl.ANY)] * len(first_come)
-        + in_vmem(len(came))
-        + hbm_specs(len(far_args)),
+        + in_vmem(len(came) + len(sent)),
         out_specs=in_vmem(3),
         out_shape=[far_shape, far_shape, far_both_shape],
-        scratch_shapes=fetch_scratch(*far_args),
         compiler_params=pltpu.CompilerParams(vmem_limit_bytes=SMALL_VMEM),
         cost_estimate=SHORT,
-    )(*first_come, *came, *far_args)
+    )(*first_come, *came, *sent)
     far_own, far_other, far_both = far_halves
     far_other = after(far_other, *near_crossed[final])
     far_planes, far_crossed = spread(far_own, far_other, far_both, True)
@@ -633,7 +630,6 @@
                 jax.ShapeDtypeStruct((rows, width + GATE_COLUMNS), jnp.bfloat16),
                 *hidden_shape,
             ],
-            scratch_shapes=[pltpu.VMEM((rows, width), jnp.float32)],
             compiler_params=pltpu.CompilerParams(vmem_limit_bytes=SMALL_VMEM),
             cost_estimate=NOTHING,
         )(at, gain, *parts)

time: 122 us -> 120 us (0.984)
  Pallas kernels: 28.6 us -> 26.5 us
  waiting for transfers between devices: 54.9 us -> 57 us
    ppermute x17, waiting for transfers between devices: 38.4 us -> 40.7 us  [over_role(): return lax.ppermute(array, 'role', [(i, i ^ k) for i in range(role_count)])]
  transfers between devices with their start and end apart: 40 -> 40, of which waited for: 23 -> 23; matrix products, arithmetic and copies ran while one was open for 2% -> 2% of each run, Pallas kernels for 20% -> 19%
where the time goes in v1:
time: 120 us
  waiting for transfers between devices  57 us (48%)
  starting transfers between devices  33.6 us (28%)
  Pallas kernels  26.5 us (22%)
  other arithmetic  1.78 us (1%)
    ppermute x17, waiting for transfers between devices, over_role(): return lax.ppermute(array, 'role', [(i, i ^ k) for i in range(role_count)])  40.7 us
    ppermute x17, starting transfers between devices, over_role(): return lax.ppermute(array, 'role', [(i, i ^ k) for i in range(role_count)])  18.5 us
    ppermute x23, waiting for transfers between devices, over_seq(): return lax.ppermute(array, 'seq', [(i, i ^ j) for i in range(seq_count)])  16.4 us
    ppermute x23, starting transfers between devices, over_seq(): return lax.ppermute(array, 'seq', [(i, i ^ j) for i in range(seq_count)])  15 us
    pallas_call x4, Pallas kernels, run_expert(): pl.pallas_call(partial(expert_kernel, len(tokens)), in_specs=[pl.BlockSpe...  12.9 us
    pallas_call x2, Pallas kernels, gathered_shards(): pl.pallas_call(partial(attend_kernel, seq_count, role_count, slots, parts...  5.77 us
    pallas_call x2, Pallas kernels, gathered_shards(): pl.pallas_call(partial(project_kernel, slots, parts), in_specs=in_vmem(1)...  4.02 us
    pallas_call x4, Pallas kernels, normed_rows(): pl.pallas_call(partial(norm_kernel, chips, *firsts), in_specs=[pl.BlockSp...  3.27 us
  transfers between devices with their start and end apart: 40, of which 23 were waited for; matrix products, arithmetic and copies ran while one was open for 2% of the time, Pallas kernels for 19%

profile of v1, /device:TPU:0, one launch (start us, length us, event | category | flops | bytes accessed | tf_op | source)
XLA Modules:
  0.0 120.2 jit_solution(8038760721057297894)
XLA Ops:
  0.5 0.8 constant_dynamic-slice_fusion
  1.3 3.7 %collective-permute-start.3 = (bf16[4,16,256]{2,1,0:T(8,128)(2,1)S(1)}, bf16[4,16,256]{2,1,0:T(8,128)(2,1)S(1)}, u32[]{:S(2)}, u32[]{:S(2)}) collective-permute-start(bf16[4,16,256]{2,1,0:T(8,128)(2,1)S(1)} %pad_maximum_fusion.3), channel_id=1, source_target_pairs={{0,2},{1,3},{2,0},{3,1},{4,6},{5,7},{6,4},{7,5},{8,10},{9,11},{10,... | collective-permute-start | bytes 98312 | tf_op jit(solution)/shard_map/ppermute | solution.py:444
  5.0 1.3 %collective-permute-start.4 = (bf16[4,16,256]{2,1,0:T(8,128)(2,1)S(1)}, bf16[4,16,256]{2,1,0:T(8,128)(2,1)S(1)}, u32[]{:S(2)}, u32[]{:S(2)}) collective-permute-start(bf16[4,16,256]{2,1,0:T(8,128)(2,1)S(1)} %pad_maximum_fusion.4), channel_id=1, source_target_pairs={{0,3},{1,2},{2,1},{3,0},{4,7},{5,6},{6,5},{7,4},{8,11},{9,10},{10,... | collective-permute-start | bytes 98312 | tf_op jit(solution)/shard_map/ppermute | solution.py:444
  7.0 3.7 %collective-permute-done.4.refs_3_ = bf16[4,16,256]{2,1,0:T(8,128)(2,1)S(1)} collective-permute-done((bf16[4,16,256]{2,1,0:T(8,128)(2,1)S(1)}, bf16[4,16,256]{2,1,0:T(8,128)(2,1)S(1)}, u32[]{:S(2)}, u32[]{:S(2)}) %collective-permute-start.4) | collective-permute-done | bytes 32800 | tf_op jit(solution)/shard_map/ppermute | solution.py:444
  10.8 1.6 %collective-permute-start.5 = (bf16[4,64,256]{2,1,0:T(8,128)(2,1)S(1)}, bf16[4,64,256]{2,1,0:T(8,128)(2,1)S(1)}, u32[]{:S(2)}, u32[]{:S(2)}) collective-permute-start(bf16[4,64,256]{2,1,0:T(8,128)(2,1)S(1)} %shard_map.109.refs_2_), channel_id=1, source_target_pairs={{0,8},{4,12},{8,0},{12,4},{1,9},{5,13},{9,1},{13,5},{2,10},{6,14},... | collective-permute-start | bytes 393224 | tf_op jit(solution)/shard_map/ppermute | solution.py:447
  12.5 1.3 %collective-permute-start = (f32[64,16]{1,0:T(8,128)S(1)}, f32[64,16]{1,0:T(8,128)S(1)}, u32[]{:S(2)}, u32[]{:S(2)}) collective-permute-start(f32[64,16]{1,0:T(8,128)S(1)} %copy.15.route_ref), channel_id=1, source_target_pairs={{0,2},{1,3},{2,0},{3,1},{4,6},{5,7},{6,4},{7,5},{8,10},{9,11},{10,... | collective-permute-start | bytes 12296 | tf_op jit(solution)/shard_map/ppermute | solution.py:444
  13.7 2.1 %collective-permute-done.5.refs_4_ = bf16[4,64,256]{2,1,0:T(8,128)(2,1)S(1)} collective-permute-done((bf16[4,64,256]{2,1,0:T(8,128)(2,1)S(1)}, bf16[4,64,256]{2,1,0:T(8,128)(2,1)S(1)}, u32[]{:S(2)}, u32[]{:S(2)}) %collective-permute-start.5) | collective-permute-done | bytes 131104 | tf_op jit(solution)/shard_map/ppermute | solution.py:447
  16.0 1.2 %collective-permute-done.6.refs_0_ = bf16[4,64,256]{2,1,0:T(8,128)(2,1)S(1)} collective-permute-done((bf16[4,64,256]{2,1,0:T(8,128)(2,1)S(1)}, bf16[4,64,256]{2,1,0:T(8,128)(2,1)S(1)}, u32[]{:S(2)}, u32[]{:S(2)}) %collective-permute-start.6) | collective-permute-done | bytes 131104 | tf_op jit(solution)/shard_map/ppermute | solution.py:447
  17.2 2.9 %shard_map.111 = (bf16[128,1024]{1,0:T(8,128)(2,1)S(1)}, bf16[128,1024]{1,0:T(8,128)(2,1)S(1)}) custom-call(s32[3]{0:T(128)S(1)} %pad_add_fusion.at_ref, bf16[4,64,256]{2,1,0:T(8,128)(2,1)S(1)} %collective-permute-done.6.refs_0_, bf16[4,64,1024]{2,1,0:T(8,128)(2,1)} %refs_1_.3, bf16[4,64,256]{2,1,0:T(8,128)(2,1)} %copy-done.4, ...), custom_call_target="tpu_custom_call" | custom-call | flops 2000000000 | bytes 4194304 | tf_op jit(solution)/shard_map/pallas_call | solution.py:498
  20.2 1.6 %collective-permute-start.15 = (bf16[128,1024]{1,0:T(8,128)(2,1)S(1)}, bf16[128,1024]{1,0:T(8,128)(2,1)S(1)}, u32[]{:S(2)}, u32[]{:S(2)}) collective-permute-start(bf16[128,1024]{1,0:T(8,128)(2,1)S(1)} %get-tuple-element.57), channel_id=1, source_target_pairs={{0,8},{4,12},{8,0},{12,4},{1,9},{5,13},{9,1},{13,5},{2,10},{6,14},... | collective-permute-start | bytes 786440 | tf_op jit(solution)/shard_map/ppermute | solution.py:447
  21.8 2.9 %shard_map.110 = (bf16[128,1024]{1,0:T(8,128)(2,1)S(1)}, bf16[128,1024]{1,0:T(8,128)(2,1)S(1)}) custom-call(s32[3]{0:T(128)S(1)} %pad_add_fusion.at_ref, bf16[4,64,256]{2,1,0:T(8,128)(2,1)S(1)} %collective-permute-done.6.refs_0_, bf16[4,64,1024]{2,1,0:T(8,128)(2,1)} %refs_1_.3, bf16[4,64,256]{2,1,0:T(8,128)(2,1)} %copy-done.4, ...), custom_call_target="tpu_custom_call" | custom-call | flops 2000000000 | bytes 4194304 | tf_op jit(solution)/shard_map/pallas_call | solution.py:498
  25.3 1.5 %collective-permute-start.17 = (bf16[64,1024]{1,0:T(8,128)(2,1)S(1)}, bf16[64,1024]{1,0:T(8,128)(2,1)S(1)}, u32[]{:S(2)}, u32[]{:S(2)}) collective-permute-start(bf16[64,1024]{1,0:T(8,128)(2,1)S(1)} %pad_maximum_fusion), channel_id=1, source_target_pairs={{0,8},{4,12},{8,0},{12,4},{1,9},{5,13},{9,1},{13,5},{2,10},{6,14},... | collective-permute-start | bytes 393224 | tf_op jit(solution)/shard_map/ppermute | solution.py:447
  26.8 1.8 %collective-permute-done.8 = bf16[128,1024]{1,0:T(8,128)(2,1)S(1)} collective-permute-done((bf16[128,1024]{1,0:T(8,128)(2,1)S(1)}, bf16[128,1024]{1,0:T(8,128)(2,1)S(1)}, u32[]{:S(2)}, u32[]{:S(2)}) %collective-permute-start.8) | collective-permute-done | bytes 262176 | tf_op jit(solution)/shard_map/ppermute | solution.py:444
  28.6 1.5 %collective-permute-start.9 = (bf16[128,1024]{1,0:T(8,128)(2,1)S(1)}, bf16[128,1024]{1,0:T(8,128)(2,1)S(1)}, u32[]{:S(2)}, u32[]{:S(2)}) collective-permute-start(bf16[128,1024]{1,0:T(8,128)(2,1)S(1)} %add_convert_fusion.9.sent), channel_id=1, source_target_pairs={{0,2},{1,3},{2,0},{3,1},{4,6},{5,7},{6,4},{7,5},{8,10},{9,11},{10,... | collective-permute-start | bytes 786440 | tf_op jit(solution)/shard_map/ppermute | solution.py:444
  30.1 2.0 %shard_map.114 = bf16[128,1024]{1,0:T(8,128)(2,1)S(1)} custom-call(bf16[128,1024]{1,0:T(8,128)(2,1)S(1)} %collective-permute-done.15.attended_ref, f32[64,16]{1,0:T(8,128)S(1)} %collective-permute-done.other_route_ref.order_ref, bf16[1024,512]{1,0:T(8,128)(2,1)} %refs_0_.3, bf16[1024,512]{1,0:T(8,128)(2,1)} %copy-done.8), custom_call_target="tpu_custom_call" | custom-call | flops 2000000000 | bytes 4194304 | tf_op jit(solution)/shard_map/pallas_call | solution.py:587
  32.2 1.4 %collective-permute-start.16 = (bf16[128,1024]{1,0:T(8,128)(2,1)S(1)}, bf16[128,1024]{1,0:T(8,128)(2,1)S(1)}, u32[]{:S(2)}, u32[]{:S(2)}) collective-permute-start(bf16[128,1024]{1,0:T(8,128)(2,1)S(1)} %shard_map.114), channel_id=1, source_target_pairs={{0,1},{1,0},{2,3},{3,2},{4,5},{5,4},{6,7},{7,6},{8,9},{9,8},{10,11... | collective-permute-start | bytes 786440 | tf_op jit(solution)/shard_map/ppermute | solution.py:444
  33.6 1.5 %collective-permute-done.14.attended_ref = bf16[128,1024]{1,0:T(8,128)(2,1)S(1)} collective-permute-done((bf16[128,1024]{1,0:T(8,128)(2,1)S(1)}, bf16[128,1024]{1,0:T(8,128)(2,1)S(1)}, u32[]{:S(2)}, u32[]{:S(2)}) %collective-permute-start.14) | collective-permute-done | bytes 262176 | tf_op jit(solution)/shard_map/ppermute | solution.py:447
  35.1 2.0 %shard_map.113 = bf16[128,1024]{1,0:T(8,128)(2,1)S(1)} custom-call(bf16[128,1024]{1,0:T(8,128)(2,1)S(1)} %collective-permute-done.14.attended_ref, f32[64,16]{1,0:T(8,128)S(1)} %collective-permute-done.other_route_ref.order_ref, bf16[1024,512]{1,0:T(8,128)(2,1)} %refs_0_.3, bf16[1024,512]{1,0:T(8,128)(2,1)} %copy-done.8), custom_call_target="tpu_custom_call" | custom-call | flops 2000000000 | bytes 4194304 | tf_op jit(solution)/shard_map/pallas_call | solution.py:587
  37.1 5.8 %collective-permute-done.9.came_ref = bf16[128,1024]{1,0:T(8,128)(2,1)S(1)} collective-permute-done((bf16[128,1024]{1,0:T(8,128)(2,1)S(1)}, bf16[128,1024]{1,0:T(8,128)(2,1)S(1)}, u32[]{:S(2)}, u32[]{:S(2)}) %collective-permute-start.9) | collective-permute-done | bytes 262176 | tf_op jit(solution)/shard_map/ppermute | solution.py:444
  43.4 1.5 %collective-permute-start.10 = (bf16[128,1152]{1,0:T(8,128)(2,1)S(1)}, bf16[128,1152]{1,0:T(8,128)(2,1)S(1)}, u32[]{:S(2)}, u32[]{:S(2)}) collective-permute-start(bf16[128,1152]{1,0:T(8,128)(2,1)S(1)} %get-tuple-element.53), channel_id=1, source_target_pairs={{0,8},{4,12},{8,0},{12,4},{1,9},{5,13},{9,1},{13,5},{2,10},{6,14},... | collective-permute-start | bytes 884744 | tf_op jit(solution)/shard_map/ppermute | solution.py:447
  45.1 2.5 %collective-permute-start.18 = (bf16[128,1024]{1,0:T(8,128)(2,1)S(1)}, bf16[128,1024]{1,0:T(8,128)(2,1)S(1)}, u32[]{:S(2)}, u32[]{:S(2)}) collective-permute-start(bf16[128,1024]{1,0:T(8,128)(2,1)S(1)} %add_convert_fusion.8.refs_5_), channel_id=1, source_target_pairs={{0,2},{1,3},{2,0},{3,1},{4,6},{5,7},{6,4},{7,5},{8,10},{9,11},{10,... | collective-permute-start | bytes 786440 | tf_op jit(solution)/shard_map/ppermute | solution.py:444
  47.7 3.2 %collective-permute-done.11.refs_1_.refs_0_ = bf16[64,1152]{1,0:T(8,128)(2,1)S(1)} collective-permute-done((bf16[64,1152]{1,0:T(8,128)(2,1)S(1)}, bf16[64,1152]{1,0:T(8,128)(2,1)S(1)}, u32[]{:S(2)}, u32[]{:S(2)}) %collective-permute-start.11) | collective-permute-done | bytes 147488 | tf_op jit(solution)/shard_map/ppermute | solution.py:444
  50.9 1.4 %collective-permute-done.10.refs_0_.refs_2_ = bf16[128,1152]{1,0:T(8,128)(2,1)S(1)} collective-permute-done((bf16[128,1152]{1,0:T(8,128)(2,1)S(1)}, bf16[128,1152]{1,0:T(8,128)(2,1)S(1)}, u32[]{:S(2)}, u32[]{:S(2)}) %collective-permute-start.10) | collective-permute-done | bytes 294944 | tf_op jit(solution)/shard_map/ppermute | solution.py:447
  52.3 1.5 %collective-permute-start.12 = (bf16[64,1152]{1,0:T(8,128)(2,1)S(1)}, bf16[64,1152]{1,0:T(8,128)(2,1)S(1)}, u32[]{:S(2)}, u32[]{:S(2)}) collective-permute-start(bf16[64,1152]{1,0:T(8,128)(2,1)S(1)} %collective-permute-done.11.refs_1_.refs_0_), channel_id=1, source_target_pairs={{0,8},{4,12},{8,0},{12,4},{1,9},{5,13},{9,1},{13,5},{2,10},{6,14},... | collective-permute-start | bytes 442376 | tf_op jit(solution)/shard_map/ppermute | solution.py:447
  53.8 1.7 %collective-permute-start.20 = (bf16[64,1152]{1,0:T(8,128)(2,1)S(1)}, bf16[64,1152]{1,0:T(8,128)(2,1)S(1)}, u32[]{:S(2)}, u32[]{:S(2)}) collective-permute-start(bf16[64,1152]{1,0:T(8,128)(2,1)S(1)} %slice.72), channel_id=1, source_target_pairs={{0,1},{1,0},{2,3},{3,2},{4,5},{5,4},{6,7},{7,6},{8,9},{9,8},{10,11... | collective-permute-start | bytes 442376 | tf_op jit(solution)/shard_map/ppermute | solution.py:444
  55.5 1.6 %collective-permute-done.13.refs_3_.refs_0_ = bf16[64,1152]{1,0:T(8,128)(2,1)S(1)} collective-permute-done((bf16[64,1152]{1,0:T(8,128)(2,1)S(1)}, bf16[64,1152]{1,0:T(8,128)(2,1)S(1)}, u32[]{:S(2)}, u32[]{:S(2)}) %collective-permute-start.13) | collective-permute-done | bytes 147488 | tf_op jit(solution)/shard_map/ppermute | solution.py:444
  57.1 2.5 %collective-permute-done.18.refs_4_ = bf16[128,1024]{1,0:T(8,128)(2,1)S(1)} collective-permute-done((bf16[128,1024]{1,0:T(8,128)(2,1)S(1)}, bf16[128,1024]{1,0:T(8,128)(2,1)S(1)}, u32[]{:S(2)}, u32[]{:S(2)}) %collective-permute-start.18) | collective-permute-done | bytes 262176 | tf_op jit(solution)/shard_map/ppermute | solution.py:444
  60.3 1.7 %collective-permute-done.20.refs_2_ = bf16[64,1152]{1,0:T(8,128)(2,1)S(1)} collective-permute-done((bf16[64,1152]{1,0:T(8,128)(2,1)S(1)}, bf16[64,1152]{1,0:T(8,128)(2,1)S(1)}, u32[]{:S(2)}, u32[]{:S(2)}) %collective-permute-start.20) | collective-permute-done | bytes 147488 | tf_op jit(solution)/shard_map/ppermute | solution.py:444
  62.0 5.0 %collective-permute-done.21.refs_1_ = bf16[64,1024]{1,0:T(8,128)(2,1)S(1)} collective-permute-done((bf16[64,1024]{1,0:T(8,128)(2,1)S(1)}, bf16[64,1024]{1,0:T(8,128)(2,1)S(1)}, u32[]{:S(2)}, u32[]{:S(2)}) %collective-permute-start.21) | collective-permute-done | bytes 131104 | tf_op jit(solution)/shard_map/ppermute | solution.py:444
  67.8 1.8 %collective-permute-start.24 = (bf16[64,1024]{1,0:T(8,128)(2,1)S(1)}, bf16[64,1024]{1,0:T(8,128)(2,1)S(1)}, u32[]{:S(2)}, u32[]{:S(2)}) collective-permute-start(bf16[64,1024]{1,0:T(8,128)(2,1)S(1)} %slice.73), channel_id=1, source_target_pairs={{0,1},{1,0},{2,3},{3,2},{4,5},{5,4},{6,7},{7,6},{8,9},{9,8},{10,11... | collective-permute-start | bytes 393224 | tf_op jit(solution)/shard_map/ppermute | solution.py:444
  69.6 2.6 %collective-permute-done.23.refs_1_ = bf16[64,1024]{1,0:T(8,128)(2,1)S(1)} collective-permute-done((bf16[64,1024]{1,0:T(8,128)(2,1)S(1)}, bf16[64,1024]{1,0:T(8,128)(2,1)S(1)}, u32[]{:S(2)}, u32[]{:S(2)}) %collective-permute-start.23) | collective-permute-done | bytes 131104 | tf_op jit(solution)/shard_map/ppermute | solution.py:444
  72.2 1.4 %collective-permute-done.24.refs_3_ = bf16[64,1024]{1,0:T(8,128)(2,1)S(1)} collective-permute-done((bf16[64,1024]{1,0:T(8,128)(2,1)S(1)}, bf16[64,1024]{1,0:T(8,128)(2,1)S(1)}, u32[]{:S(2)}, u32[]{:S(2)}) %collective-permute-start.24) | collective-permute-done | bytes 131104 | tf_op jit(solution)/shard_map/ppermute | solution.py:444
  74.5 0.8 shard_map.117.refs_0_
  75.3 1.1 collective-permute-done.25.refs_1_
  76.5 3.2 %shard_map.118 = (bf16[128,2048]{1,0:T(8,128)(2,1)S(1)}, bf16[128,2048]{1,0:T(8,128)(2,1)S(1)}) custom-call(s32[3]{0:T(128)S(1)} %pad_add_fusion.at_ref, bf16[128,2176]{1,0:T(8,128)(2,1)S(1)} %shard_map.116.refs_0_, bf16[128,2176]{1,0:T(8,128)(2,1)S(1)} %collective-permute-done.25.refs_1_, bf16[1,2048,768]{2,1,0:T(8,128)(2,1)S(1)} %copy-done, ...), custom_call_target="tpu_custom_call" | custom-call | flops 1 | bytes 1 | tf_op jit(solution)/shard_map/pallas_call | solution.py:398
  81.3 0.8 shard_map.119
  83.2 3.2 %shard_map.121 = (bf16[128,2048]{1,0:T(8,128)(2,1)S(1)}, bf16[128,2048]{1,0:T(8,128)(2,1)S(1)}) custom-call(s32[3]{0:T(128)S(1)} %pad_add_fusion.at_ref, bf16[128,2176]{1,0:T(8,128)(2,1)S(1)} %shard_map.120.refs_0_, bf16[128,2176]{1,0:T(8,128)(2,1)S(1)} %collective-permute-done.28.refs_1_, bf16[1,2048,768]{2,1,0:T(8,128)(2,1)S(1)} %copy-done, ...), custom_call_target="tpu_custom_call" | custom-call | flops 1 | bytes 1 | tf_op jit(solution)/shard_map/pallas_call | solution.py:398
  87.0 3.4 %shard_map.122 = (bf16[128,2048]{1,0:T(8,128)(2,1)S(1)}, bf16[128,2048]{1,0:T(8,128)(2,1)S(1)}) custom-call(s32[3]{0:T(128)S(1)} %pad_add_fusion.at_ref, bf16[128,2176]{1,0:T(8,128)(2,1)S(1)} %shard_map.117.refs_0_, bf16[128,2176]{1,0:T(8,128)(2,1)S(1)} %collective-permute-done.27.refs_1_, bf16[1,2048,768]{2,1,0:T(8,128)(2,1)S(1)} %copy-done, ...), custom_call_target="tpu_custom_call" | custom-call | flops 1 | bytes 1 | tf_op jit(solution)/shard_map/pallas_call | solution.py:398
  90.9 1.3 %collective-permute-start.38 = (bf16[64,2048]{1,0:T(8,128)(2,1)S(1)}, bf16[64,2048]{1,0:T(8,128)(2,1)S(1)}, u32[]{:S(2)}, u32[]{:S(2)}) collective-permute-start(bf16[64,2048]{1,0:T(8,128)(2,1)S(1)} %add_convert_fusion.2), channel_id=1, source_target_pairs={{0,1},{1,0},{2,3},{3,2},{4,5},{5,4},{6,7},{7,6},{8,9},{9,8},{10,11... | collective-permute-start | bytes 786440 | tf_op jit(solution)/shard_map/ppermute | solution.py:444
  92.3 1.3 %collective-permute-start.32 = (bf16[64,2048]{1,0:T(8,128)(2,1)S(1)}, bf16[64,2048]{1,0:T(8,128)(2,1)S(1)}, u32[]{:S(2)}, u32[]{:S(2)}) collective-permute-start(bf16[64,2048]{1,0:T(8,128)(2,1)S(1)} %add_convert_fusion.6), channel_id=1, source_target_pairs={{0,8},{4,12},{8,0},{12,4},{1,9},{5,13},{9,1},{13,5},{2,10},{6,14},... | collective-permute-start | bytes 786440 | tf_op jit(solution)/shard_map/ppermute | solution.py:447
  93.6 3.2 %shard_map.123 = (bf16[128,2048]{1,0:T(8,128)(2,1)S(1)}, bf16[128,2048]{1,0:T(8,128)(2,1)S(1)}) custom-call(s32[3]{0:T(128)S(1)} %pad_add_fusion.at_ref, bf16[128,2176]{1,0:T(8,128)(2,1)S(1)} %get-tuple-element.83.refs_0_, bf16[128,2176]{1,0:T(8,128)(2,1)S(1)} %collective-permute-done.26.refs_1_, bf16[1,2048,768]{2,1,0:T(8,128)(2,1)S(1)} %copy-done, ...), custom_call_target="tpu_custom_call" | custom-call | flops 1 | bytes 1 | tf_op jit(solution)/shard_map/pallas_call | solution.py:398
  96.9 0.8 collective-permute-start.36
  97.7 3.8 %collective-permute-done.32 = bf16[64,2048]{1,0:T(8,128)(2,1)S(1)} collective-permute-done((bf16[64,2048]{1,0:T(8,128)(2,1)S(1)}, bf16[64,2048]{1,0:T(8,128)(2,1)S(1)}, u32[]{:S(2)}, u32[]{:S(2)}) %collective-permute-start.32) | collective-permute-done | bytes 262176 | tf_op jit(solution)/shard_map/ppermute | solution.py:447
  102.1 4.2 %collective-permute-done.36 = bf16[64,2048]{1,0:T(8,128)(2,1)S(1)} collective-permute-done((bf16[64,2048]{1,0:T(8,128)(2,1)S(1)}, bf16[64,2048]{1,0:T(8,128)(2,1)S(1)}, u32[]{:S(2)}, u32[]{:S(2)}) %collective-permute-start.36) | collective-permute-done | bytes 262176 | tf_op jit(solution)/shard_map/ppermute | solution.py:447
  106.4 1.0 collective-permute-start.37
  108.2 8.8 %collective-permute-done.39 = bf16[64,2048]{1,0:T(8,128)(2,1)S(1)} collective-permute-done((bf16[64,2048]{1,0:T(8,128)(2,1)S(1)}, bf16[64,2048]{1,0:T(8,128)(2,1)S(1)}, u32[]{:S(2)}, u32[]{:S(2)}) %collective-permute-start.39) | collective-permute-done | bytes 262176 | tf_op jit(solution)/shard_map/ppermute | solution.py:444
  117.0 2.3 %collective-permute-done.37 = bf16[64,2048]{1,0:T(8,128)(2,1)S(1)} collective-permute-done((bf16[64,2048]{1,0:T(8,128)(2,1)S(1)}, bf16[64,2048]{1,0:T(8,128)(2,1)S(1)}, u32[]{:S(2)}, u32[]{:S(2)}) %collective-permute-start.37) | collective-permute-done | bytes 262176 | tf_op jit(solution)/shard_map/ppermute | solution.py:444
  119.3 0.9 fusion.2
  (92 shorter events, 10.8 us)
Async XLA Ops:
  0.0 6.3 %collective-permute-start.1 = (bf16[1024,512]{1,0:T(8,128)(2,1)}, bf16[1024,512]{1,0:T(8,128)(2,1)S(1)}, u32[]{:S(2)}, u32[]{:S(2)}) collective-permute-start(bf16[1024,512]{1,0:T(8,128)(2,1)} %refs_0_.3), channel_id=1, source_target_pairs={{0,4},{4,0},{8,12},{12,8},{1,5},{5,1},{9,13},{13,9},{2,6},{6,2},{1... | collective-permute-start | bytes 3145736 | tf_op jit(solution)/shard_map/ppermute | solution.py:447
  1.3 5.7 %collective-permute-start.3 = (bf16[4,16,256]{2,1,0:T(8,128)(2,1)S(1)}, bf16[4,16,256]{2,1,0:T(8,128)(2,1)S(1)}, u32[]{:S(2)}, u32[]{:S(2)}) collective-permute-start(bf16[4,16,256]{2,1,0:T(8,128)(2,1)S(1)} %pad_maximum_fusion.3), channel_id=1, source_target_pairs={{0,2},{1,3},{2,0},{3,1},{4,6},{5,7},{6,4},{7,5},{8,10},{9,11},{10,... | collective-permute-start | bytes 98312 | tf_op jit(solution)/shard_map/ppermute | solution.py:444
  5.0 5.8 %collective-permute-start.4 = (bf16[4,16,256]{2,1,0:T(8,128)(2,1)S(1)}, bf16[4,16,256]{2,1,0:T(8,128)(2,1)S(1)}, u32[]{:S(2)}, u32[]{:S(2)}) collective-permute-start(bf16[4,16,256]{2,1,0:T(8,128)(2,1)S(1)} %pad_maximum_fusion.4), channel_id=1, source_target_pairs={{0,3},{1,2},{2,1},{3,0},{4,7},{5,6},{6,5},{7,4},{8,11},{9,10},{10,... | collective-permute-start | bytes 98312 | tf_op jit(solution)/shard_map/ppermute | solution.py:444
  6.3 4.4 %collective-permute-start.2 = (bf16[4,16,256]{2,1,0:T(8,128)(2,1)S(1)}, bf16[4,16,256]{2,1,0:T(8,128)(2,1)S(1)}, u32[]{:S(2)}, u32[]{:S(2)}) collective-permute-start(bf16[4,16,256]{2,1,0:T(8,128)(2,1)S(1)} %pad_maximum_fusion.2), channel_id=1, source_target_pairs={{0,1},{1,0},{2,3},{3,2},{4,5},{5,4},{6,7},{7,6},{8,9},{9,8},{10,11... | collective-permute-start | bytes 98312 | tf_op jit(solution)/shard_map/ppermute | solution.py:444
  6.7 5.7 %copy-start.6 = (s32[1,64,8]{1,2,0:T(8,128)S(1)}, s32[1,64,8]{1,2,0:T(8,128)}, u32[]{:S(2)}) copy-start(s32[1,64,8]{1,2,0:T(8,128)} %param.17) | copy-start | bytes 6148
  6.7 5.7 %copy-start.7 = (f32[1,64,8]{1,2,0:T(8,128)S(1)}, f32[1,64,8]{1,2,0:T(8,128)}, u32[]{:S(2)}) copy-start(f32[1,64,8]{1,2,0:T(8,128)} %param.18) | copy-start | bytes 6148
  6.7 9.3 %copy-start.5 = (bf16[1,64,2048]{2,1,0:T(8,128)(2,1)S(1)}, bf16[1,64,2048]{2,1,0:T(8,128)(2,1)}, u32[]{:S(2)}) copy-start(bf16[1,64,2048]{2,1,0:T(8,128)(2,1)} %param.15) | copy-start | bytes 786436
  10.8 6.4 %copy-start.4 = (bf16[4,64,256]{2,1,0:T(8,128)(2,1)}, bf16[4,64,256]{2,1,0:T(8,128)(2,1)S(1)}, u32[]{:S(2)}) copy-start(bf16[4,64,256]{2,1,0:T(8,128)(2,1)S(1)} %shard_map.109.refs_2_) | copy-start | bytes 393220
  10.8 5.0 %collective-permute-start.5 = (bf16[4,64,256]{2,1,0:T(8,128)(2,1)S(1)}, bf16[4,64,256]{2,1,0:T(8,128)(2,1)S(1)}, u32[]{:S(2)}, u32[]{:S(2)}) collective-permute-start(bf16[4,64,256]{2,1,0:T(8,128)(2,1)S(1)} %shard_map.109.refs_2_), channel_id=1, source_target_pairs={{0,8},{4,12},{8,0},{12,4},{1,9},{5,13},{9,1},{13,5},{2,10},{6,14},... | collective-permute-start | bytes 393224 | tf_op jit(solution)/shard_map/ppermute | solution.py:447
  12.5 17.7 %collective-permute-start = (f32[64,16]{1,0:T(8,128)S(1)}, f32[64,16]{1,0:T(8,128)S(1)}, u32[]{:S(2)}, u32[]{:S(2)}) collective-permute-start(f32[64,16]{1,0:T(8,128)S(1)} %copy.15.route_ref), channel_id=1, source_target_pairs={{0,2},{1,3},{2,0},{3,1},{4,6},{5,7},{6,4},{7,5},{8,10},{9,11},{10,... | collective-permute-start | bytes 12296 | tf_op jit(solution)/shard_map/ppermute | solution.py:444
  13.7 2.2 %collective-permute-start.7 = (bf16[4,64,256]{2,1,0:T(8,128)(2,1)S(1)}, bf16[4,64,256]{2,1,0:T(8,128)(2,1)S(1)}, u32[]{:S(2)}, u32[]{:S(2)}) collective-permute-start(bf16[4,64,256]{2,1,0:T(8,128)(2,1)S(1)} %shard_map.109.refs_2_), channel_id=1, source_target_pairs={{0,4},{4,0},{8,12},{12,8},{1,5},{5,1},{9,13},{13,9},{2,6},{6,2},{1... | collective-permute-start | bytes 393224 | tf_op jit(solution)/shard_map/ppermute | solution.py:447
  15.9 1.3 %collective-permute-start.6 = (bf16[4,64,256]{2,1,0:T(8,128)(2,1)S(1)}, bf16[4,64,256]{2,1,0:T(8,128)(2,1)S(1)}, u32[]{:S(2)}, u32[]{:S(2)}) collective-permute-start(bf16[4,64,256]{2,1,0:T(8,128)(2,1)S(1)} %collective-permute-done.5.refs_4_), channel_id=1, source_target_pairs={{0,4},{4,0},{8,12},{12,8},{1,5},{5,1},{9,13},{13,9},{2,6},{6,2},{1... | collective-permute-start | bytes 393224 | tf_op jit(solution)/shard_map/ppermute | solution.py:447
  20.1 8.4 %collective-permute-start.8 = (bf16[128,1024]{1,0:T(8,128)(2,1)S(1)}, bf16[128,1024]{1,0:T(8,128)(2,1)S(1)}, u32[]{:S(2)}, u32[]{:S(2)}) collective-permute-start(bf16[128,1024]{1,0:T(8,128)(2,1)S(1)} %get-tuple-element.51), channel_id=1, source_target_pairs={{0,1},{1,0},{2,3},{3,2},{4,5},{5,4},{6,7},{7,6},{8,9},{9,8},{10,11... | collective-permute-start | bytes 786440 | tf_op jit(solution)/shard_map/ppermute | solution.py:444
  20.2 9.9 %collective-permute-start.15 = (bf16[128,1024]{1,0:T(8,128)(2,1)S(1)}, bf16[128,1024]{1,0:T(8,128)(2,1)S(1)}, u32[]{:S(2)}, u32[]{:S(2)}) collective-permute-start(bf16[128,1024]{1,0:T(8,128)(2,1)S(1)} %get-tuple-element.57), channel_id=1, source_target_pairs={{0,8},{4,12},{8,0},{12,4},{1,9},{5,13},{9,1},{13,5},{2,10},{6,14},... | collective-permute-start | bytes 786440 | tf_op jit(solution)/shard_map/ppermute | solution.py:447
  24.7 10.4 %collective-permute-start.14 = (bf16[128,1024]{1,0:T(8,128)(2,1)S(1)}, bf16[128,1024]{1,0:T(8,128)(2,1)S(1)}, u32[]{:S(2)}, u32[]{:S(2)}) collective-permute-start(bf16[128,1024]{1,0:T(8,128)(2,1)S(1)} %get-tuple-element.56), channel_id=1, source_target_pairs={{0,8},{4,12},{8,0},{12,4},{1,9},{5,13},{9,1},{13,5},{2,10},{6,14},... | collective-permute-start | bytes 786440 | tf_op jit(solution)/shard_map/ppermute | solution.py:447
  25.3 19.6 %collective-permute-start.17 = (bf16[64,1024]{1,0:T(8,128)(2,1)S(1)}, bf16[64,1024]{1,0:T(8,128)(2,1)S(1)}, u32[]{:S(2)}, u32[]{:S(2)}) collective-permute-start(bf16[64,1024]{1,0:T(8,128)(2,1)S(1)} %pad_maximum_fusion), channel_id=1, source_target_pairs={{0,8},{4,12},{8,0},{12,4},{1,9},{5,13},{9,1},{13,5},{2,10},{6,14},... | collective-permute-start | bytes 393224 | tf_op jit(solution)/shard_map/ppermute | solution.py:447
  28.6 14.2 %collective-permute-start.9 = (bf16[128,1024]{1,0:T(8,128)(2,1)S(1)}, bf16[128,1024]{1,0:T(8,128)(2,1)S(1)}, u32[]{:S(2)}, u32[]{:S(2)}) collective-permute-start(bf16[128,1024]{1,0:T(8,128)(2,1)S(1)} %add_convert_fusion.9.sent), channel_id=1, source_target_pairs={{0,2},{1,3},{2,0},{3,1},{4,6},{5,7},{6,4},{7,5},{8,10},{9,11},{10,... | collective-permute-start | bytes 786440 | tf_op jit(solution)/shard_map/ppermute | solution.py:444
  32.2 12.8 %collective-permute-start.16 = (bf16[128,1024]{1,0:T(8,128)(2,1)S(1)}, bf16[128,1024]{1,0:T(8,128)(2,1)S(1)}, u32[]{:S(2)}, u32[]{:S(2)}) collective-permute-start(bf16[128,1024]{1,0:T(8,128)(2,1)S(1)} %shard_map.114), channel_id=1, source_target_pairs={{0,1},{1,0},{2,3},{3,2},{4,5},{5,4},{6,7},{7,6},{8,9},{9,8},{10,11... | collective-permute-start | bytes 786440 | tf_op jit(solution)/shard_map/ppermute | solution.py:444
  43.3 7.6 %collective-permute-start.11 = (bf16[64,1152]{1,0:T(8,128)(2,1)S(1)}, bf16[64,1152]{1,0:T(8,128)(2,1)S(1)}, u32[]{:S(2)}, u32[]{:S(2)}) collective-permute-start(bf16[64,1152]{1,0:T(8,128)(2,1)S(1)} %get-tuple-element.54.refs_0_), channel_id=1, source_target_pairs={{0,1},{1,0},{2,3},{3,2},{4,5},{5,4},{6,7},{7,6},{8,9},{9,8},{10,11... | collective-permute-start | bytes 442376 | tf_op jit(solution)/shard_map/ppermute | solution.py:444
  43.4 8.9 %collective-permute-start.10 = (bf16[128,1152]{1,0:T(8,128)(2,1)S(1)}, bf16[128,1152]{1,0:T(8,128)(2,1)S(1)}, u32[]{:S(2)}, u32[]{:S(2)}) collective-permute-start(bf16[128,1152]{1,0:T(8,128)(2,1)S(1)} %get-tuple-element.53), channel_id=1, source_target_pairs={{0,8},{4,12},{8,0},{12,4},{1,9},{5,13},{9,1},{13,5},{2,10},{6,14},... | collective-permute-start | bytes 884744 | tf_op jit(solution)/shard_map/ppermute | solution.py:447
  45.1 14.5 %collective-permute-start.18 = (bf16[128,1024]{1,0:T(8,128)(2,1)S(1)}, bf16[128,1024]{1,0:T(8,128)(2,1)S(1)}, u32[]{:S(2)}, u32[]{:S(2)}) collective-permute-start(bf16[128,1024]{1,0:T(8,128)(2,1)S(1)} %add_convert_fusion.8.refs_5_), channel_id=1, source_target_pairs={{0,2},{1,3},{2,0},{3,1},{4,6},{5,7},{6,4},{7,5},{8,10},{9,11},{10,... | collective-permute-start | bytes 786440 | tf_op jit(solution)/shard_map/ppermute | solution.py:444
  47.6 9.6 %collective-permute-start.13 = (bf16[64,1152]{1,0:T(8,128)(2,1)S(1)}, bf16[64,1152]{1,0:T(8,128)(2,1)S(1)}, u32[]{:S(2)}, u32[]{:S(2)}) collective-permute-start(bf16[64,1152]{1,0:T(8,128)(2,1)S(1)} %get-tuple-element.52.refs_0_), channel_id=1, source_target_pairs={{0,1},{1,0},{2,3},{3,2},{4,5},{5,4},{6,7},{7,6},{8,9},{9,8},{10,11... | collective-permute-start | bytes 442376 | tf_op jit(solution)/shard_map/ppermute | solution.py:444
  52.3 7.3 %collective-permute-start.12 = (bf16[64,1152]{1,0:T(8,128)(2,1)S(1)}, bf16[64,1152]{1,0:T(8,128)(2,1)S(1)}, u32[]{:S(2)}, u32[]{:S(2)}) collective-permute-start(bf16[64,1152]{1,0:T(8,128)(2,1)S(1)} %collective-permute-done.11.refs_1_.refs_0_), channel_id=1, source_target_pairs={{0,8},{4,12},{8,0},{12,4},{1,9},{5,13},{9,1},{13,5},{2,10},{6,14},... | collective-permute-start | bytes 442376 | tf_op jit(solution)/shard_map/ppermute | solution.py:447
  53.8 19.9 %copy-start.3 = (f32[2048]{0:T(1024)S(1)}, f32[2048]{0:T(1024)}, u32[]{:S(2)}) copy-start(f32[2048]{0:T(1024)} %param.16) | copy-start | bytes 24580
  53.8 22.7 %copy-start = (bf16[1,2048,768]{2,1,0:T(8,128)(2,1)S(1)}, bf16[1,2048,768]{2,1,0:T(8,128)(2,1)}, u32[]{:S(2)}) copy-start(bf16[1,2048,768]{2,1,0:T(8,128)(2,1)} %refs_2_.7) | copy-start | bytes 9437188
  53.8 22.7 %copy-start.1 = (bf16[1,2048,768]{2,1,0:T(8,128)(2,1)S(1)}, bf16[1,2048,768]{2,1,0:T(8,128)(2,1)}, u32[]{:S(2)}) copy-start(bf16[1,2048,768]{2,1,0:T(8,128)(2,1)} %refs_3_.7) | copy-start | bytes 9437188
  53.8 22.7 %copy-start.2 = (bf16[1,768,2048]{2,1,0:T(8,128)(2,1)S(1)}, bf16[1,768,2048]{2,1,0:T(8,128)(2,1)}, u32[]{:S(2)}) copy-start(bf16[1,768,2048]{2,1,0:T(8,128)(2,1)} %refs_4_.7) | copy-start | bytes 9437188
  53.8 8.2 %collective-permute-start.20 = (bf16[64,1152]{1,0:T(8,128)(2,1)S(1)}, bf16[64,1152]{1,0:T(8,128)(2,1)S(1)}, u32[]{:S(2)}, u32[]{:S(2)}) collective-permute-start(bf16[64,1152]{1,0:T(8,128)(2,1)S(1)} %slice.72), channel_id=1, source_target_pairs={{0,1},{1,0},{2,3},{3,2},{4,5},{5,4},{6,7},{7,6},{8,9},{9,8},{10,11... | collective-permute-start | bytes 442376 | tf_op jit(solution)/shard_map/ppermute | solution.py:444
  59.7 7.3 %collective-permute-start.19 = (bf16[128,1024]{1,0:T(8,128)(2,1)S(1)}, bf16[128,1024]{1,0:T(8,128)(2,1)S(1)}, u32[]{:S(2)}, u32[]{:S(2)}) collective-permute-start(bf16[128,1024]{1,0:T(8,128)(2,1)S(1)} %get-tuple-element.61), channel_id=1, source_target_pairs={{0,8},{4,12},{8,0},{12,4},{1,9},{5,13},{9,1},{13,5},{2,10},{6,14},... | collective-permute-start | bytes 786440 | tf_op jit(solution)/shard_map/ppermute | solution.py:447
  62.0 5.0 %collective-permute-start.21 = (bf16[64,1024]{1,0:T(8,128)(2,1)S(1)}, bf16[64,1024]{1,0:T(8,128)(2,1)S(1)}, u32[]{:S(2)}, u32[]{:S(2)}) collective-permute-start(bf16[64,1024]{1,0:T(8,128)(2,1)S(1)} %get-tuple-element.63.refs_1_), channel_id=1, source_target_pairs={{0,1},{1,0},{2,3},{3,2},{4,5},{5,4},{6,7},{7,6},{8,9},{9,8},{10,11... | collective-permute-start | bytes 393224 | tf_op jit(solution)/shard_map/ppermute | solution.py:444
  67.0 5.2 %collective-permute-start.23 = (bf16[64,1024]{1,0:T(8,128)(2,1)S(1)}, bf16[64,1024]{1,0:T(8,128)(2,1)S(1)}, u32[]{:S(2)}, u32[]{:S(2)}) collective-permute-start(bf16[64,1024]{1,0:T(8,128)(2,1)S(1)} %get-tuple-element.65.refs_1_), channel_id=1, source_target_pairs={{0,1},{1,0},{2,3},{3,2},{4,5},{5,4},{6,7},{7,6},{8,9},{9,8},{10,11... | collective-permute-start | bytes 393224 | tf_op jit(solution)/shard_map/ppermute | solution.py:444
  67.0 5.2 %collective-permute-start.22 = (bf16[64,1024]{1,0:T(8,128)(2,1)S(1)}, bf16[64,1024]{1,0:T(8,128)(2,1)S(1)}, u32[]{:S(2)}, u32[]{:S(2)}) collective-permute-start(bf16[64,1024]{1,0:T(8,128)(2,1)S(1)} %collective-permute-done.21.refs_1_), channel_id=1, source_target_pairs={{0,8},{4,12},{8,0},{12,4},{1,9},{5,13},{9,1},{13,5},{2,10},{6,14},... | collective-permute-start | bytes 393224 | tf_op jit(solution)/shard_map/ppermute | solution.py:447
  67.8 5.8 %collective-permute-start.24 = (bf16[64,1024]{1,0:T(8,128)(2,1)S(1)}, bf16[64,1024]{1,0:T(8,128)(2,1)S(1)}, u32[]{:S(2)}, u32[]{:S(2)}) collective-permute-start(bf16[64,1024]{1,0:T(8,128)(2,1)S(1)} %slice.73), channel_id=1, source_target_pairs={{0,1},{1,0},{2,3},{3,2},{4,5},{5,4},{6,7},{7,6},{8,9},{9,8},{10,11... | collective-permute-start | bytes 393224 | tf_op jit(solution)/shard_map/ppermute | solution.py:444
  74.4 2.0 %collective-permute-start.25 = (bf16[128,2176]{1,0:T(8,128)(2,1)S(1)}, bf16[128,2176]{1,0:T(8,128)(2,1)S(1)}, u32[]{:S(2)}, u32[]{:S(2)}) collective-permute-start(bf16[128,2176]{1,0:T(8,128)(2,1)S(1)} %shard_map.116.refs_0_), channel_id=1, source_target_pairs={{0,4},{4,0},{8,12},{12,8},{1,5},{5,1},{9,13},{13,9},{2,6},{6,2},{1... | collective-permute-start | bytes 1671176 | tf_op jit(solution)/shard_map/ppermute | solution.py:447
  79.7 2.4 %collective-permute-start.29 = (bf16[128,2048]{1,0:T(8,128)(2,1)S(1)}, bf16[128,2048]{1,0:T(8,128)(2,1)S(1)}, u32[]{:S(2)}, u32[]{:S(2)}) collective-permute-start(bf16[128,2048]{1,0:T(8,128)(2,1)S(1)} %get-tuple-element.73), channel_id=1, source_target_pairs={{0,4},{4,0},{8,12},{12,8},{1,5},{5,1},{9,13},{13,9},{2,6},{6,2},{1... | collective-permute-start | bytes 1572872 | tf_op jit(solution)/shard_map/ppermute | solution.py:447
  79.9 7.1 %collective-permute-start.27 = (bf16[128,2176]{1,0:T(8,128)(2,1)S(1)}, bf16[128,2176]{1,0:T(8,128)(2,1)S(1)}, u32[]{:S(2)}, u32[]{:S(2)}) collective-permute-start(bf16[128,2176]{1,0:T(8,128)(2,1)S(1)} %shard_map.117.refs_0_), channel_id=1, source_target_pairs={{0,4},{4,0},{8,12},{12,8},{1,5},{5,1},{9,13},{13,9},{2,6},{6,2},{1... | collective-permute-start | bytes 1671176 | tf_op jit(solution)/shard_map/ppermute | solution.py:447
  81.1 2.2 %collective-permute-start.28 = (bf16[128,2176]{1,0:T(8,128)(2,1)S(1)}, bf16[128,2176]{1,0:T(8,128)(2,1)S(1)}, u32[]{:S(2)}, u32[]{:S(2)}) collective-permute-start(bf16[128,2176]{1,0:T(8,128)(2,1)S(1)} %shard_map.120.refs_0_), channel_id=1, source_target_pairs={{0,4},{4,0},{8,12},{12,8},{1,5},{5,1},{9,13},{13,9},{2,6},{6,2},{1... | collective-permute-start | bytes 1671176 | tf_op jit(solution)/shard_map/ppermute | solution.py:447
  82.2 8.7 %collective-permute-start.31 = (bf16[64,2048]{1,0:T(8,128)(2,1)S(1)}, bf16[64,2048]{1,0:T(8,128)(2,1)S(1)}, u32[]{:S(2)}, u32[]{:S(2)}) collective-permute-start(bf16[64,2048]{1,0:T(8,128)(2,1)S(1)} %add_convert_fusion.7), channel_id=1, source_target_pairs={{0,8},{4,12},{8,0},{12,4},{1,9},{5,13},{9,1},{13,5},{2,10},{6,14},... | collective-permute-start | bytes 786440 | tf_op jit(solution)/shard_map/ppermute | solution.py:447
  86.4 5.8 %collective-permute-start.30 = (bf16[128,2048]{1,0:T(8,128)(2,1)S(1)}, bf16[128,2048]{1,0:T(8,128)(2,1)S(1)}, u32[]{:S(2)}, u32[]{:S(2)}) collective-permute-start(bf16[128,2048]{1,0:T(8,128)(2,1)S(1)} %get-tuple-element.81), channel_id=1, source_target_pairs={{0,4},{4,0},{8,12},{12,8},{1,5},{5,1},{9,13},{13,9},{2,6},{6,2},{1... | collective-permute-start | bytes 1572872 | tf_op jit(solution)/shard_map/ppermute | solution.py:447
  86.6 7.0 %collective-permute-start.26 = (bf16[128,2176]{1,0:T(8,128)(2,1)S(1)}, bf16[128,2176]{1,0:T(8,128)(2,1)S(1)}, u32[]{:S(2)}, u32[]{:S(2)}) collective-permute-start(bf16[128,2176]{1,0:T(8,128)(2,1)S(1)} %get-tuple-element.83.refs_0_), channel_id=1, source_target_pairs={{0,4},{4,0},{8,12},{12,8},{1,5},{5,1},{9,13},{13,9},{2,6},{6,2},{1... | collective-permute-start | bytes 1671176 | tf_op jit(solution)/shard_map/ppermute | solution.py:447
  90.8 6.0 %collective-permute-start.34 = (bf16[128,2048]{1,0:T(8,128)(2,1)S(1)}, bf16[128,2048]{1,0:T(8,128)(2,1)S(1)}, u32[]{:S(2)}, u32[]{:S(2)}) collective-permute-start(bf16[128,2048]{1,0:T(8,128)(2,1)S(1)} %get-tuple-element.89), channel_id=1, source_target_pairs={{0,4},{4,0},{8,12},{12,8},{1,5},{5,1},{9,13},{13,9},{2,6},{6,2},{1... | collective-permute-start | bytes 1572872 | tf_op jit(solution)/shard_map/ppermute | solution.py:447
  90.9 10.6 %collective-permute-start.38 = (bf16[64,2048]{1,0:T(8,128)(2,1)S(1)}, bf16[64,2048]{1,0:T(8,128)(2,1)S(1)}, u32[]{:S(2)}, u32[]{:S(2)}) collective-permute-start(bf16[64,2048]{1,0:T(8,128)(2,1)S(1)} %add_convert_fusion.2), channel_id=1, source_target_pairs={{0,1},{1,0},{2,3},{3,2},{4,5},{5,4},{6,7},{7,6},{8,9},{9,8},{10,11... | collective-permute-start | bytes 786440 | tf_op jit(solution)/shard_map/ppermute | solution.py:444
  92.3 9.2 %collective-permute-start.32 = (bf16[64,2048]{1,0:T(8,128)(2,1)S(1)}, bf16[64,2048]{1,0:T(8,128)(2,1)S(1)}, u32[]{:S(2)}, u32[]{:S(2)}) collective-permute-start(bf16[64,2048]{1,0:T(8,128)(2,1)S(1)} %add_convert_fusion.6), channel_id=1, source_target_pairs={{0,8},{4,12},{8,0},{12,4},{1,9},{5,13},{9,1},{13,5},{2,10},{6,14},... | collective-permute-start | bytes 786440 | tf_op jit(solution)/shard_map/ppermute | solution.py:447
  96.9 9.5 %collective-permute-start.36 = (bf16[64,2048]{1,0:T(8,128)(2,1)S(1)}, bf16[64,2048]{1,0:T(8,128)(2,1)S(1)}, u32[]{:S(2)}, u32[]{:S(2)}) collective-permute-start(bf16[64,2048]{1,0:T(8,128)(2,1)S(1)} %add_convert_fusion.4), channel_id=1, source_target_pairs={{0,8},{4,12},{8,0},{12,4},{1,9},{5,13},{9,1},{13,5},{2,10},{6,14},... | collective-permute-start | bytes 786440 | tf_op jit(solution)/shard_map/ppermute | solution.py:447
  101.5 5.9 %collective-permute-start.33 = (bf16[128,2048]{1,0:T(8,128)(2,1)S(1)}, bf16[128,2048]{1,0:T(8,128)(2,1)S(1)}, u32[]{:S(2)}, u32[]{:S(2)}) collective-permute-start(bf16[128,2048]{1,0:T(8,128)(2,1)S(1)} %get-tuple-element.87), channel_id=1, source_target_pairs={{0,4},{4,0},{8,12},{12,8},{1,5},{5,1},{9,13},{13,9},{2,6},{6,2},{1... | collective-permute-start | bytes 1572872 | tf_op jit(solution)/shard_map/ppermute | solution.py:447
  101.6 15.4 %collective-permute-start.39 = (bf16[64,2048]{1,0:T(8,128)(2,1)S(1)}, bf16[64,2048]{1,0:T(8,128)(2,1)S(1)}, u32[]{:S(2)}, u32[]{:S(2)}) collective-permute-start(bf16[64,2048]{1,0:T(8,128)(2,1)S(1)} %add_convert_fusion.1), channel_id=1, source_target_pairs={{0,2},{1,3},{2,0},{3,1},{4,6},{5,7},{6,4},{7,5},{8,10},{9,11},{10,... | collective-permute-start | bytes 786440 | tf_op jit(solution)/shard_map/ppermute | solution.py:444
  106.4 12.9 %collective-permute-start.37 = (bf16[64,2048]{1,0:T(8,128)(2,1)S(1)}, bf16[64,2048]{1,0:T(8,128)(2,1)S(1)}, u32[]{:S(2)}, u32[]{:S(2)}) collective-permute-start(bf16[64,2048]{1,0:T(8,128)(2,1)S(1)} %add_convert_fusion.3), channel_id=1, source_target_pairs={{0,1},{1,0},{2,3},{3,2},{4,5},{5,4},{6,7},{7,6},{8,9},{9,8},{10,11... | collective-permute-start | bytes 786440 | tf_op jit(solution)/shard_map/ppermute | solution.py:444
  107.5 11.8 %collective-permute-start.35 = (bf16[64,2048]{1,0:T(8,128)(2,1)S(1)}, bf16[64,2048]{1,0:T(8,128)(2,1)S(1)}, u32[]{:S(2)}, u32[]{:S(2)}) collective-permute-start(bf16[64,2048]{1,0:T(8,128)(2,1)S(1)} %add_convert_fusion.5), channel_id=1, source_target_pairs={{0,8},{4,12},{8,0},{12,4},{1,9},{5,13},{9,1},{13,5},{2,10},{6,14},... | collective-permute-start | bytes 786440 | tf_op jit(solution)/shard_map/ppermute | solution.py:447
  (3 other events, 7.1 us)

commit v2 on v1

--- a/solution.py
+++ b/solution.py
@@ -602,7 +602,7 @@
         jax.ShapeDtypeStruct((size, near_width), jnp.bfloat16) for size in (far_rows, 2 * far_rows)
     ]
     first_come = [*near_crossed[0], near_planes[far_plane], *near_crossed[far_plane]]
-    first_come.append(near_planes[final])
+    first_come += [near_planes[final], gate_weight, up_weight, down_weight]
     far_halves = pl.pallas_call(
         partial(far_sum_kernel, local_length, len(first_come)),
         in_specs=[pl.BlockSpec(memory_space=pl.ANY)] * len(first_come)
@@ -619,7 +619,7 @@
     width = residual.shape[2]
     gain = norm_gain.reshape(1, width)
 
-    def normed_rows(parts, second, *hidden_shape):
+    def normed_rows(parts, second, cost, *hidden_shape):
         rows = chips * local_length
         firsts = (local_length, far_rows) if second else (0, 0)
         return pl.pallas_call(
@@ -631,7 +631,7 @@
                 *hidden_shape,
             ],
             compiler_params=pltpu.CompilerParams(vmem_limit_bytes=SMALL_VMEM),
-            cost_estimate=NOTHING,
+            cost_estimate=cost,
         )(at, gain, *parts)
 
     keep, send, slots, leaving, passed = {}, {}, {}, {}, {}
@@ -649,7 +649,7 @@
         parts = [near_planes[k], far_planes[k]]
         for pair in zip(near_crossed[k], late):
             parts += pair
-        normed, *own = normed_rows(parts, k == last, *([] if k else [hidden_shape]))
+        normed, *own = normed_rows(parts, k == last, LONG if k == final else NOTHING, *([] if k else [hidden_shape]))
         hidden.extend(own)
         return [normed, over_seq(normed, 1)]
 
@@ -670,7 +670,7 @@
         passed[k] = [over_seq(part, j) for part, j in zip(leaving[k], across_steps)]
         slots[k] += passed[k]
 
-    ready = {far_plane: prepared(far_plane, far_planes[final], *far_crossed[final])}
+    ready = {far_plane: prepared(far_plane, far_planes[final])}
     ready[final] = prepared(final)
     keep[far_plane], send[far_plane] = expert(ready[far_plane], ready[final][0])
     ready |= {k: prepared(k, keep[far_plane]) for k in (last, 0)}

time: 120 us -> 120 us (level)
  no operation moved by 1% of the time
where the time goes in v2:
time: 120 us
  waiting for transfers between devices  56.9 us (47%)
  starting transfers between devices  33.2 us (28%)
  Pallas kernels  26.5 us (22%)
  other arithmetic  1.81 us (2%)
    ppermute x17, waiting for transfers between devices, over_role(): return lax.ppermute(array, 'role', [(i, i ^ k) for i in range(role_count)])  40.7 us
    ppermute x17, starting transfers between devices, over_role(): return lax.ppermute(array, 'role', [(i, i ^ k) for i in range(role_count)])  18.1 us
    ppermute x23, waiting for transfers between devices, over_seq(): return lax.ppermute(array, 'seq', [(i, i ^ j) for i in range(seq_count)])  16.2 us
    ppermute x23, starting transfers between devices, over_seq(): return lax.ppermute(array, 'seq', [(i, i ^ j) for i in range(seq_count)])  15.1 us
    pallas_call x4, Pallas kernels, run_expert(): pl.pallas_call(partial(expert_kernel, len(tokens)), in_specs=[pl.BlockSpe...  13 us
    pallas_call x2, Pallas kernels, gathered_shards(): pl.pallas_call(partial(attend_kernel, seq_count, role_count, slots, parts...  5.77 us
    pallas_call x2, Pallas kernels, gathered_shards(): pl.pallas_call(partial(project_kernel, slots, parts), in_specs=in_vmem(1)...  4.02 us
    pallas_call x4, Pallas kernels, normed_rows(): pl.pallas_call(partial(norm_kernel, chips, *firsts), in_specs=[pl.BlockSp...  3.26 us
  transfers between devices with their start and end apart: 40, of which 23 were waited for; matrix products, arithmetic and copies ran while one was open for 2% of the time, Pallas kernels for 19%

profile of v2, /device:TPU:0, one launch (start us, length us, event | category | flops | bytes accessed | tf_op | source)
XLA Modules:
  0.0 119.8 jit_solution(9075093310234268867)
XLA Ops:
  0.5 0.8 constant_dynamic-slice_fusion
  1.3 3.7 %collective-permute-start.3 = (bf16[4,16,256]{2,1,0:T(8,128)(2,1)S(1)}, bf16[4,16,256]{2,1,0:T(8,128)(2,1)S(1)}, u32[]{:S(2)}, u32[]{:S(2)}) collective-permute-start(bf16[4,16,256]{2,1,0:T(8,128)(2,1)S(1)} %pad_maximum_fusion.3), channel_id=1, source_target_pairs={{0,2},{1,3},{2,0},{3,1},{4,6},{5,7},{6,4},{7,5},{8,10},{9,11},{10,... | collective-permute-start | bytes 98312 | tf_op jit(solution)/shard_map/ppermute | solution.py:444
  5.0 1.3 %collective-permute-start.4 = (bf16[4,16,256]{2,1,0:T(8,128)(2,1)S(1)}, bf16[4,16,256]{2,1,0:T(8,128)(2,1)S(1)}, u32[]{:S(2)}, u32[]{:S(2)}) collective-permute-start(bf16[4,16,256]{2,1,0:T(8,128)(2,1)S(1)} %pad_maximum_fusion.4), channel_id=1, source_target_pairs={{0,3},{1,2},{2,1},{3,0},{4,7},{5,6},{6,5},{7,4},{8,11},{9,10},{10,... | collective-permute-start | bytes 98312 | tf_op jit(solution)/shard_map/ppermute | solution.py:444
  7.0 3.7 %collective-permute-done.4.refs_3_ = bf16[4,16,256]{2,1,0:T(8,128)(2,1)S(1)} collective-permute-done((bf16[4,16,256]{2,1,0:T(8,128)(2,1)S(1)}, bf16[4,16,256]{2,1,0:T(8,128)(2,1)S(1)}, u32[]{:S(2)}, u32[]{:S(2)}) %collective-permute-start.4) | collective-permute-done | bytes 32800 | tf_op jit(solution)/shard_map/ppermute | solution.py:444
  10.8 1.6 %collective-permute-start.5 = (bf16[4,64,256]{2,1,0:T(8,128)(2,1)S(1)}, bf16[4,64,256]{2,1,0:T(8,128)(2,1)S(1)}, u32[]{:S(2)}, u32[]{:S(2)}) collective-permute-start(bf16[4,64,256]{2,1,0:T(8,128)(2,1)S(1)} %shard_map.109.refs_2_), channel_id=1, source_target_pairs={{0,8},{4,12},{8,0},{12,4},{1,9},{5,13},{9,1},{13,5},{2,10},{6,14},... | collective-permute-start | bytes 393224 | tf_op jit(solution)/shard_map/ppermute | solution.py:447
  12.5 1.3 %collective-permute-start = (f32[64,16]{1,0:T(8,128)S(1)}, f32[64,16]{1,0:T(8,128)S(1)}, u32[]{:S(2)}, u32[]{:S(2)}) collective-permute-start(f32[64,16]{1,0:T(8,128)S(1)} %copy.15.route_ref), channel_id=1, source_target_pairs={{0,2},{1,3},{2,0},{3,1},{4,6},{5,7},{6,4},{7,5},{8,10},{9,11},{10,... | collective-permute-start | bytes 12296 | tf_op jit(solution)/shard_map/ppermute | solution.py:444
  13.7 2.1 %collective-permute-done.5.refs_4_ = bf16[4,64,256]{2,1,0:T(8,128)(2,1)S(1)} collective-permute-done((bf16[4,64,256]{2,1,0:T(8,128)(2,1)S(1)}, bf16[4,64,256]{2,1,0:T(8,128)(2,1)S(1)}, u32[]{:S(2)}, u32[]{:S(2)}) %collective-permute-start.5) | collective-permute-done | bytes 131104 | tf_op jit(solution)/shard_map/ppermute | solution.py:447
  16.0 1.2 %collective-permute-done.6.refs_0_ = bf16[4,64,256]{2,1,0:T(8,128)(2,1)S(1)} collective-permute-done((bf16[4,64,256]{2,1,0:T(8,128)(2,1)S(1)}, bf16[4,64,256]{2,1,0:T(8,128)(2,1)S(1)}, u32[]{:S(2)}, u32[]{:S(2)}) %collective-permute-start.6) | collective-permute-done | bytes 131104 | tf_op jit(solution)/shard_map/ppermute | solution.py:447
  17.2 2.9 %shard_map.111 = (bf16[128,1024]{1,0:T(8,128)(2,1)S(1)}, bf16[128,1024]{1,0:T(8,128)(2,1)S(1)}) custom-call(s32[3]{0:T(128)S(1)} %pad_add_fusion.at_ref, bf16[4,64,256]{2,1,0:T(8,128)(2,1)S(1)} %collective-permute-done.6.refs_0_, bf16[4,64,1024]{2,1,0:T(8,128)(2,1)} %refs_1_.3, bf16[4,64,256]{2,1,0:T(8,128)(2,1)} %copy-done.4, ...), custom_call_target="tpu_custom_call" | custom-call | flops 2000000000 | bytes 4194304 | tf_op jit(solution)/shard_map/pallas_call | solution.py:498
  20.2 1.6 %collective-permute-start.15 = (bf16[128,1024]{1,0:T(8,128)(2,1)S(1)}, bf16[128,1024]{1,0:T(8,128)(2,1)S(1)}, u32[]{:S(2)}, u32[]{:S(2)}) collective-permute-start(bf16[128,1024]{1,0:T(8,128)(2,1)S(1)} %get-tuple-element.57), channel_id=1, source_target_pairs={{0,8},{4,12},{8,0},{12,4},{1,9},{5,13},{9,1},{13,5},{2,10},{6,14},... | collective-permute-start | bytes 786440 | tf_op jit(solution)/shard_map/ppermute | solution.py:447
  21.8 2.9 %shard_map.110 = (bf16[128,1024]{1,0:T(8,128)(2,1)S(1)}, bf16[128,1024]{1,0:T(8,128)(2,1)S(1)}) custom-call(s32[3]{0:T(128)S(1)} %pad_add_fusion.at_ref, bf16[4,64,256]{2,1,0:T(8,128)(2,1)S(1)} %collective-permute-done.6.refs_0_, bf16[4,64,1024]{2,1,0:T(8,128)(2,1)} %refs_1_.3, bf16[4,64,256]{2,1,0:T(8,128)(2,1)} %copy-done.4, ...), custom_call_target="tpu_custom_call" | custom-call | flops 2000000000 | bytes 4194304 | tf_op jit(solution)/shard_map/pallas_call | solution.py:498
  25.3 1.5 %collective-permute-start.17 = (bf16[64,1024]{1,0:T(8,128)(2,1)S(1)}, bf16[64,1024]{1,0:T(8,128)(2,1)S(1)}, u32[]{:S(2)}, u32[]{:S(2)}) collective-permute-start(bf16[64,1024]{1,0:T(8,128)(2,1)S(1)} %pad_maximum_fusion), channel_id=1, source_target_pairs={{0,8},{4,12},{8,0},{12,4},{1,9},{5,13},{9,1},{13,5},{2,10},{6,14},... | collective-permute-start | bytes 393224 | tf_op jit(solution)/shard_map/ppermute | solution.py:447
  26.8 1.8 %collective-permute-done.8 = bf16[128,1024]{1,0:T(8,128)(2,1)S(1)} collective-permute-done((bf16[128,1024]{1,0:T(8,128)(2,1)S(1)}, bf16[128,1024]{1,0:T(8,128)(2,1)S(1)}, u32[]{:S(2)}, u32[]{:S(2)}) %collective-permute-start.8) | collective-permute-done | bytes 262176 | tf_op jit(solution)/shard_map/ppermute | solution.py:444
  28.6 1.5 %collective-permute-start.9 = (bf16[128,1024]{1,0:T(8,128)(2,1)S(1)}, bf16[128,1024]{1,0:T(8,128)(2,1)S(1)}, u32[]{:S(2)}, u32[]{:S(2)}) collective-permute-start(bf16[128,1024]{1,0:T(8,128)(2,1)S(1)} %add_convert_fusion.9.sent), channel_id=1, source_target_pairs={{0,2},{1,3},{2,0},{3,1},{4,6},{5,7},{6,4},{7,5},{8,10},{9,11},{10,... | collective-permute-start | bytes 786440 | tf_op jit(solution)/shard_map/ppermute | solution.py:444
  30.1 2.0 %shard_map.114 = bf16[128,1024]{1,0:T(8,128)(2,1)S(1)} custom-call(bf16[128,1024]{1,0:T(8,128)(2,1)S(1)} %collective-permute-done.15.attended_ref, f32[64,16]{1,0:T(8,128)S(1)} %collective-permute-done.other_route_ref.order_ref, bf16[1024,512]{1,0:T(8,128)(2,1)} %refs_0_.3, bf16[1024,512]{1,0:T(8,128)(2,1)} %copy-done.8), custom_call_target="tpu_custom_call" | custom-call | flops 2000000000 | bytes 4194304 | tf_op jit(solution)/shard_map/pallas_call | solution.py:587
  32.2 1.4 %collective-permute-start.16 = (bf16[128,1024]{1,0:T(8,128)(2,1)S(1)}, bf16[128,1024]{1,0:T(8,128)(2,1)S(1)}, u32[]{:S(2)}, u32[]{:S(2)}) collective-permute-start(bf16[128,1024]{1,0:T(8,128)(2,1)S(1)} %shard_map.114), channel_id=1, source_target_pairs={{0,1},{1,0},{2,3},{3,2},{4,5},{5,4},{6,7},{7,6},{8,9},{9,8},{10,11... | collective-permute-start | bytes 786440 | tf_op jit(solution)/shard_map/ppermute | solution.py:444
  33.6 1.5 %collective-permute-done.14.attended_ref = bf16[128,1024]{1,0:T(8,128)(2,1)S(1)} collective-permute-done((bf16[128,1024]{1,0:T(8,128)(2,1)S(1)}, bf16[128,1024]{1,0:T(8,128)(2,1)S(1)}, u32[]{:S(2)}, u32[]{:S(2)}) %collective-permute-start.14) | collective-permute-done | bytes 262176 | tf_op jit(solution)/shard_map/ppermute | solution.py:447
  35.1 2.0 %shard_map.113 = bf16[128,1024]{1,0:T(8,128)(2,1)S(1)} custom-call(bf16[128,1024]{1,0:T(8,128)(2,1)S(1)} %collective-permute-done.14.attended_ref, f32[64,16]{1,0:T(8,128)S(1)} %collective-permute-done.other_route_ref.order_ref, bf16[1024,512]{1,0:T(8,128)(2,1)} %refs_0_.3, bf16[1024,512]{1,0:T(8,128)(2,1)} %copy-done.8), custom_call_target="tpu_custom_call" | custom-call | flops 2000000000 | bytes 4194304 | tf_op jit(solution)/shard_map/pallas_call | solution.py:587
  37.1 5.8 %collective-permute-done.9.came_ref = bf16[128,1024]{1,0:T(8,128)(2,1)S(1)} collective-permute-done((bf16[128,1024]{1,0:T(8,128)(2,1)S(1)}, bf16[128,1024]{1,0:T(8,128)(2,1)S(1)}, u32[]{:S(2)}, u32[]{:S(2)}) %collective-permute-start.9) | collective-permute-done | bytes 262176 | tf_op jit(solution)/shard_map/ppermute | solution.py:444
  43.4 1.5 %collective-permute-start.10 = (bf16[128,1152]{1,0:T(8,128)(2,1)S(1)}, bf16[128,1152]{1,0:T(8,128)(2,1)S(1)}, u32[]{:S(2)}, u32[]{:S(2)}) collective-permute-start(bf16[128,1152]{1,0:T(8,128)(2,1)S(1)} %get-tuple-element.53), channel_id=1, source_target_pairs={{0,8},{4,12},{8,0},{12,4},{1,9},{5,13},{9,1},{13,5},{2,10},{6,14},... | collective-permute-start | bytes 884744 | tf_op jit(solution)/shard_map/ppermute | solution.py:447
  45.1 2.5 %collective-permute-start.18 = (bf16[128,1024]{1,0:T(8,128)(2,1)S(1)}, bf16[128,1024]{1,0:T(8,128)(2,1)S(1)}, u32[]{:S(2)}, u32[]{:S(2)}) collective-permute-start(bf16[128,1024]{1,0:T(8,128)(2,1)S(1)} %add_convert_fusion.8.refs_8_), channel_id=1, source_target_pairs={{0,2},{1,3},{2,0},{3,1},{4,6},{5,7},{6,4},{7,5},{8,10},{9,11},{10,... | collective-permute-start | bytes 786440 | tf_op jit(solution)/shard_map/ppermute | solution.py:444
  47.7 3.2 %collective-permute-done.11.refs_1_.refs_0_ = bf16[64,1152]{1,0:T(8,128)(2,1)S(1)} collective-permute-done((bf16[64,1152]{1,0:T(8,128)(2,1)S(1)}, bf16[64,1152]{1,0:T(8,128)(2,1)S(1)}, u32[]{:S(2)}, u32[]{:S(2)}) %collective-permute-start.11) | collective-permute-done | bytes 147488 | tf_op jit(solution)/shard_map/ppermute | solution.py:444
  50.9 1.4 %collective-permute-done.10.refs_0_.refs_2_ = bf16[128,1152]{1,0:T(8,128)(2,1)S(1)} collective-permute-done((bf16[128,1152]{1,0:T(8,128)(2,1)S(1)}, bf16[128,1152]{1,0:T(8,128)(2,1)S(1)}, u32[]{:S(2)}, u32[]{:S(2)}) %collective-permute-start.10) | collective-permute-done | bytes 294944 | tf_op jit(solution)/shard_map/ppermute | solution.py:447
  52.3 1.5 %collective-permute-start.12 = (bf16[64,1152]{1,0:T(8,128)(2,1)S(1)}, bf16[64,1152]{1,0:T(8,128)(2,1)S(1)}, u32[]{:S(2)}, u32[]{:S(2)}) collective-permute-start(bf16[64,1152]{1,0:T(8,128)(2,1)S(1)} %collective-permute-done.11.refs_1_.refs_0_), channel_id=1, source_target_pairs={{0,8},{4,12},{8,0},{12,4},{1,9},{5,13},{9,1},{13,5},{2,10},{6,14},... | collective-permute-start | bytes 442376 | tf_op jit(solution)/shard_map/ppermute | solution.py:447
  53.8 1.7 %collective-permute-start.20 = (bf16[64,1152]{1,0:T(8,128)(2,1)S(1)}, bf16[64,1152]{1,0:T(8,128)(2,1)S(1)}, u32[]{:S(2)}, u32[]{:S(2)}) collective-permute-start(bf16[64,1152]{1,0:T(8,128)(2,1)S(1)} %slice.72), channel_id=1, source_target_pairs={{0,1},{1,0},{2,3},{3,2},{4,5},{5,4},{6,7},{7,6},{8,9},{9,8},{10,11... | collective-permute-start | bytes 442376 | tf_op jit(solution)/shard_map/ppermute | solution.py:444
  55.5 1.7 %collective-permute-done.13.refs_3_.refs_0_ = bf16[64,1152]{1,0:T(8,128)(2,1)S(1)} collective-permute-done((bf16[64,1152]{1,0:T(8,128)(2,1)S(1)}, bf16[64,1152]{1,0:T(8,128)(2,1)S(1)}, u32[]{:S(2)}, u32[]{:S(2)}) %collective-permute-start.13) | collective-permute-done | bytes 147488 | tf_op jit(solution)/shard_map/ppermute | solution.py:444
  57.2 2.4 %collective-permute-done.18.refs_7_ = bf16[128,1024]{1,0:T(8,128)(2,1)S(1)} collective-permute-done((bf16[128,1024]{1,0:T(8,128)(2,1)S(1)}, bf16[128,1024]{1,0:T(8,128)(2,1)S(1)}, u32[]{:S(2)}, u32[]{:S(2)}) %collective-permute-start.18) | collective-permute-done | bytes 262176 | tf_op jit(solution)/shard_map/ppermute | solution.py:444
  60.3 1.7 %collective-permute-done.20.refs_2_ = bf16[64,1152]{1,0:T(8,128)(2,1)S(1)} collective-permute-done((bf16[64,1152]{1,0:T(8,128)(2,1)S(1)}, bf16[64,1152]{1,0:T(8,128)(2,1)S(1)}, u32[]{:S(2)}, u32[]{:S(2)}) %collective-permute-start.20) | collective-permute-done | bytes 147488 | tf_op jit(solution)/shard_map/ppermute | solution.py:444
  62.0 5.0 %collective-permute-done.21.refs_1_ = bf16[64,1024]{1,0:T(8,128)(2,1)S(1)} collective-permute-done((bf16[64,1024]{1,0:T(8,128)(2,1)S(1)}, bf16[64,1024]{1,0:T(8,128)(2,1)S(1)}, u32[]{:S(2)}, u32[]{:S(2)}) %collective-permute-start.21) | collective-permute-done | bytes 131104 | tf_op jit(solution)/shard_map/ppermute | solution.py:444
  67.8 1.8 %collective-permute-start.25 = (bf16[64,1024]{1,0:T(8,128)(2,1)S(1)}, bf16[64,1024]{1,0:T(8,128)(2,1)S(1)}, u32[]{:S(2)}, u32[]{:S(2)}) collective-permute-start(bf16[64,1024]{1,0:T(8,128)(2,1)S(1)} %slice.73), channel_id=1, source_target_pairs={{0,1},{1,0},{2,3},{3,2},{4,5},{5,4},{6,7},{7,6},{8,9},{9,8},{10,11... | collective-permute-start | bytes 393224 | tf_op jit(solution)/shard_map/ppermute | solution.py:444
  69.6 2.6 %collective-permute-done.23.refs_1_ = bf16[64,1024]{1,0:T(8,128)(2,1)S(1)} collective-permute-done((bf16[64,1024]{1,0:T(8,128)(2,1)S(1)}, bf16[64,1024]{1,0:T(8,128)(2,1)S(1)}, u32[]{:S(2)}, u32[]{:S(2)}) %collective-permute-start.23) | collective-permute-done | bytes 131104 | tf_op jit(solution)/shard_map/ppermute | solution.py:444
  72.2 0.8 shard_map.116.refs_0_
  73.6 0.8 shard_map.117.refs_0_
  75.0 3.2 %shard_map.118 = (bf16[128,2048]{1,0:T(8,128)(2,1)S(1)}, bf16[128,2048]{1,0:T(8,128)(2,1)S(1)}) custom-call(s32[3]{0:T(128)S(1)} %pad_add_fusion.at_ref, bf16[128,2176]{1,0:T(8,128)(2,1)S(1)} %shard_map.116.refs_0_, bf16[128,2176]{1,0:T(8,128)(2,1)S(1)} %collective-permute-done.24.refs_1_, bf16[1,2048,768]{2,1,0:T(8,128)(2,1)S(1)} %copy-done, ...), custom_call_target="tpu_custom_call" | custom-call | flops 1 | bytes 1 | tf_op jit(solution)/shard_map/pallas_call | solution.py:398
  78.8 0.8 shard_map.120.refs_0_
  79.8 0.8 shard_map.119
  81.8 3.2 %shard_map.121 = (bf16[128,2048]{1,0:T(8,128)(2,1)S(1)}, bf16[128,2048]{1,0:T(8,128)(2,1)S(1)}) custom-call(s32[3]{0:T(128)S(1)} %pad_add_fusion.at_ref, bf16[128,2176]{1,0:T(8,128)(2,1)S(1)} %shard_map.120.refs_0_, bf16[128,2176]{1,0:T(8,128)(2,1)S(1)} %collective-permute-done.28.refs_1_, bf16[1,2048,768]{2,1,0:T(8,128)(2,1)S(1)} %copy-done, ...), custom_call_target="tpu_custom_call" | custom-call | flops 1 | bytes 1 | tf_op jit(solution)/shard_map/pallas_call | solution.py:398
  85.6 3.4 %shard_map.122 = (bf16[128,2048]{1,0:T(8,128)(2,1)S(1)}, bf16[128,2048]{1,0:T(8,128)(2,1)S(1)}) custom-call(s32[3]{0:T(128)S(1)} %pad_add_fusion.at_ref, bf16[128,2176]{1,0:T(8,128)(2,1)S(1)} %shard_map.117.refs_0_, bf16[128,2176]{1,0:T(8,128)(2,1)S(1)} %collective-permute-done.27.refs_1_, bf16[1,2048,768]{2,1,0:T(8,128)(2,1)S(1)} %copy-done, ...), custom_call_target="tpu_custom_call" | custom-call | flops 1 | bytes 1 | tf_op jit(solution)/shard_map/pallas_call | solution.py:398
  89.5 1.8 %collective-permute-start.38 = (bf16[64,2048]{1,0:T(8,128)(2,1)S(1)}, bf16[64,2048]{1,0:T(8,128)(2,1)S(1)}, u32[]{:S(2)}, u32[]{:S(2)}) collective-permute-start(bf16[64,2048]{1,0:T(8,128)(2,1)S(1)} %add_convert_fusion.2), channel_id=1, source_target_pairs={{0,1},{1,0},{2,3},{3,2},{4,5},{5,4},{6,7},{7,6},{8,9},{9,8},{10,11... | collective-permute-start | bytes 786440 | tf_op jit(solution)/shard_map/ppermute | solution.py:444
  91.4 0.9 collective-permute-start.32
  92.3 3.2 %shard_map.123 = (bf16[128,2048]{1,0:T(8,128)(2,1)S(1)}, bf16[128,2048]{1,0:T(8,128)(2,1)S(1)}) custom-call(s32[3]{0:T(128)S(1)} %pad_add_fusion.at_ref, bf16[128,2176]{1,0:T(8,128)(2,1)S(1)} %get-tuple-element.83.refs_0_, bf16[128,2176]{1,0:T(8,128)(2,1)S(1)} %collective-permute-done.26.refs_1_, bf16[1,2048,768]{2,1,0:T(8,128)(2,1)S(1)} %copy-done, ...), custom_call_target="tpu_custom_call" | custom-call | flops 1 | bytes 1 | tf_op jit(solution)/shard_map/pallas_call | solution.py:398
  95.6 1.3 %collective-permute-start.36 = (bf16[64,2048]{1,0:T(8,128)(2,1)S(1)}, bf16[64,2048]{1,0:T(8,128)(2,1)S(1)}, u32[]{:S(2)}, u32[]{:S(2)}) collective-permute-start(bf16[64,2048]{1,0:T(8,128)(2,1)S(1)} %add_convert_fusion.4), channel_id=1, source_target_pairs={{0,8},{4,12},{8,0},{12,4},{1,9},{5,13},{9,1},{13,5},{2,10},{6,14},... | collective-permute-start | bytes 786440 | tf_op jit(solution)/shard_map/ppermute | solution.py:447
  96.9 3.8 %collective-permute-done.32 = bf16[64,2048]{1,0:T(8,128)(2,1)S(1)} collective-permute-done((bf16[64,2048]{1,0:T(8,128)(2,1)S(1)}, bf16[64,2048]{1,0:T(8,128)(2,1)S(1)}, u32[]{:S(2)}, u32[]{:S(2)}) %collective-permute-start.32) | collective-permute-done | bytes 262176 | tf_op jit(solution)/shard_map/ppermute | solution.py:447
  100.8 4.7 %collective-permute-done.36 = bf16[64,2048]{1,0:T(8,128)(2,1)S(1)} collective-permute-done((bf16[64,2048]{1,0:T(8,128)(2,1)S(1)}, bf16[64,2048]{1,0:T(8,128)(2,1)S(1)}, u32[]{:S(2)}, u32[]{:S(2)}) %collective-permute-start.36) | collective-permute-done | bytes 262176 | tf_op jit(solution)/shard_map/ppermute | solution.py:447
  106.1 0.8 collective-permute-start.35
  106.9 9.0 %collective-permute-done.39 = bf16[64,2048]{1,0:T(8,128)(2,1)S(1)} collective-permute-done((bf16[64,2048]{1,0:T(8,128)(2,1)S(1)}, bf16[64,2048]{1,0:T(8,128)(2,1)S(1)}, u32[]{:S(2)}, u32[]{:S(2)}) %collective-permute-start.39) | collective-permute-done | bytes 262176 | tf_op jit(solution)/shard_map/ppermute | solution.py:444
  115.9 3.0 %collective-permute-done.37 = bf16[64,2048]{1,0:T(8,128)(2,1)S(1)} collective-permute-done((bf16[64,2048]{1,0:T(8,128)(2,1)S(1)}, bf16[64,2048]{1,0:T(8,128)(2,1)S(1)}, u32[]{:S(2)}, u32[]{:S(2)}) %collective-permute-start.37) | collective-permute-done | bytes 262176 | tf_op jit(solution)/shard_map/ppermute | solution.py:444
  118.8 0.9 fusion.2
  (92 shorter events, 9.5 us)
Async XLA Ops:
  0.0 6.3 %collective-permute-start.1 = (bf16[1024,512]{1,0:T(8,128)(2,1)}, bf16[1024,512]{1,0:T(8,128)(2,1)S(1)}, u32[]{:S(2)}, u32[]{:S(2)}) collective-permute-start(bf16[1024,512]{1,0:T(8,128)(2,1)} %refs_0_.3), channel_id=1, source_target_pairs={{0,4},{4,0},{8,12},{12,8},{1,5},{5,1},{9,13},{13,9},{2,6},{6,2},{1... | collective-permute-start | bytes 3145736 | tf_op jit(solution)/shard_map/ppermute | solution.py:447
  1.3 5.7 %collective-permute-start.3 = (bf16[4,16,256]{2,1,0:T(8,128)(2,1)S(1)}, bf16[4,16,256]{2,1,0:T(8,128)(2,1)S(1)}, u32[]{:S(2)}, u32[]{:S(2)}) collective-permute-start(bf16[4,16,256]{2,1,0:T(8,128)(2,1)S(1)} %pad_maximum_fusion.3), channel_id=1, source_target_pairs={{0,2},{1,3},{2,0},{3,1},{4,6},{5,7},{6,4},{7,5},{8,10},{9,11},{10,... | collective-permute-start | bytes 98312 | tf_op jit(solution)/shard_map/ppermute | solution.py:444
  5.0 5.8 %collective-permute-start.4 = (bf16[4,16,256]{2,1,0:T(8,128)(2,1)S(1)}, bf16[4,16,256]{2,1,0:T(8,128)(2,1)S(1)}, u32[]{:S(2)}, u32[]{:S(2)}) collective-permute-start(bf16[4,16,256]{2,1,0:T(8,128)(2,1)S(1)} %pad_maximum_fusion.4), channel_id=1, source_target_pairs={{0,3},{1,2},{2,1},{3,0},{4,7},{5,6},{6,5},{7,4},{8,11},{9,10},{10,... | collective-permute-start | bytes 98312 | tf_op jit(solution)/shard_map/ppermute | solution.py:444
  6.3 4.4 %collective-permute-start.2 = (bf16[4,16,256]{2,1,0:T(8,128)(2,1)S(1)}, bf16[4,16,256]{2,1,0:T(8,128)(2,1)S(1)}, u32[]{:S(2)}, u32[]{:S(2)}) collective-permute-start(bf16[4,16,256]{2,1,0:T(8,128)(2,1)S(1)} %pad_maximum_fusion.2), channel_id=1, source_target_pairs={{0,1},{1,0},{2,3},{3,2},{4,5},{5,4},{6,7},{7,6},{8,9},{9,8},{10,11... | collective-permute-start | bytes 98312 | tf_op jit(solution)/shard_map/ppermute | solution.py:444
  6.7 5.7 %copy-start.6 = (s32[1,64,8]{1,2,0:T(8,128)S(1)}, s32[1,64,8]{1,2,0:T(8,128)}, u32[]{:S(2)}) copy-start(s32[1,64,8]{1,2,0:T(8,128)} %param.17) | copy-start | bytes 6148
  6.7 5.7 %copy-start.7 = (f32[1,64,8]{1,2,0:T(8,128)S(1)}, f32[1,64,8]{1,2,0:T(8,128)}, u32[]{:S(2)}) copy-start(f32[1,64,8]{1,2,0:T(8,128)} %param.18) | copy-start | bytes 6148
  6.7 9.3 %copy-start.5 = (bf16[1,64,2048]{2,1,0:T(8,128)(2,1)S(1)}, bf16[1,64,2048]{2,1,0:T(8,128)(2,1)}, u32[]{:S(2)}) copy-start(bf16[1,64,2048]{2,1,0:T(8,128)(2,1)} %param.15) | copy-start | bytes 786436
  10.8 6.4 %copy-start.4 = (bf16[4,64,256]{2,1,0:T(8,128)(2,1)}, bf16[4,64,256]{2,1,0:T(8,128)(2,1)S(1)}, u32[]{:S(2)}) copy-start(bf16[4,64,256]{2,1,0:T(8,128)(2,1)S(1)} %shard_map.109.refs_2_) | copy-start | bytes 393220
  10.8 5.0 %collective-permute-start.5 = (bf16[4,64,256]{2,1,0:T(8,128)(2,1)S(1)}, bf16[4,64,256]{2,1,0:T(8,128)(2,1)S(1)}, u32[]{:S(2)}, u32[]{:S(2)}) collective-permute-start(bf16[4,64,256]{2,1,0:T(8,128)(2,1)S(1)} %shard_map.109.refs_2_), channel_id=1, source_target_pairs={{0,8},{4,12},{8,0},{12,4},{1,9},{5,13},{9,1},{13,5},{2,10},{6,14},... | collective-permute-start | bytes 393224 | tf_op jit(solution)/shard_map/ppermute | solution.py:447
  12.5 17.7 %collective-permute-start = (f32[64,16]{1,0:T(8,128)S(1)}, f32[64,16]{1,0:T(8,128)S(1)}, u32[]{:S(2)}, u32[]{:S(2)}) collective-permute-start(f32[64,16]{1,0:T(8,128)S(1)} %copy.15.route_ref), channel_id=1, source_target_pairs={{0,2},{1,3},{2,0},{3,1},{4,6},{5,7},{6,4},{7,5},{8,10},{9,11},{10,... | collective-permute-start | bytes 12296 | tf_op jit(solution)/shard_map/ppermute | solution.py:444
  13.7 2.2 %collective-permute-start.7 = (bf16[4,64,256]{2,1,0:T(8,128)(2,1)S(1)}, bf16[4,64,256]{2,1,0:T(8,128)(2,1)S(1)}, u32[]{:S(2)}, u32[]{:S(2)}) collective-permute-start(bf16[4,64,256]{2,1,0:T(8,128)(2,1)S(1)} %shard_map.109.refs_2_), channel_id=1, source_target_pairs={{0,4},{4,0},{8,12},{12,8},{1,5},{5,1},{9,13},{13,9},{2,6},{6,2},{1... | collective-permute-start | bytes 393224 | tf_op jit(solution)/shard_map/ppermute | solution.py:447
  15.9 1.3 %collective-permute-start.6 = (bf16[4,64,256]{2,1,0:T(8,128)(2,1)S(1)}, bf16[4,64,256]{2,1,0:T(8,128)(2,1)S(1)}, u32[]{:S(2)}, u32[]{:S(2)}) collective-permute-start(bf16[4,64,256]{2,1,0:T(8,128)(2,1)S(1)} %collective-permute-done.5.refs_4_), channel_id=1, source_target_pairs={{0,4},{4,0},{8,12},{12,8},{1,5},{5,1},{9,13},{13,9},{2,6},{6,2},{1... | collective-permute-start | bytes 393224 | tf_op jit(solution)/shard_map/ppermute | solution.py:447
  20.1 8.4 %collective-permute-start.8 = (bf16[128,1024]{1,0:T(8,128)(2,1)S(1)}, bf16[128,1024]{1,0:T(8,128)(2,1)S(1)}, u32[]{:S(2)}, u32[]{:S(2)}) collective-permute-start(bf16[128,1024]{1,0:T(8,128)(2,1)S(1)} %get-tuple-element.51), channel_id=1, source_target_pairs={{0,1},{1,0},{2,3},{3,2},{4,5},{5,4},{6,7},{7,6},{8,9},{9,8},{10,11... | collective-permute-start | bytes 786440 | tf_op jit(solution)/shard_map/ppermute | solution.py:444
  20.2 9.9 %collective-permute-start.15 = (bf16[128,1024]{1,0:T(8,128)(2,1)S(1)}, bf16[128,1024]{1,0:T(8,128)(2,1)S(1)}, u32[]{:S(2)}, u32[]{:S(2)}) collective-permute-start(bf16[128,1024]{1,0:T(8,128)(2,1)S(1)} %get-tuple-element.57), channel_id=1, source_target_pairs={{0,8},{4,12},{8,0},{12,4},{1,9},{5,13},{9,1},{13,5},{2,10},{6,14},... | collective-permute-start | bytes 786440 | tf_op jit(solution)/shard_map/ppermute | solution.py:447
  24.7 10.4 %collective-permute-start.14 = (bf16[128,1024]{1,0:T(8,128)(2,1)S(1)}, bf16[128,1024]{1,0:T(8,128)(2,1)S(1)}, u32[]{:S(2)}, u32[]{:S(2)}) collective-permute-start(bf16[128,1024]{1,0:T(8,128)(2,1)S(1)} %get-tuple-element.56), channel_id=1, source_target_pairs={{0,8},{4,12},{8,0},{12,4},{1,9},{5,13},{9,1},{13,5},{2,10},{6,14},... | collective-permute-start | bytes 786440 | tf_op jit(solution)/shard_map/ppermute | solution.py:447
  25.3 19.6 %collective-permute-start.17 = (bf16[64,1024]{1,0:T(8,128)(2,1)S(1)}, bf16[64,1024]{1,0:T(8,128)(2,1)S(1)}, u32[]{:S(2)}, u32[]{:S(2)}) collective-permute-start(bf16[64,1024]{1,0:T(8,128)(2,1)S(1)} %pad_maximum_fusion), channel_id=1, source_target_pairs={{0,8},{4,12},{8,0},{12,4},{1,9},{5,13},{9,1},{13,5},{2,10},{6,14},... | collective-permute-start | bytes 393224 | tf_op jit(solution)/shard_map/ppermute | solution.py:447
  28.6 14.2 %collective-permute-start.9 = (bf16[128,1024]{1,0:T(8,128)(2,1)S(1)}, bf16[128,1024]{1,0:T(8,128)(2,1)S(1)}, u32[]{:S(2)}, u32[]{:S(2)}) collective-permute-start(bf16[128,1024]{1,0:T(8,128)(2,1)S(1)} %add_convert_fusion.9.sent), channel_id=1, source_target_pairs={{0,2},{1,3},{2,0},{3,1},{4,6},{5,7},{6,4},{7,5},{8,10},{9,11},{10,... | collective-permute-start | bytes 786440 | tf_op jit(solution)/shard_map/ppermute | solution.py:444
  32.2 12.8 %collective-permute-start.16 = (bf16[128,1024]{1,0:T(8,128)(2,1)S(1)}, bf16[128,1024]{1,0:T(8,128)(2,1)S(1)}, u32[]{:S(2)}, u32[]{:S(2)}) collective-permute-start(bf16[128,1024]{1,0:T(8,128)(2,1)S(1)} %shard_map.114), channel_id=1, source_target_pairs={{0,1},{1,0},{2,3},{3,2},{4,5},{5,4},{6,7},{7,6},{8,9},{9,8},{10,11... | collective-permute-start | bytes 786440 | tf_op jit(solution)/shard_map/ppermute | solution.py:444
  42.9 16.8 %copy-start = (bf16[1,2048,768]{2,1,0:T(8,128)(2,1)S(1)}, bf16[1,2048,768]{2,1,0:T(8,128)(2,1)}, u32[]{:S(2)}) copy-start(bf16[1,2048,768]{2,1,0:T(8,128)(2,1)} %refs_2_.7) | copy-start | bytes 9437188
  42.9 16.8 %copy-start.1 = (bf16[1,2048,768]{2,1,0:T(8,128)(2,1)S(1)}, bf16[1,2048,768]{2,1,0:T(8,128)(2,1)}, u32[]{:S(2)}) copy-start(bf16[1,2048,768]{2,1,0:T(8,128)(2,1)} %refs_3_.7) | copy-start | bytes 9437188
  42.9 16.8 %copy-start.2 = (bf16[1,768,2048]{2,1,0:T(8,128)(2,1)S(1)}, bf16[1,768,2048]{2,1,0:T(8,128)(2,1)}, u32[]{:S(2)}) copy-start(bf16[1,768,2048]{2,1,0:T(8,128)(2,1)} %refs_4_.9) | copy-start | bytes 9437188
  43.3 7.6 %collective-permute-start.11 = (bf16[64,1152]{1,0:T(8,128)(2,1)S(1)}, bf16[64,1152]{1,0:T(8,128)(2,1)S(1)}, u32[]{:S(2)}, u32[]{:S(2)}) collective-permute-start(bf16[64,1152]{1,0:T(8,128)(2,1)S(1)} %get-tuple-element.54.refs_0_), channel_id=1, source_target_pairs={{0,1},{1,0},{2,3},{3,2},{4,5},{5,4},{6,7},{7,6},{8,9},{9,8},{10,11... | collective-permute-start | bytes 442376 | tf_op jit(solution)/shard_map/ppermute | solution.py:444
  43.4 8.9 %collective-permute-start.10 = (bf16[128,1152]{1,0:T(8,128)(2,1)S(1)}, bf16[128,1152]{1,0:T(8,128)(2,1)S(1)}, u32[]{:S(2)}, u32[]{:S(2)}) collective-permute-start(bf16[128,1152]{1,0:T(8,128)(2,1)S(1)} %get-tuple-element.53), channel_id=1, source_target_pairs={{0,8},{4,12},{8,0},{12,4},{1,9},{5,13},{9,1},{13,5},{2,10},{6,14},... | collective-permute-start | bytes 884744 | tf_op jit(solution)/shard_map/ppermute | solution.py:447
  45.1 14.6 %collective-permute-start.18 = (bf16[128,1024]{1,0:T(8,128)(2,1)S(1)}, bf16[128,1024]{1,0:T(8,128)(2,1)S(1)}, u32[]{:S(2)}, u32[]{:S(2)}) collective-permute-start(bf16[128,1024]{1,0:T(8,128)(2,1)S(1)} %add_convert_fusion.8.refs_8_), channel_id=1, source_target_pairs={{0,2},{1,3},{2,0},{3,1},{4,6},{5,7},{6,4},{7,5},{8,10},{9,11},{10,... | collective-permute-start | bytes 786440 | tf_op jit(solution)/shard_map/ppermute | solution.py:444
  47.6 9.6 %collective-permute-start.13 = (bf16[64,1152]{1,0:T(8,128)(2,1)S(1)}, bf16[64,1152]{1,0:T(8,128)(2,1)S(1)}, u32[]{:S(2)}, u32[]{:S(2)}) collective-permute-start(bf16[64,1152]{1,0:T(8,128)(2,1)S(1)} %get-tuple-element.52.refs_0_), channel_id=1, source_target_pairs={{0,1},{1,0},{2,3},{3,2},{4,5},{5,4},{6,7},{7,6},{8,9},{9,8},{10,11... | collective-permute-start | bytes 442376 | tf_op jit(solution)/shard_map/ppermute | solution.py:444
  52.3 7.3 %collective-permute-start.12 = (bf16[64,1152]{1,0:T(8,128)(2,1)S(1)}, bf16[64,1152]{1,0:T(8,128)(2,1)S(1)}, u32[]{:S(2)}, u32[]{:S(2)}) collective-permute-start(bf16[64,1152]{1,0:T(8,128)(2,1)S(1)} %collective-permute-done.11.refs_1_.refs_0_), channel_id=1, source_target_pairs={{0,8},{4,12},{8,0},{12,4},{1,9},{5,13},{9,1},{13,5},{2,10},{6,14},... | collective-permute-start | bytes 442376 | tf_op jit(solution)/shard_map/ppermute | solution.py:447
  53.8 18.4 %copy-start.3 = (f32[2048]{0:T(1024)S(1)}, f32[2048]{0:T(1024)}, u32[]{:S(2)}) copy-start(f32[2048]{0:T(1024)} %param.16) | copy-start | bytes 24580
  53.8 8.2 %collective-permute-start.20 = (bf16[64,1152]{1,0:T(8,128)(2,1)S(1)}, bf16[64,1152]{1,0:T(8,128)(2,1)S(1)}, u32[]{:S(2)}, u32[]{:S(2)}) collective-permute-start(bf16[64,1152]{1,0:T(8,128)(2,1)S(1)} %slice.72), channel_id=1, source_target_pairs={{0,1},{1,0},{2,3},{3,2},{4,5},{5,4},{6,7},{7,6},{8,9},{9,8},{10,11... | collective-permute-start | bytes 442376 | tf_op jit(solution)/shard_map/ppermute | solution.py:444
  59.7 7.3 %collective-permute-start.19 = (bf16[128,1024]{1,0:T(8,128)(2,1)S(1)}, bf16[128,1024]{1,0:T(8,128)(2,1)S(1)}, u32[]{:S(2)}, u32[]{:S(2)}) collective-permute-start(bf16[128,1024]{1,0:T(8,128)(2,1)S(1)} %get-tuple-element.61), channel_id=1, source_target_pairs={{0,8},{4,12},{8,0},{12,4},{1,9},{5,13},{9,1},{13,5},{2,10},{6,14},... | collective-permute-start | bytes 786440 | tf_op jit(solution)/shard_map/ppermute | solution.py:447
  62.0 5.0 %collective-permute-start.21 = (bf16[64,1024]{1,0:T(8,128)(2,1)S(1)}, bf16[64,1024]{1,0:T(8,128)(2,1)S(1)}, u32[]{:S(2)}, u32[]{:S(2)}) collective-permute-start(bf16[64,1024]{1,0:T(8,128)(2,1)S(1)} %get-tuple-element.63.refs_1_), channel_id=1, source_target_pairs={{0,1},{1,0},{2,3},{3,2},{4,5},{5,4},{6,7},{7,6},{8,9},{9,8},{10,11... | collective-permute-start | bytes 393224 | tf_op jit(solution)/shard_map/ppermute | solution.py:444
  67.0 5.2 %collective-permute-start.23 = (bf16[64,1024]{1,0:T(8,128)(2,1)S(1)}, bf16[64,1024]{1,0:T(8,128)(2,1)S(1)}, u32[]{:S(2)}, u32[]{:S(2)}) collective-permute-start(bf16[64,1024]{1,0:T(8,128)(2,1)S(1)} %get-tuple-element.65.refs_1_), channel_id=1, source_target_pairs={{0,1},{1,0},{2,3},{3,2},{4,5},{5,4},{6,7},{7,6},{8,9},{9,8},{10,11... | collective-permute-start | bytes 393224 | tf_op jit(solution)/shard_map/ppermute | solution.py:444
  67.0 5.2 %collective-permute-start.22 = (bf16[64,1024]{1,0:T(8,128)(2,1)S(1)}, bf16[64,1024]{1,0:T(8,128)(2,1)S(1)}, u32[]{:S(2)}, u32[]{:S(2)}) collective-permute-start(bf16[64,1024]{1,0:T(8,128)(2,1)S(1)} %collective-permute-done.21.refs_1_), channel_id=1, source_target_pairs={{0,8},{4,12},{8,0},{12,4},{1,9},{5,13},{9,1},{13,5},{2,10},{6,14},... | collective-permute-start | bytes 393224 | tf_op jit(solution)/shard_map/ppermute | solution.py:447
  67.8 5.8 %collective-permute-start.25 = (bf16[64,1024]{1,0:T(8,128)(2,1)S(1)}, bf16[64,1024]{1,0:T(8,128)(2,1)S(1)}, u32[]{:S(2)}, u32[]{:S(2)}) collective-permute-start(bf16[64,1024]{1,0:T(8,128)(2,1)S(1)} %slice.73), channel_id=1, source_target_pairs={{0,1},{1,0},{2,3},{3,2},{4,5},{5,4},{6,7},{7,6},{8,9},{9,8},{10,11... | collective-permute-start | bytes 393224 | tf_op jit(solution)/shard_map/ppermute | solution.py:444
  73.0 2.0 %collective-permute-start.24 = (bf16[128,2176]{1,0:T(8,128)(2,1)S(1)}, bf16[128,2176]{1,0:T(8,128)(2,1)S(1)}, u32[]{:S(2)}, u32[]{:S(2)}) collective-permute-start(bf16[128,2176]{1,0:T(8,128)(2,1)S(1)} %shard_map.116.refs_0_), channel_id=1, source_target_pairs={{0,4},{4,0},{8,12},{12,8},{1,5},{5,1},{9,13},{13,9},{2,6},{6,2},{1... | collective-permute-start | bytes 1671176 | tf_op jit(solution)/shard_map/ppermute | solution.py:447
  78.3 2.4 %collective-permute-start.29 = (bf16[128,2048]{1,0:T(8,128)(2,1)S(1)}, bf16[128,2048]{1,0:T(8,128)(2,1)S(1)}, u32[]{:S(2)}, u32[]{:S(2)}) collective-permute-start(bf16[128,2048]{1,0:T(8,128)(2,1)S(1)} %get-tuple-element.73), channel_id=1, source_target_pairs={{0,4},{4,0},{8,12},{12,8},{1,5},{5,1},{9,13},{13,9},{2,6},{6,2},{1... | collective-permute-start | bytes 1572872 | tf_op jit(solution)/shard_map/ppermute | solution.py:447
  78.5 7.2 %collective-permute-start.27 = (bf16[128,2176]{1,0:T(8,128)(2,1)S(1)}, bf16[128,2176]{1,0:T(8,128)(2,1)S(1)}, u32[]{:S(2)}, u32[]{:S(2)}) collective-permute-start(bf16[128,2176]{1,0:T(8,128)(2,1)S(1)} %shard_map.117.refs_0_), channel_id=1, source_target_pairs={{0,4},{4,0},{8,12},{12,8},{1,5},{5,1},{9,13},{13,9},{2,6},{6,2},{1... | collective-permute-start | bytes 1671176 | tf_op jit(solution)/shard_map/ppermute | solution.py:447
  79.6 2.2 %collective-permute-start.28 = (bf16[128,2176]{1,0:T(8,128)(2,1)S(1)}, bf16[128,2176]{1,0:T(8,128)(2,1)S(1)}, u32[]{:S(2)}, u32[]{:S(2)}) collective-permute-start(bf16[128,2176]{1,0:T(8,128)(2,1)S(1)} %shard_map.120.refs_0_), channel_id=1, source_target_pairs={{0,4},{4,0},{8,12},{12,8},{1,5},{5,1},{9,13},{13,9},{2,6},{6,2},{1... | collective-permute-start | bytes 1671176 | tf_op jit(solution)/shard_map/ppermute | solution.py:447
  80.8 8.7 %collective-permute-start.31 = (bf16[64,2048]{1,0:T(8,128)(2,1)S(1)}, bf16[64,2048]{1,0:T(8,128)(2,1)S(1)}, u32[]{:S(2)}, u32[]{:S(2)}) collective-permute-start(bf16[64,2048]{1,0:T(8,128)(2,1)S(1)} %add_convert_fusion.7), channel_id=1, source_target_pairs={{0,8},{4,12},{8,0},{12,4},{1,9},{5,13},{9,1},{13,5},{2,10},{6,14},... | collective-permute-start | bytes 786440 | tf_op jit(solution)/shard_map/ppermute | solution.py:447
  85.0 6.3 %collective-permute-start.30 = (bf16[128,2048]{1,0:T(8,128)(2,1)S(1)}, bf16[128,2048]{1,0:T(8,128)(2,1)S(1)}, u32[]{:S(2)}, u32[]{:S(2)}) collective-permute-start(bf16[128,2048]{1,0:T(8,128)(2,1)S(1)} %get-tuple-element.81), channel_id=1, source_target_pairs={{0,4},{4,0},{8,12},{12,8},{1,5},{5,1},{9,13},{13,9},{2,6},{6,2},{1... | collective-permute-start | bytes 1572872 | tf_op jit(solution)/shard_map/ppermute | solution.py:447
  85.2 7.1 %collective-permute-start.26 = (bf16[128,2176]{1,0:T(8,128)(2,1)S(1)}, bf16[128,2176]{1,0:T(8,128)(2,1)S(1)}, u32[]{:S(2)}, u32[]{:S(2)}) collective-permute-start(bf16[128,2176]{1,0:T(8,128)(2,1)S(1)} %get-tuple-element.83.refs_0_), channel_id=1, source_target_pairs={{0,4},{4,0},{8,12},{12,8},{1,5},{5,1},{9,13},{13,9},{2,6},{6,2},{1... | collective-permute-start | bytes 1671176 | tf_op jit(solution)/shard_map/ppermute | solution.py:447
  89.4 6.1 %collective-permute-start.34 = (bf16[128,2048]{1,0:T(8,128)(2,1)S(1)}, bf16[128,2048]{1,0:T(8,128)(2,1)S(1)}, u32[]{:S(2)}, u32[]{:S(2)}) collective-permute-start(bf16[128,2048]{1,0:T(8,128)(2,1)S(1)} %get-tuple-element.89), channel_id=1, source_target_pairs={{0,4},{4,0},{8,12},{12,8},{1,5},{5,1},{9,13},{13,9},{2,6},{6,2},{1... | collective-permute-start | bytes 1572872 | tf_op jit(solution)/shard_map/ppermute | solution.py:447
  89.5 11.1 %collective-permute-start.38 = (bf16[64,2048]{1,0:T(8,128)(2,1)S(1)}, bf16[64,2048]{1,0:T(8,128)(2,1)S(1)}, u32[]{:S(2)}, u32[]{:S(2)}) collective-permute-start(bf16[64,2048]{1,0:T(8,128)(2,1)S(1)} %add_convert_fusion.2), channel_id=1, source_target_pairs={{0,1},{1,0},{2,3},{3,2},{4,5},{5,4},{6,7},{7,6},{8,9},{9,8},{10,11... | collective-permute-start | bytes 786440 | tf_op jit(solution)/shard_map/ppermute | solution.py:444
  91.4 9.2 %collective-permute-start.32 = (bf16[64,2048]{1,0:T(8,128)(2,1)S(1)}, bf16[64,2048]{1,0:T(8,128)(2,1)S(1)}, u32[]{:S(2)}, u32[]{:S(2)}) collective-permute-start(bf16[64,2048]{1,0:T(8,128)(2,1)S(1)} %add_convert_fusion.6), channel_id=1, source_target_pairs={{0,8},{4,12},{8,0},{12,4},{1,9},{5,13},{9,1},{13,5},{2,10},{6,14},... | collective-permute-start | bytes 786440 | tf_op jit(solution)/shard_map/ppermute | solution.py:447
  95.6 10.0 %collective-permute-start.36 = (bf16[64,2048]{1,0:T(8,128)(2,1)S(1)}, bf16[64,2048]{1,0:T(8,128)(2,1)S(1)}, u32[]{:S(2)}, u32[]{:S(2)}) collective-permute-start(bf16[64,2048]{1,0:T(8,128)(2,1)S(1)} %add_convert_fusion.4), channel_id=1, source_target_pairs={{0,8},{4,12},{8,0},{12,4},{1,9},{5,13},{9,1},{13,5},{2,10},{6,14},... | collective-permute-start | bytes 786440 | tf_op jit(solution)/shard_map/ppermute | solution.py:447
  100.6 5.4 %collective-permute-start.33 = (bf16[128,2048]{1,0:T(8,128)(2,1)S(1)}, bf16[128,2048]{1,0:T(8,128)(2,1)S(1)}, u32[]{:S(2)}, u32[]{:S(2)}) collective-permute-start(bf16[128,2048]{1,0:T(8,128)(2,1)S(1)} %get-tuple-element.87), channel_id=1, source_target_pairs={{0,4},{4,0},{8,12},{12,8},{1,5},{5,1},{9,13},{13,9},{2,6},{6,2},{1... | collective-permute-start | bytes 1572872 | tf_op jit(solution)/shard_map/ppermute | solution.py:447
  100.8 15.1 %collective-permute-start.39 = (bf16[64,2048]{1,0:T(8,128)(2,1)S(1)}, bf16[64,2048]{1,0:T(8,128)(2,1)S(1)}, u32[]{:S(2)}, u32[]{:S(2)}) collective-permute-start(bf16[64,2048]{1,0:T(8,128)(2,1)S(1)} %add_convert_fusion.1), channel_id=1, source_target_pairs={{0,2},{1,3},{2,0},{3,1},{4,6},{5,7},{6,4},{7,5},{8,10},{9,11},{10,... | collective-permute-start | bytes 786440 | tf_op jit(solution)/shard_map/ppermute | solution.py:444
  105.6 13.2 %collective-permute-start.37 = (bf16[64,2048]{1,0:T(8,128)(2,1)S(1)}, bf16[64,2048]{1,0:T(8,128)(2,1)S(1)}, u32[]{:S(2)}, u32[]{:S(2)}) collective-permute-start(bf16[64,2048]{1,0:T(8,128)(2,1)S(1)} %add_convert_fusion.3), channel_id=1, source_target_pairs={{0,1},{1,0},{2,3},{3,2},{4,5},{5,4},{6,7},{7,6},{8,9},{9,8},{10,11... | collective-permute-start | bytes 786440 | tf_op jit(solution)/shard_map/ppermute | solution.py:444
  106.1 12.8 %collective-permute-start.35 = (bf16[64,2048]{1,0:T(8,128)(2,1)S(1)}, bf16[64,2048]{1,0:T(8,128)(2,1)S(1)}, u32[]{:S(2)}, u32[]{:S(2)}) collective-permute-start(bf16[64,2048]{1,0:T(8,128)(2,1)S(1)} %add_convert_fusion.5), channel_id=1, source_target_pairs={{0,8},{4,12},{8,0},{12,4},{1,9},{5,13},{9,1},{13,5},{2,10},{6,14},... | collective-permute-start | bytes 786440 | tf_op jit(solution)/shard_map/ppermute | solution.py:447
  (3 other events, 7.1 us)

commit v3 on v2

--- a/solution.py
+++ b/solution.py
@@ -193,11 +193,11 @@
 
 
 def attend_kernel(seq_count, role_count, slots, groups, at_ref, *refs):
-    last_block, *refs = refs
-    count = seq_count + 2
+    last_block, proj_ref, *refs = refs
+    count = seq_count
     attended_ref, *partial_refs = refs[count : count + 1 + len(groups)]
     copies, (query_ref, *buffers) = start_fetch(refs[:count], refs[count + 1 + len(groups) :])
-    blocks, proj_refs = buffers[: seq_count - 1] + [last_block], buffers[seq_count - 1 :]
+    blocks = buffers + [last_block]
     seq_index, role_index = at_ref[0], at_ref[1]
     local_length = query_ref.shape[1]
     local_heads = query_ref.shape[2] // HEAD_WIDTH
@@ -217,7 +217,7 @@
     )
     seen = key_position <= query_position
     scale = HEAD_WIDTH ** (-0.5) * LOG2_E
-    for copy in copies[:seq_count]:
+    for copy in copies:
         copy.wait()
     for n, k in enumerate(slots):
         b = role_index ^ k
@@ -239,13 +239,23 @@
             attended_ref[
                 n * local_length : (n + 1) * local_length, h * HEAD_WIDTH : (h + 1) * HEAD_WIDTH
             ] = attended[h * local_length : (h + 1) * local_length]
-    for copy in copies[seq_count:]:
+    project_into(slots, groups, attended_ref, proj_ref, partial_refs)
+
+
+def columns_kernel(*refs):
+    *from_refs, to_ref, sems = refs
+    copies, at = [], 0
+    for n, ref in enumerate(from_refs):
+        width = ref.shape[1]
+        copies.append(pltpu.make_async_copy(ref, to_ref.at[:, at : at + width], sems.at[n]))
+        copies[-1].start()
+        at += width
+    for copy in copies:
         copy.wait()
-    project_into(slots, groups, attended_ref, proj_refs, partial_refs)
 
 
 def join_kernel(*refs):
-    *piece_refs, out_ref = refs
+    *piece_refs, _, out_ref = refs
     at = 0
     for ref in piece_refs:
         size = ref.shape[1]
@@ -259,14 +269,13 @@
     return [[k for k in range(role_count) if k & -k == bit] for bit in bits] + [[0, last]]
 
 
-def project_into(slots, groups, attended_ref, proj_refs, partial_refs):
+def project_into(slots, groups, attended_ref, proj_ref, partial_refs):
     slots = list(slots)
     rows = attended_ref.shape[0] // len(slots)
-    at = 0
-    for proj_ref in proj_refs:
-        width = proj_ref.shape[1]
+    width = 512 if proj_ref.shape[1] % 512 == 0 else proj_ref.shape[1]
+    for at in range(0, proj_ref.shape[1], width):
         product = jnp.dot(
-            attended_ref[...], proj_ref[...], preferred_element_type=jnp.float32
+            attended_ref[...], proj_ref[:, at : at + width], preferred_element_type=jnp.float32
         ).astype(jnp.bfloat16)
         for group, partial_ref in zip(groups, partial_refs):
             for n, k in enumerate(group):
@@ -274,15 +283,10 @@
                 partial_ref[n * rows : (n + 1) * rows, at : at + width] = product[
                     start : start + rows
                 ]
-        at += width
-
-
-def project_kernel(slots, groups, attended_ref, order_ref, *refs):
-    count = (len(refs) - len(groups) - 1) // 2
-    copies, proj_refs = start_fetch(refs[:count], refs[count + len(groups) :])
-    for copy in copies:
-        copy.wait()
-    project_into(slots, groups, attended_ref, proj_refs, refs[count : count + len(groups)])
+
+
+def project_kernel(slots, groups, attended_ref, proj_ref, order_ref, *partial_refs):
+    project_into(slots, groups, attended_ref, proj_ref, partial_refs)
 
 
 def partial_shapes(groups, rows, width):
@@ -461,18 +465,27 @@
             axis=2,
         )
         pieces.append(piece)
+    near_proj = pl.pallas_call(
+        columns_kernel,
+        in_specs=hbm_specs(1) + in_vmem(1),
+        out_specs=pl.BlockSpec(memory_space=pltpu.VMEM),
+        out_shape=jax.ShapeDtypeStruct((query_width, 2 * block_width), jnp.bfloat16),
+        scratch_shapes=[pltpu.SemaphoreType.DMA((2,))],
+        compiler_params=pltpu.CompilerParams(vmem_limit_bytes=COPY_VMEM),
+        cost_estimate=NOTHING,
+    )(*in_hbm(output_weight), beside_proj)
     pieces[1] = after(pieces[1], beside_proj)
     pieces = [piece if k == 0 else over_role(piece, k) for k, piece in enumerate(pieces)]
     block = pl.pallas_call(
         join_kernel,
-        in_specs=in_vmem(len(pieces)),
+        in_specs=in_vmem(len(pieces)) + [pl.BlockSpec(memory_space=pl.ANY)],
         out_specs=pl.BlockSpec(memory_space=pltpu.VMEM),
         out_shape=jax.ShapeDtypeStruct(
             (batch_count, local_length, 2 * HEAD_WIDTH), jnp.bfloat16
         ),
         compiler_params=pltpu.CompilerParams(vmem_limit_bytes=COPY_VMEM),
         cost_estimate=SHORT,
-    )(*pieces)
+    )(*pieces, near_proj)
     same_core = [block] + [over_seq(block, j) for j in across_steps]
     blocks = []
     for part in same_core:
@@ -490,7 +503,7 @@
     rows = batch_count * local_length
     near_width = 2 * output_weight.shape[1]
     groups = role_groups(role_count)
-    attend_args = in_hbm(query_rows, *blocks[:-1], output_weight, beside_proj)
+    attend_args = in_hbm(query_rows, *blocks[:-1])
     slot_sets = [(range(1, role_count, 2), groups[:1]), (range(0, role_count, 2), groups[1:])]
     attended, near = [], []
     for slots, parts in slot_sets:
@@ -498,14 +511,14 @@
         half, *partials = pl.pallas_call(
             partial(attend_kernel, seq_count, role_count, slots, parts),
             in_specs=[pl.BlockSpec(memory_space=pltpu.SMEM)]
-            + in_vmem(1)
+            + in_vmem(2)
             + hbm_specs(len(attend_args)),
             out_specs=in_vmem(1 + len(parts)),
             out_shape=[half_rows] + partial_shapes(parts, local_length, near_width),
             scratch_shapes=fetch_scratch(*attend_args),
             compiler_params=pltpu.CompilerParams(vmem_limit_bytes=SMALL_VMEM),
             cost_estimate=SHORT,
-        )(at, blocks[-1], *attend_args)
+        )(at, blocks[-1], near_proj, *attend_args)
         attended.append(half)
         near += partials
 
@@ -586,13 +599,12 @@
         for half, (slots, parts) in zip(attended, slot_sets):
             far += pl.pallas_call(
                 partial(project_kernel, slots, parts),
-                in_specs=in_vmem(1) + [pl.BlockSpec(memory_space=pl.ANY)] + hbm_specs(2),
+                in_specs=in_vmem(2) + [pl.BlockSpec(memory_space=pl.ANY)],
                 out_specs=in_vmem(len(parts)),
                 out_shape=partial_shapes(parts, local_length, near_width),
-                scratch_shapes=fetch_scratch(output_weight, beside_proj),
                 compiler_params=pltpu.CompilerParams(vmem_limit_bytes=SMALL_VMEM),
                 cost_estimate=SHORT,
-            )(over_seq(half, j), other_routes, *in_hbm(output_weight, beside_proj))
+            )(over_seq(half, j), near_proj, other_routes)
         sent.append(summed_over_role(far, residuals[n], near_halves[0]))
         came.append(over_role(sent[-1], last))
 

time: 120 us -> 120 us (level)
  Pallas kernels: 26.5 us -> 24.3 us
  waiting for transfers between devices: 56.9 us -> 59 us
    pallas_call x3 -> x4, Pallas kernels: 4.03 us -> 2.19 us  [the longest x1 1.24 us: gathered_shards(): pl.pallas_call(columns_kernel, in_specs=hbm_specs(1) + in_vmem(1), out_sp...]
    ppermute x23, waiting for transfers between devices: 16.2 us -> 17.8 us  [over_seq(): return lax.ppermute(array, 'seq', [(i, i ^ j) for i in range(seq_count)])]
  transfers between devices with their start and end apart: 40 -> 40, of which waited for: 23 -> 21; matrix products, arithmetic and copies ran while one was open for 2% -> 2% of each run, Pallas kernels for 19% -> 18%
where the time goes in v3:
time: 120 us
  waiting for transfers between devices  59 us (49%)
  starting transfers between devices  33.1 us (28%)
  Pallas kernels  24.3 us (20%)
  other arithmetic  1.81 us (2%)
    ppermute x17, waiting for transfers between devices, over_role(): return lax.ppermute(array, 'role', [(i, i ^ k) for i in range(role_count)])  41.2 us
    ppermute x17, starting transfers between devices, over_role(): return lax.ppermute(array, 'role', [(i, i ^ k) for i in range(role_count)])  18 us
    ppermute x23, waiting for transfers between devices, over_seq(): return lax.ppermute(array, 'seq', [(i, i ^ j) for i in range(seq_count)])  17.8 us
    ppermute x23, starting transfers between devices, over_seq(): return lax.ppermute(array, 'seq', [(i, i ^ j) for i in range(seq_count)])  15.1 us
    pallas_call x4, Pallas kernels, run_expert(): pl.pallas_call(partial(expert_kernel, len(tokens)), in_specs=[pl.BlockSpe...  13 us
    pallas_call x2, Pallas kernels, gathered_shards(): pl.pallas_call(partial(attend_kernel, seq_count, role_count, slots, parts...  5.35 us
    pallas_call x4, Pallas kernels, normed_rows(): pl.pallas_call(partial(norm_kernel, chips, *firsts), in_specs=[pl.BlockSp...  3.26 us
  transfers between devices with their start and end apart: 40, of which 21 were waited for; matrix products, arithmetic and copies ran while one was open for 2% of the time, Pallas kernels for 18%

profile of v3, /device:TPU:0, one launch (start us, length us, event | category | flops | bytes accessed | tf_op | source)
XLA Modules:
  0.0 119.5 jit_solution(9251409606204973881)
XLA Ops:
  0.5 0.8 constant_dynamic-slice_fusion
  1.3 3.7 %collective-permute-start.3 = (bf16[4,16,256]{2,1,0:T(8,128)(2,1)S(1)}, bf16[4,16,256]{2,1,0:T(8,128)(2,1)S(1)}, u32[]{:S(2)}, u32[]{:S(2)}) collective-permute-start(bf16[4,16,256]{2,1,0:T(8,128)(2,1)S(1)} %pad_maximum_fusion.3), channel_id=1, source_target_pairs={{0,2},{1,3},{2,0},{3,1},{4,6},{5,7},{6,4},{7,5},{8,10},{9,11},{10,... | collective-permute-start | bytes 98312 | tf_op jit(solution)/shard_map/ppermute | solution.py:448
  5.0 1.3 %collective-permute-start.4 = (bf16[4,16,256]{2,1,0:T(8,128)(2,1)S(1)}, bf16[4,16,256]{2,1,0:T(8,128)(2,1)S(1)}, u32[]{:S(2)}, u32[]{:S(2)}) collective-permute-start(bf16[4,16,256]{2,1,0:T(8,128)(2,1)S(1)} %pad_maximum_fusion.4), channel_id=1, source_target_pairs={{0,3},{1,2},{2,1},{3,0},{4,7},{5,6},{6,5},{7,4},{8,11},{9,10},{10,... | collective-permute-start | bytes 98312 | tf_op jit(solution)/shard_map/ppermute | solution.py:448
  6.7 1.2 %shard_map.109.refs_4_.refs_1_.proj_ref = bf16[1024,1024]{1,0:T(8,128)(2,1)S(1)} custom-call(bf16[1024,512]{1,0:T(8,128)(2,1)} %refs_0_.1, bf16[1024,512]{1,0:T(8,128)(2,1)S(1)} %collective-permute-done.1.refs_1_), custom_call_target="tpu_custom_call" | custom-call | flops 1 | bytes 1 | tf_op jit(solution)/shard_map/pallas_call | solution.py:468
  8.0 2.8 %collective-permute-done.4.refs_3_ = bf16[4,16,256]{2,1,0:T(8,128)(2,1)S(1)} collective-permute-done((bf16[4,16,256]{2,1,0:T(8,128)(2,1)S(1)}, bf16[4,16,256]{2,1,0:T(8,128)(2,1)S(1)}, u32[]{:S(2)}, u32[]{:S(2)}) %collective-permute-start.4) | collective-permute-done | bytes 32800 | tf_op jit(solution)/shard_map/ppermute | solution.py:448
  10.8 1.6 %collective-permute-start.5 = (bf16[4,64,256]{2,1,0:T(8,128)(2,1)S(1)}, bf16[4,64,256]{2,1,0:T(8,128)(2,1)S(1)}, u32[]{:S(2)}, u32[]{:S(2)}) collective-permute-start(bf16[4,64,256]{2,1,0:T(8,128)(2,1)S(1)} %shard_map.110.refs_3_), channel_id=1, source_target_pairs={{0,8},{4,12},{8,0},{12,4},{1,9},{5,13},{9,1},{13,5},{2,10},{6,14},... | collective-permute-start | bytes 393224 | tf_op jit(solution)/shard_map/ppermute | solution.py:451
  12.5 1.3 %collective-permute-start = (f32[64,16]{1,0:T(8,128)S(1)}, f32[64,16]{1,0:T(8,128)S(1)}, u32[]{:S(2)}, u32[]{:S(2)}) collective-permute-start(f32[64,16]{1,0:T(8,128)S(1)} %copy.15.route_ref), channel_id=1, source_target_pairs={{0,2},{1,3},{2,0},{3,1},{4,6},{5,7},{6,4},{7,5},{8,10},{9,11},{10,... | collective-permute-start | bytes 12296 | tf_op jit(solution)/shard_map/ppermute | solution.py:448
  13.7 2.1 %collective-permute-done.5.refs_5_ = bf16[4,64,256]{2,1,0:T(8,128)(2,1)S(1)} collective-permute-done((bf16[4,64,256]{2,1,0:T(8,128)(2,1)S(1)}, bf16[4,64,256]{2,1,0:T(8,128)(2,1)S(1)}, u32[]{:S(2)}, u32[]{:S(2)}) %collective-permute-start.5) | collective-permute-done | bytes 131104 | tf_op jit(solution)/shard_map/ppermute | solution.py:451
  16.0 1.2 %collective-permute-done.6.refs_0_ = bf16[4,64,256]{2,1,0:T(8,128)(2,1)S(1)} collective-permute-done((bf16[4,64,256]{2,1,0:T(8,128)(2,1)S(1)}, bf16[4,64,256]{2,1,0:T(8,128)(2,1)S(1)}, u32[]{:S(2)}, u32[]{:S(2)}) %collective-permute-start.6) | collective-permute-done | bytes 131104 | tf_op jit(solution)/shard_map/ppermute | solution.py:451
  17.2 2.7 %shard_map.112 = (bf16[128,1024]{1,0:T(8,128)(2,1)S(1)}, bf16[128,1024]{1,0:T(8,128)(2,1)S(1)}) custom-call(s32[3]{0:T(128)S(1)} %pad_add_fusion.at_ref, bf16[4,64,256]{2,1,0:T(8,128)(2,1)S(1)} %collective-permute-done.6.refs_0_, bf16[1024,1024]{1,0:T(8,128)(2,1)S(1)} %shard_map.109.refs_4_.refs_1_.proj_ref, bf16[4,64,1024]{2,1,0:T(8,128)(2,1)} %refs_2_.7, ...), custom_call_target="tpu_custom_call" | custom-call | flops 2000000000 | bytes 4194304 | tf_op jit(solution)/shard_map/pallas_call | solution.py:511
  20.0 1.6 %collective-permute-start.15 = (bf16[128,1024]{1,0:T(8,128)(2,1)S(1)}, bf16[128,1024]{1,0:T(8,128)(2,1)S(1)}, u32[]{:S(2)}, u32[]{:S(2)}) collective-permute-start(bf16[128,1024]{1,0:T(8,128)(2,1)S(1)} %get-tuple-element.57), channel_id=1, source_target_pairs={{0,8},{4,12},{8,0},{12,4},{1,9},{5,13},{9,1},{13,5},{2,10},{6,14},... | collective-permute-start | bytes 786440 | tf_op jit(solution)/shard_map/ppermute | solution.py:451
  21.6 2.7 %shard_map.111 = (bf16[128,1024]{1,0:T(8,128)(2,1)S(1)}, bf16[128,1024]{1,0:T(8,128)(2,1)S(1)}) custom-call(s32[3]{0:T(128)S(1)} %pad_add_fusion.at_ref, bf16[4,64,256]{2,1,0:T(8,128)(2,1)S(1)} %collective-permute-done.6.refs_0_, bf16[1024,1024]{1,0:T(8,128)(2,1)S(1)} %shard_map.109.refs_4_.refs_1_.proj_ref, bf16[4,64,1024]{2,1,0:T(8,128)(2,1)} %refs_2_.7, ...), custom_call_target="tpu_custom_call" | custom-call | flops 2000000000 | bytes 4194304 | tf_op jit(solution)/shard_map/pallas_call | solution.py:511
  24.8 1.5 %collective-permute-start.17 = (bf16[64,1024]{1,0:T(8,128)(2,1)S(1)}, bf16[64,1024]{1,0:T(8,128)(2,1)S(1)}, u32[]{:S(2)}, u32[]{:S(2)}) collective-permute-start(bf16[64,1024]{1,0:T(8,128)(2,1)S(1)} %pad_maximum_fusion), channel_id=1, source_target_pairs={{0,8},{4,12},{8,0},{12,4},{1,9},{5,13},{9,1},{13,5},{2,10},{6,14},... | collective-permute-start | bytes 393224 | tf_op jit(solution)/shard_map/ppermute | solution.py:451
  26.3 2.0 %collective-permute-done.8 = bf16[128,1024]{1,0:T(8,128)(2,1)S(1)} collective-permute-done((bf16[128,1024]{1,0:T(8,128)(2,1)S(1)}, bf16[128,1024]{1,0:T(8,128)(2,1)S(1)}, u32[]{:S(2)}, u32[]{:S(2)}) %collective-permute-start.8) | collective-permute-done | bytes 262176 | tf_op jit(solution)/shard_map/ppermute | solution.py:448
  28.4 1.5 %collective-permute-start.9 = (bf16[128,1024]{1,0:T(8,128)(2,1)S(1)}, bf16[128,1024]{1,0:T(8,128)(2,1)S(1)}, u32[]{:S(2)}, u32[]{:S(2)}) collective-permute-start(bf16[128,1024]{1,0:T(8,128)(2,1)S(1)} %add_convert_fusion.9.sent), channel_id=1, source_target_pairs={{0,2},{1,3},{2,0},{3,1},{4,6},{5,7},{6,4},{7,5},{8,10},{9,11},{10,... | collective-permute-start | bytes 786440 | tf_op jit(solution)/shard_map/ppermute | solution.py:448
  30.4 1.4 %collective-permute-start.16 = (bf16[128,1024]{1,0:T(8,128)(2,1)S(1)}, bf16[128,1024]{1,0:T(8,128)(2,1)S(1)}, u32[]{:S(2)}, u32[]{:S(2)}) collective-permute-start(bf16[128,1024]{1,0:T(8,128)(2,1)S(1)} %shard_map.115), channel_id=1, source_target_pairs={{0,1},{1,0},{2,3},{3,2},{4,5},{5,4},{6,7},{7,6},{8,9},{9,8},{10,11... | collective-permute-start | bytes 786440 | tf_op jit(solution)/shard_map/ppermute | solution.py:448
  31.8 3.1 %collective-permute-done.14.attended_ref = bf16[128,1024]{1,0:T(8,128)(2,1)S(1)} collective-permute-done((bf16[128,1024]{1,0:T(8,128)(2,1)S(1)}, bf16[128,1024]{1,0:T(8,128)(2,1)S(1)}, u32[]{:S(2)}, u32[]{:S(2)}) %collective-permute-start.14) | collective-permute-done | bytes 262176 | tf_op jit(solution)/shard_map/ppermute | solution.py:451
  35.3 7.3 %collective-permute-done.9.came_ref = bf16[128,1024]{1,0:T(8,128)(2,1)S(1)} collective-permute-done((bf16[128,1024]{1,0:T(8,128)(2,1)S(1)}, bf16[128,1024]{1,0:T(8,128)(2,1)S(1)}, u32[]{:S(2)}, u32[]{:S(2)}) %collective-permute-start.9) | collective-permute-done | bytes 262176 | tf_op jit(solution)/shard_map/ppermute | solution.py:448
  43.1 1.6 %collective-permute-start.10 = (bf16[128,1152]{1,0:T(8,128)(2,1)S(1)}, bf16[128,1152]{1,0:T(8,128)(2,1)S(1)}, u32[]{:S(2)}, u32[]{:S(2)}) collective-permute-start(bf16[128,1152]{1,0:T(8,128)(2,1)S(1)} %get-tuple-element.53), channel_id=1, source_target_pairs={{0,8},{4,12},{8,0},{12,4},{1,9},{5,13},{9,1},{13,5},{2,10},{6,14},... | collective-permute-start | bytes 884744 | tf_op jit(solution)/shard_map/ppermute | solution.py:451
  44.8 2.5 %collective-permute-start.18 = (bf16[128,1024]{1,0:T(8,128)(2,1)S(1)}, bf16[128,1024]{1,0:T(8,128)(2,1)S(1)}, u32[]{:S(2)}, u32[]{:S(2)}) collective-permute-start(bf16[128,1024]{1,0:T(8,128)(2,1)S(1)} %add_convert_fusion.8.refs_8_), channel_id=1, source_target_pairs={{0,2},{1,3},{2,0},{3,1},{4,6},{5,7},{6,4},{7,5},{8,10},{9,11},{10,... | collective-permute-start | bytes 786440 | tf_op jit(solution)/shard_map/ppermute | solution.py:448
  47.3 3.3 %collective-permute-done.11.refs_1_.refs_0_ = bf16[64,1152]{1,0:T(8,128)(2,1)S(1)} collective-permute-done((bf16[64,1152]{1,0:T(8,128)(2,1)S(1)}, bf16[64,1152]{1,0:T(8,128)(2,1)S(1)}, u32[]{:S(2)}, u32[]{:S(2)}) %collective-permute-start.11) | collective-permute-done | bytes 147488 | tf_op jit(solution)/shard_map/ppermute | solution.py:448
  50.6 1.4 %collective-permute-done.10.refs_0_.refs_2_ = bf16[128,1152]{1,0:T(8,128)(2,1)S(1)} collective-permute-done((bf16[128,1152]{1,0:T(8,128)(2,1)S(1)}, bf16[128,1152]{1,0:T(8,128)(2,1)S(1)}, u32[]{:S(2)}, u32[]{:S(2)}) %collective-permute-start.10) | collective-permute-done | bytes 294944 | tf_op jit(solution)/shard_map/ppermute | solution.py:451
  52.0 1.5 %collective-permute-start.12 = (bf16[64,1152]{1,0:T(8,128)(2,1)S(1)}, bf16[64,1152]{1,0:T(8,128)(2,1)S(1)}, u32[]{:S(2)}, u32[]{:S(2)}) collective-permute-start(bf16[64,1152]{1,0:T(8,128)(2,1)S(1)} %collective-permute-done.11.refs_1_.refs_0_), channel_id=1, source_target_pairs={{0,8},{4,12},{8,0},{12,4},{1,9},{5,13},{9,1},{13,5},{2,10},{6,14},... | collective-permute-start | bytes 442376 | tf_op jit(solution)/shard_map/ppermute | solution.py:451
  53.6 1.7 %collective-permute-start.20 = (bf16[64,1152]{1,0:T(8,128)(2,1)S(1)}, bf16[64,1152]{1,0:T(8,128)(2,1)S(1)}, u32[]{:S(2)}, u32[]{:S(2)}) collective-permute-start(bf16[64,1152]{1,0:T(8,128)(2,1)S(1)} %slice.72), channel_id=1, source_target_pairs={{0,1},{1,0},{2,3},{3,2},{4,5},{5,4},{6,7},{7,6},{8,9},{9,8},{10,11... | collective-permute-start | bytes 442376 | tf_op jit(solution)/shard_map/ppermute | solution.py:448
  55.3 1.6 %collective-permute-done.13.refs_3_.refs_0_ = bf16[64,1152]{1,0:T(8,128)(2,1)S(1)} collective-permute-done((bf16[64,1152]{1,0:T(8,128)(2,1)S(1)}, bf16[64,1152]{1,0:T(8,128)(2,1)S(1)}, u32[]{:S(2)}, u32[]{:S(2)}) %collective-permute-start.13) | collective-permute-done | bytes 147488 | tf_op jit(solution)/shard_map/ppermute | solution.py:448
  56.9 2.5 %collective-permute-done.18.refs_7_ = bf16[128,1024]{1,0:T(8,128)(2,1)S(1)} collective-permute-done((bf16[128,1024]{1,0:T(8,128)(2,1)S(1)}, bf16[128,1024]{1,0:T(8,128)(2,1)S(1)}, u32[]{:S(2)}, u32[]{:S(2)}) %collective-permute-start.18) | collective-permute-done | bytes 262176 | tf_op jit(solution)/shard_map/ppermute | solution.py:448
  60.1 1.7 %collective-permute-done.20.refs_2_ = bf16[64,1152]{1,0:T(8,128)(2,1)S(1)} collective-permute-done((bf16[64,1152]{1,0:T(8,128)(2,1)S(1)}, bf16[64,1152]{1,0:T(8,128)(2,1)S(1)}, u32[]{:S(2)}, u32[]{:S(2)}) %collective-permute-start.20) | collective-permute-done | bytes 147488 | tf_op jit(solution)/shard_map/ppermute | solution.py:448
  61.8 5.0 %collective-permute-done.21.refs_1_ = bf16[64,1024]{1,0:T(8,128)(2,1)S(1)} collective-permute-done((bf16[64,1024]{1,0:T(8,128)(2,1)S(1)}, bf16[64,1024]{1,0:T(8,128)(2,1)S(1)}, u32[]{:S(2)}, u32[]{:S(2)}) %collective-permute-start.21) | collective-permute-done | bytes 131104 | tf_op jit(solution)/shard_map/ppermute | solution.py:448
  66.7 0.8 collective-permute-start.22
  67.5 1.8 %collective-permute-start.25 = (bf16[64,1024]{1,0:T(8,128)(2,1)S(1)}, bf16[64,1024]{1,0:T(8,128)(2,1)S(1)}, u32[]{:S(2)}, u32[]{:S(2)}) collective-permute-start(bf16[64,1024]{1,0:T(8,128)(2,1)S(1)} %slice.73), channel_id=1, source_target_pairs={{0,1},{1,0},{2,3},{3,2},{4,5},{5,4},{6,7},{7,6},{8,9},{9,8},{10,11... | collective-permute-start | bytes 393224 | tf_op jit(solution)/shard_map/ppermute | solution.py:448
  69.4 2.6 %collective-permute-done.23.refs_1_ = bf16[64,1024]{1,0:T(8,128)(2,1)S(1)} collective-permute-done((bf16[64,1024]{1,0:T(8,128)(2,1)S(1)}, bf16[64,1024]{1,0:T(8,128)(2,1)S(1)}, u32[]{:S(2)}, u32[]{:S(2)}) %collective-permute-start.23) | collective-permute-done | bytes 131104 | tf_op jit(solution)/shard_map/ppermute | solution.py:448
  72.0 0.8 shard_map.117.refs_0_
  73.4 0.8 shard_map.118.refs_0_
  74.8 3.2 %shard_map.119 = (bf16[128,2048]{1,0:T(8,128)(2,1)S(1)}, bf16[128,2048]{1,0:T(8,128)(2,1)S(1)}) custom-call(s32[3]{0:T(128)S(1)} %pad_add_fusion.at_ref, bf16[128,2176]{1,0:T(8,128)(2,1)S(1)} %shard_map.117.refs_0_, bf16[128,2176]{1,0:T(8,128)(2,1)S(1)} %collective-permute-done.24.refs_1_, bf16[1,2048,768]{2,1,0:T(8,128)(2,1)S(1)} %copy-done, ...), custom_call_target="tpu_custom_call" | custom-call | flops 1 | bytes 1 | tf_op jit(solution)/shard_map/pallas_call | solution.py:402
  78.6 0.8 shard_map.121.refs_0_
  79.6 0.8 shard_map.120
  81.6 3.2 %shard_map.122 = (bf16[128,2048]{1,0:T(8,128)(2,1)S(1)}, bf16[128,2048]{1,0:T(8,128)(2,1)S(1)}) custom-call(s32[3]{0:T(128)S(1)} %pad_add_fusion.at_ref, bf16[128,2176]{1,0:T(8,128)(2,1)S(1)} %shard_map.121.refs_0_, bf16[128,2176]{1,0:T(8,128)(2,1)S(1)} %collective-permute-done.28.refs_1_, bf16[1,2048,768]{2,1,0:T(8,128)(2,1)S(1)} %copy-done, ...), custom_call_target="tpu_custom_call" | custom-call | flops 1 | bytes 1 | tf_op jit(solution)/shard_map/pallas_call | solution.py:402
  85.4 3.4 %shard_map.123 = (bf16[128,2048]{1,0:T(8,128)(2,1)S(1)}, bf16[128,2048]{1,0:T(8,128)(2,1)S(1)}) custom-call(s32[3]{0:T(128)S(1)} %pad_add_fusion.at_ref, bf16[128,2176]{1,0:T(8,128)(2,1)S(1)} %shard_map.118.refs_0_, bf16[128,2176]{1,0:T(8,128)(2,1)S(1)} %collective-permute-done.27.refs_1_, bf16[1,2048,768]{2,1,0:T(8,128)(2,1)S(1)} %copy-done, ...), custom_call_target="tpu_custom_call" | custom-call | flops 1 | bytes 1 | tf_op jit(solution)/shard_map/pallas_call | solution.py:402
  89.3 1.8 %collective-permute-start.38 = (bf16[64,2048]{1,0:T(8,128)(2,1)S(1)}, bf16[64,2048]{1,0:T(8,128)(2,1)S(1)}, u32[]{:S(2)}, u32[]{:S(2)}) collective-permute-start(bf16[64,2048]{1,0:T(8,128)(2,1)S(1)} %add_convert_fusion.2), channel_id=1, source_target_pairs={{0,1},{1,0},{2,3},{3,2},{4,5},{5,4},{6,7},{7,6},{8,9},{9,8},{10,11... | collective-permute-start | bytes 786440 | tf_op jit(solution)/shard_map/ppermute | solution.py:448
  91.2 0.9 collective-permute-start.32
  92.1 3.2 %shard_map.124 = (bf16[128,2048]{1,0:T(8,128)(2,1)S(1)}, bf16[128,2048]{1,0:T(8,128)(2,1)S(1)}) custom-call(s32[3]{0:T(128)S(1)} %pad_add_fusion.at_ref, bf16[128,2176]{1,0:T(8,128)(2,1)S(1)} %get-tuple-element.83.refs_0_, bf16[128,2176]{1,0:T(8,128)(2,1)S(1)} %collective-permute-done.26.refs_1_, bf16[1,2048,768]{2,1,0:T(8,128)(2,1)S(1)} %copy-done, ...), custom_call_target="tpu_custom_call" | custom-call | flops 1 | bytes 1 | tf_op jit(solution)/shard_map/pallas_call | solution.py:402
  95.4 1.3 %collective-permute-start.36 = (bf16[64,2048]{1,0:T(8,128)(2,1)S(1)}, bf16[64,2048]{1,0:T(8,128)(2,1)S(1)}, u32[]{:S(2)}, u32[]{:S(2)}) collective-permute-start(bf16[64,2048]{1,0:T(8,128)(2,1)S(1)} %add_convert_fusion.4), channel_id=1, source_target_pairs={{0,8},{4,12},{8,0},{12,4},{1,9},{5,13},{9,1},{13,5},{2,10},{6,14},... | collective-permute-start | bytes 786440 | tf_op jit(solution)/shard_map/ppermute | solution.py:451
  96.6 3.8 %collective-permute-done.32 = bf16[64,2048]{1,0:T(8,128)(2,1)S(1)} collective-permute-done((bf16[64,2048]{1,0:T(8,128)(2,1)S(1)}, bf16[64,2048]{1,0:T(8,128)(2,1)S(1)}, u32[]{:S(2)}, u32[]{:S(2)}) %collective-permute-start.32) | collective-permute-done | bytes 262176 | tf_op jit(solution)/shard_map/ppermute | solution.py:451
  100.6 4.7 %collective-permute-done.36 = bf16[64,2048]{1,0:T(8,128)(2,1)S(1)} collective-permute-done((bf16[64,2048]{1,0:T(8,128)(2,1)S(1)}, bf16[64,2048]{1,0:T(8,128)(2,1)S(1)}, u32[]{:S(2)}, u32[]{:S(2)}) %collective-permute-start.36) | collective-permute-done | bytes 262176 | tf_op jit(solution)/shard_map/ppermute | solution.py:451
  105.9 0.8 collective-permute-start.35
  106.7 9.0 %collective-permute-done.39 = bf16[64,2048]{1,0:T(8,128)(2,1)S(1)} collective-permute-done((bf16[64,2048]{1,0:T(8,128)(2,1)S(1)}, bf16[64,2048]{1,0:T(8,128)(2,1)S(1)}, u32[]{:S(2)}, u32[]{:S(2)}) %collective-permute-start.39) | collective-permute-done | bytes 262176 | tf_op jit(solution)/shard_map/ppermute | solution.py:448
  115.7 3.0 %collective-permute-done.37 = bf16[64,2048]{1,0:T(8,128)(2,1)S(1)} collective-permute-done((bf16[64,2048]{1,0:T(8,128)(2,1)S(1)}, bf16[64,2048]{1,0:T(8,128)(2,1)S(1)}, u32[]{:S(2)}, u32[]{:S(2)}) %collective-permute-start.37) | collective-permute-done | bytes 262176 | tf_op jit(solution)/shard_map/ppermute | solution.py:448
  118.6 0.9 fusion.2
  (91 shorter events, 9.2 us)
Async XLA Ops:
  0.0 6.3 %collective-permute-start.1 = (bf16[1024,512]{1,0:T(8,128)(2,1)}, bf16[1024,512]{1,0:T(8,128)(2,1)S(1)}, u32[]{:S(2)}, u32[]{:S(2)}) collective-permute-start(bf16[1024,512]{1,0:T(8,128)(2,1)} %refs_0_.1), channel_id=1, source_target_pairs={{0,4},{4,0},{8,12},{12,8},{1,5},{5,1},{9,13},{13,9},{2,6},{6,2},{1... | collective-permute-start | bytes 3145736 | tf_op jit(solution)/shard_map/ppermute | solution.py:451
  1.3 6.6 %collective-permute-start.3 = (bf16[4,16,256]{2,1,0:T(8,128)(2,1)S(1)}, bf16[4,16,256]{2,1,0:T(8,128)(2,1)S(1)}, u32[]{:S(2)}, u32[]{:S(2)}) collective-permute-start(bf16[4,16,256]{2,1,0:T(8,128)(2,1)S(1)} %pad_maximum_fusion.3), channel_id=1, source_target_pairs={{0,2},{1,3},{2,0},{3,1},{4,6},{5,7},{6,4},{7,5},{8,10},{9,11},{10,... | collective-permute-start | bytes 98312 | tf_op jit(solution)/shard_map/ppermute | solution.py:448
  5.0 5.8 %collective-permute-start.4 = (bf16[4,16,256]{2,1,0:T(8,128)(2,1)S(1)}, bf16[4,16,256]{2,1,0:T(8,128)(2,1)S(1)}, u32[]{:S(2)}, u32[]{:S(2)}) collective-permute-start(bf16[4,16,256]{2,1,0:T(8,128)(2,1)S(1)} %pad_maximum_fusion.4), channel_id=1, source_target_pairs={{0,3},{1,2},{2,1},{3,0},{4,7},{5,6},{6,5},{7,4},{8,11},{9,10},{10,... | collective-permute-start | bytes 98312 | tf_op jit(solution)/shard_map/ppermute | solution.py:448
  6.3 4.4 %collective-permute-start.2 = (bf16[4,16,256]{2,1,0:T(8,128)(2,1)S(1)}, bf16[4,16,256]{2,1,0:T(8,128)(2,1)S(1)}, u32[]{:S(2)}, u32[]{:S(2)}) collective-permute-start(bf16[4,16,256]{2,1,0:T(8,128)(2,1)S(1)} %pad_maximum_fusion.2), channel_id=1, source_target_pairs={{0,1},{1,0},{2,3},{3,2},{4,5},{5,4},{6,7},{7,6},{8,9},{9,8},{10,11... | collective-permute-start | bytes 98312 | tf_op jit(solution)/shard_map/ppermute | solution.py:448
  7.9 4.5 %copy-start.6 = (s32[1,64,8]{1,2,0:T(8,128)S(1)}, s32[1,64,8]{1,2,0:T(8,128)}, u32[]{:S(2)}) copy-start(s32[1,64,8]{1,2,0:T(8,128)} %param.17) | copy-start | bytes 6148
  7.9 4.4 %copy-start.7 = (f32[1,64,8]{1,2,0:T(8,128)S(1)}, f32[1,64,8]{1,2,0:T(8,128)}, u32[]{:S(2)}) copy-start(f32[1,64,8]{1,2,0:T(8,128)} %param.18) | copy-start | bytes 6148
  7.9 8.0 %copy-start.5 = (bf16[1,64,2048]{2,1,0:T(8,128)(2,1)S(1)}, bf16[1,64,2048]{2,1,0:T(8,128)(2,1)}, u32[]{:S(2)}) copy-start(bf16[1,64,2048]{2,1,0:T(8,128)(2,1)} %param.15) | copy-start | bytes 786436
  10.8 6.4 %copy-start.4 = (bf16[4,64,256]{2,1,0:T(8,128)(2,1)}, bf16[4,64,256]{2,1,0:T(8,128)(2,1)S(1)}, u32[]{:S(2)}) copy-start(bf16[4,64,256]{2,1,0:T(8,128)(2,1)S(1)} %shard_map.110.refs_3_) | copy-start | bytes 393220
  10.8 5.0 %collective-permute-start.5 = (bf16[4,64,256]{2,1,0:T(8,128)(2,1)S(1)}, bf16[4,64,256]{2,1,0:T(8,128)(2,1)S(1)}, u32[]{:S(2)}, u32[]{:S(2)}) collective-permute-start(bf16[4,64,256]{2,1,0:T(8,128)(2,1)S(1)} %shard_map.110.refs_3_), channel_id=1, source_target_pairs={{0,8},{4,12},{8,0},{12,4},{1,9},{5,13},{9,1},{13,5},{2,10},{6,14},... | collective-permute-start | bytes 393224 | tf_op jit(solution)/shard_map/ppermute | solution.py:451
  12.5 17.4 %collective-permute-start = (f32[64,16]{1,0:T(8,128)S(1)}, f32[64,16]{1,0:T(8,128)S(1)}, u32[]{:S(2)}, u32[]{:S(2)}) collective-permute-start(f32[64,16]{1,0:T(8,128)S(1)} %copy.15.route_ref), channel_id=1, source_target_pairs={{0,2},{1,3},{2,0},{3,1},{4,6},{5,7},{6,4},{7,5},{8,10},{9,11},{10,... | collective-permute-start | bytes 12296 | tf_op jit(solution)/shard_map/ppermute | solution.py:448
  13.7 2.2 %collective-permute-start.7 = (bf16[4,64,256]{2,1,0:T(8,128)(2,1)S(1)}, bf16[4,64,256]{2,1,0:T(8,128)(2,1)S(1)}, u32[]{:S(2)}, u32[]{:S(2)}) collective-permute-start(bf16[4,64,256]{2,1,0:T(8,128)(2,1)S(1)} %shard_map.110.refs_3_), channel_id=1, source_target_pairs={{0,4},{4,0},{8,12},{12,8},{1,5},{5,1},{9,13},{13,9},{2,6},{6,2},{1... | collective-permute-start | bytes 393224 | tf_op jit(solution)/shard_map/ppermute | solution.py:451
  15.8 1.3 %collective-permute-start.6 = (bf16[4,64,256]{2,1,0:T(8,128)(2,1)S(1)}, bf16[4,64,256]{2,1,0:T(8,128)(2,1)S(1)}, u32[]{:S(2)}, u32[]{:S(2)}) collective-permute-start(bf16[4,64,256]{2,1,0:T(8,128)(2,1)S(1)} %collective-permute-done.5.refs_5_), channel_id=1, source_target_pairs={{0,4},{4,0},{8,12},{12,8},{1,5},{5,1},{9,13},{13,9},{2,6},{6,2},{1... | collective-permute-start | bytes 393224 | tf_op jit(solution)/shard_map/ppermute | solution.py:451
  19.9 8.4 %collective-permute-start.8 = (bf16[128,1024]{1,0:T(8,128)(2,1)S(1)}, bf16[128,1024]{1,0:T(8,128)(2,1)S(1)}, u32[]{:S(2)}, u32[]{:S(2)}) collective-permute-start(bf16[128,1024]{1,0:T(8,128)(2,1)S(1)} %get-tuple-element.51), channel_id=1, source_target_pairs={{0,1},{1,0},{2,3},{3,2},{4,5},{5,4},{6,7},{7,6},{8,9},{9,8},{10,11... | collective-permute-start | bytes 786440 | tf_op jit(solution)/shard_map/ppermute | solution.py:448
  20.0 9.9 %collective-permute-start.15 = (bf16[128,1024]{1,0:T(8,128)(2,1)S(1)}, bf16[128,1024]{1,0:T(8,128)(2,1)S(1)}, u32[]{:S(2)}, u32[]{:S(2)}) collective-permute-start(bf16[128,1024]{1,0:T(8,128)(2,1)S(1)} %get-tuple-element.57), channel_id=1, source_target_pairs={{0,8},{4,12},{8,0},{12,4},{1,9},{5,13},{9,1},{13,5},{2,10},{6,14},... | collective-permute-start | bytes 786440 | tf_op jit(solution)/shard_map/ppermute | solution.py:451
  24.2 10.6 %collective-permute-start.14 = (bf16[128,1024]{1,0:T(8,128)(2,1)S(1)}, bf16[128,1024]{1,0:T(8,128)(2,1)S(1)}, u32[]{:S(2)}, u32[]{:S(2)}) collective-permute-start(bf16[128,1024]{1,0:T(8,128)(2,1)S(1)} %get-tuple-element.56), channel_id=1, source_target_pairs={{0,8},{4,12},{8,0},{12,4},{1,9},{5,13},{9,1},{13,5},{2,10},{6,14},... | collective-permute-start | bytes 786440 | tf_op jit(solution)/shard_map/ppermute | solution.py:451
  24.8 19.8 %collective-permute-start.17 = (bf16[64,1024]{1,0:T(8,128)(2,1)S(1)}, bf16[64,1024]{1,0:T(8,128)(2,1)S(1)}, u32[]{:S(2)}, u32[]{:S(2)}) collective-permute-start(bf16[64,1024]{1,0:T(8,128)(2,1)S(1)} %pad_maximum_fusion), channel_id=1, source_target_pairs={{0,8},{4,12},{8,0},{12,4},{1,9},{5,13},{9,1},{13,5},{2,10},{6,14},... | collective-permute-start | bytes 393224 | tf_op jit(solution)/shard_map/ppermute | solution.py:451
  28.4 14.2 %collective-permute-start.9 = (bf16[128,1024]{1,0:T(8,128)(2,1)S(1)}, bf16[128,1024]{1,0:T(8,128)(2,1)S(1)}, u32[]{:S(2)}, u32[]{:S(2)}) collective-permute-start(bf16[128,1024]{1,0:T(8,128)(2,1)S(1)} %add_convert_fusion.9.sent), channel_id=1, source_target_pairs={{0,2},{1,3},{2,0},{3,1},{4,6},{5,7},{6,4},{7,5},{8,10},{9,11},{10,... | collective-permute-start | bytes 786440 | tf_op jit(solution)/shard_map/ppermute | solution.py:448
  30.4 14.3 %collective-permute-start.16 = (bf16[128,1024]{1,0:T(8,128)(2,1)S(1)}, bf16[128,1024]{1,0:T(8,128)(2,1)S(1)}, u32[]{:S(2)}, u32[]{:S(2)}) collective-permute-start(bf16[128,1024]{1,0:T(8,128)(2,1)S(1)} %shard_map.115), channel_id=1, source_target_pairs={{0,1},{1,0},{2,3},{3,2},{4,5},{5,4},{6,7},{7,6},{8,9},{9,8},{10,11... | collective-permute-start | bytes 786440 | tf_op jit(solution)/shard_map/ppermute | solution.py:448
  42.6 16.8 %copy-start = (bf16[1,2048,768]{2,1,0:T(8,128)(2,1)S(1)}, bf16[1,2048,768]{2,1,0:T(8,128)(2,1)}, u32[]{:S(2)}) copy-start(bf16[1,2048,768]{2,1,0:T(8,128)(2,1)} %refs_2_.11) | copy-start | bytes 9437188
  42.6 16.8 %copy-start.1 = (bf16[1,2048,768]{2,1,0:T(8,128)(2,1)S(1)}, bf16[1,2048,768]{2,1,0:T(8,128)(2,1)}, u32[]{:S(2)}) copy-start(bf16[1,2048,768]{2,1,0:T(8,128)(2,1)} %refs_3_.7) | copy-start | bytes 9437188
  42.6 16.8 %copy-start.2 = (bf16[1,768,2048]{2,1,0:T(8,128)(2,1)S(1)}, bf16[1,768,2048]{2,1,0:T(8,128)(2,1)}, u32[]{:S(2)}) copy-start(bf16[1,768,2048]{2,1,0:T(8,128)(2,1)} %refs_4_.9) | copy-start | bytes 9437188
  43.0 7.6 %collective-permute-start.11 = (bf16[64,1152]{1,0:T(8,128)(2,1)S(1)}, bf16[64,1152]{1,0:T(8,128)(2,1)S(1)}, u32[]{:S(2)}, u32[]{:S(2)}) collective-permute-start(bf16[64,1152]{1,0:T(8,128)(2,1)S(1)} %get-tuple-element.54.refs_0_), channel_id=1, source_target_pairs={{0,1},{1,0},{2,3},{3,2},{4,5},{5,4},{6,7},{7,6},{8,9},{9,8},{10,11... | collective-permute-start | bytes 442376 | tf_op jit(solution)/shard_map/ppermute | solution.py:448
  43.1 8.9 %collective-permute-start.10 = (bf16[128,1152]{1,0:T(8,128)(2,1)S(1)}, bf16[128,1152]{1,0:T(8,128)(2,1)S(1)}, u32[]{:S(2)}, u32[]{:S(2)}) collective-permute-start(bf16[128,1152]{1,0:T(8,128)(2,1)S(1)} %get-tuple-element.53), channel_id=1, source_target_pairs={{0,8},{4,12},{8,0},{12,4},{1,9},{5,13},{9,1},{13,5},{2,10},{6,14},... | collective-permute-start | bytes 884744 | tf_op jit(solution)/shard_map/ppermute | solution.py:451
  44.8 14.6 %collective-permute-start.18 = (bf16[128,1024]{1,0:T(8,128)(2,1)S(1)}, bf16[128,1024]{1,0:T(8,128)(2,1)S(1)}, u32[]{:S(2)}, u32[]{:S(2)}) collective-permute-start(bf16[128,1024]{1,0:T(8,128)(2,1)S(1)} %add_convert_fusion.8.refs_8_), channel_id=1, source_target_pairs={{0,2},{1,3},{2,0},{3,1},{4,6},{5,7},{6,4},{7,5},{8,10},{9,11},{10,... | collective-permute-start | bytes 786440 | tf_op jit(solution)/shard_map/ppermute | solution.py:448
  47.2 9.7 %collective-permute-start.13 = (bf16[64,1152]{1,0:T(8,128)(2,1)S(1)}, bf16[64,1152]{1,0:T(8,128)(2,1)S(1)}, u32[]{:S(2)}, u32[]{:S(2)}) collective-permute-start(bf16[64,1152]{1,0:T(8,128)(2,1)S(1)} %get-tuple-element.52.refs_0_), channel_id=1, source_target_pairs={{0,1},{1,0},{2,3},{3,2},{4,5},{5,4},{6,7},{7,6},{8,9},{9,8},{10,11... | collective-permute-start | bytes 442376 | tf_op jit(solution)/shard_map/ppermute | solution.py:448
  52.0 7.3 %collective-permute-start.12 = (bf16[64,1152]{1,0:T(8,128)(2,1)S(1)}, bf16[64,1152]{1,0:T(8,128)(2,1)S(1)}, u32[]{:S(2)}, u32[]{:S(2)}) collective-permute-start(bf16[64,1152]{1,0:T(8,128)(2,1)S(1)} %collective-permute-done.11.refs_1_.refs_0_), channel_id=1, source_target_pairs={{0,8},{4,12},{8,0},{12,4},{1,9},{5,13},{9,1},{13,5},{2,10},{6,14},... | collective-permute-start | bytes 442376 | tf_op jit(solution)/shard_map/ppermute | solution.py:451
  53.5 18.4 %copy-start.3 = (f32[2048]{0:T(1024)S(1)}, f32[2048]{0:T(1024)}, u32[]{:S(2)}) copy-start(f32[2048]{0:T(1024)} %param.16) | copy-start | bytes 24580
  53.6 8.2 %collective-permute-start.20 = (bf16[64,1152]{1,0:T(8,128)(2,1)S(1)}, bf16[64,1152]{1,0:T(8,128)(2,1)S(1)}, u32[]{:S(2)}, u32[]{:S(2)}) collective-permute-start(bf16[64,1152]{1,0:T(8,128)(2,1)S(1)} %slice.72), channel_id=1, source_target_pairs={{0,1},{1,0},{2,3},{3,2},{4,5},{5,4},{6,7},{7,6},{8,9},{9,8},{10,11... | collective-permute-start | bytes 442376 | tf_op jit(solution)/shard_map/ppermute | solution.py:448
  59.5 7.3 %collective-permute-start.19 = (bf16[128,1024]{1,0:T(8,128)(2,1)S(1)}, bf16[128,1024]{1,0:T(8,128)(2,1)S(1)}, u32[]{:S(2)}, u32[]{:S(2)}) collective-permute-start(bf16[128,1024]{1,0:T(8,128)(2,1)S(1)} %get-tuple-element.61), channel_id=1, source_target_pairs={{0,8},{4,12},{8,0},{12,4},{1,9},{5,13},{9,1},{13,5},{2,10},{6,14},... | collective-permute-start | bytes 786440 | tf_op jit(solution)/shard_map/ppermute | solution.py:451
  61.8 5.0 %collective-permute-start.21 = (bf16[64,1024]{1,0:T(8,128)(2,1)S(1)}, bf16[64,1024]{1,0:T(8,128)(2,1)S(1)}, u32[]{:S(2)}, u32[]{:S(2)}) collective-permute-start(bf16[64,1024]{1,0:T(8,128)(2,1)S(1)} %get-tuple-element.63.refs_1_), channel_id=1, source_target_pairs={{0,1},{1,0},{2,3},{3,2},{4,5},{5,4},{6,7},{7,6},{8,9},{9,8},{10,11... | collective-permute-start | bytes 393224 | tf_op jit(solution)/shard_map/ppermute | solution.py:448
  66.7 5.2 %collective-permute-start.23 = (bf16[64,1024]{1,0:T(8,128)(2,1)S(1)}, bf16[64,1024]{1,0:T(8,128)(2,1)S(1)}, u32[]{:S(2)}, u32[]{:S(2)}) collective-permute-start(bf16[64,1024]{1,0:T(8,128)(2,1)S(1)} %get-tuple-element.65.refs_1_), channel_id=1, source_target_pairs={{0,1},{1,0},{2,3},{3,2},{4,5},{5,4},{6,7},{7,6},{8,9},{9,8},{10,11... | collective-permute-start | bytes 393224 | tf_op jit(solution)/shard_map/ppermute | solution.py:448
  66.7 5.2 %collective-permute-start.22 = (bf16[64,1024]{1,0:T(8,128)(2,1)S(1)}, bf16[64,1024]{1,0:T(8,128)(2,1)S(1)}, u32[]{:S(2)}, u32[]{:S(2)}) collective-permute-start(bf16[64,1024]{1,0:T(8,128)(2,1)S(1)} %collective-permute-done.21.refs_1_), channel_id=1, source_target_pairs={{0,8},{4,12},{8,0},{12,4},{1,9},{5,13},{9,1},{13,5},{2,10},{6,14},... | collective-permute-start | bytes 393224 | tf_op jit(solution)/shard_map/ppermute | solution.py:451
  67.5 5.8 %collective-permute-start.25 = (bf16[64,1024]{1,0:T(8,128)(2,1)S(1)}, bf16[64,1024]{1,0:T(8,128)(2,1)S(1)}, u32[]{:S(2)}, u32[]{:S(2)}) collective-permute-start(bf16[64,1024]{1,0:T(8,128)(2,1)S(1)} %slice.73), channel_id=1, source_target_pairs={{0,1},{1,0},{2,3},{3,2},{4,5},{5,4},{6,7},{7,6},{8,9},{9,8},{10,11... | collective-permute-start | bytes 393224 | tf_op jit(solution)/shard_map/ppermute | solution.py:448
  72.8 2.0 %collective-permute-start.24 = (bf16[128,2176]{1,0:T(8,128)(2,1)S(1)}, bf16[128,2176]{1,0:T(8,128)(2,1)S(1)}, u32[]{:S(2)}, u32[]{:S(2)}) collective-permute-start(bf16[128,2176]{1,0:T(8,128)(2,1)S(1)} %shard_map.117.refs_0_), channel_id=1, source_target_pairs={{0,4},{4,0},{8,12},{12,8},{1,5},{5,1},{9,13},{13,9},{2,6},{6,2},{1... | collective-permute-start | bytes 1671176 | tf_op jit(solution)/shard_map/ppermute | solution.py:451
  78.0 2.4 %collective-permute-start.29 = (bf16[128,2048]{1,0:T(8,128)(2,1)S(1)}, bf16[128,2048]{1,0:T(8,128)(2,1)S(1)}, u32[]{:S(2)}, u32[]{:S(2)}) collective-permute-start(bf16[128,2048]{1,0:T(8,128)(2,1)S(1)} %get-tuple-element.73), channel_id=1, source_target_pairs={{0,4},{4,0},{8,12},{12,8},{1,5},{5,1},{9,13},{13,9},{2,6},{6,2},{1... | collective-permute-start | bytes 1572872 | tf_op jit(solution)/shard_map/ppermute | solution.py:451
  78.2 7.2 %collective-permute-start.27 = (bf16[128,2176]{1,0:T(8,128)(2,1)S(1)}, bf16[128,2176]{1,0:T(8,128)(2,1)S(1)}, u32[]{:S(2)}, u32[]{:S(2)}) collective-permute-start(bf16[128,2176]{1,0:T(8,128)(2,1)S(1)} %shard_map.118.refs_0_), channel_id=1, source_target_pairs={{0,4},{4,0},{8,12},{12,8},{1,5},{5,1},{9,13},{13,9},{2,6},{6,2},{1... | collective-permute-start | bytes 1671176 | tf_op jit(solution)/shard_map/ppermute | solution.py:451
  79.4 2.2 %collective-permute-start.28 = (bf16[128,2176]{1,0:T(8,128)(2,1)S(1)}, bf16[128,2176]{1,0:T(8,128)(2,1)S(1)}, u32[]{:S(2)}, u32[]{:S(2)}) collective-permute-start(bf16[128,2176]{1,0:T(8,128)(2,1)S(1)} %shard_map.121.refs_0_), channel_id=1, source_target_pairs={{0,4},{4,0},{8,12},{12,8},{1,5},{5,1},{9,13},{13,9},{2,6},{6,2},{1... | collective-permute-start | bytes 1671176 | tf_op jit(solution)/shard_map/ppermute | solution.py:451
  80.5 8.6 %collective-permute-start.31 = (bf16[64,2048]{1,0:T(8,128)(2,1)S(1)}, bf16[64,2048]{1,0:T(8,128)(2,1)S(1)}, u32[]{:S(2)}, u32[]{:S(2)}) collective-permute-start(bf16[64,2048]{1,0:T(8,128)(2,1)S(1)} %add_convert_fusion.7), channel_id=1, source_target_pairs={{0,8},{4,12},{8,0},{12,4},{1,9},{5,13},{9,1},{13,5},{2,10},{6,14},... | collective-permute-start | bytes 786440 | tf_op jit(solution)/shard_map/ppermute | solution.py:451
  84.8 6.3 %collective-permute-start.30 = (bf16[128,2048]{1,0:T(8,128)(2,1)S(1)}, bf16[128,2048]{1,0:T(8,128)(2,1)S(1)}, u32[]{:S(2)}, u32[]{:S(2)}) collective-permute-start(bf16[128,2048]{1,0:T(8,128)(2,1)S(1)} %get-tuple-element.81), channel_id=1, source_target_pairs={{0,4},{4,0},{8,12},{12,8},{1,5},{5,1},{9,13},{13,9},{2,6},{6,2},{1... | collective-permute-start | bytes 1572872 | tf_op jit(solution)/shard_map/ppermute | solution.py:451
  85.0 7.0 %collective-permute-start.26 = (bf16[128,2176]{1,0:T(8,128)(2,1)S(1)}, bf16[128,2176]{1,0:T(8,128)(2,1)S(1)}, u32[]{:S(2)}, u32[]{:S(2)}) collective-permute-start(bf16[128,2176]{1,0:T(8,128)(2,1)S(1)} %get-tuple-element.83.refs_0_), channel_id=1, source_target_pairs={{0,4},{4,0},{8,12},{12,8},{1,5},{5,1},{9,13},{13,9},{2,6},{6,2},{1... | collective-permute-start | bytes 1671176 | tf_op jit(solution)/shard_map/ppermute | solution.py:451
  89.2 6.1 %collective-permute-start.34 = (bf16[128,2048]{1,0:T(8,128)(2,1)S(1)}, bf16[128,2048]{1,0:T(8,128)(2,1)S(1)}, u32[]{:S(2)}, u32[]{:S(2)}) collective-permute-start(bf16[128,2048]{1,0:T(8,128)(2,1)S(1)} %get-tuple-element.89), channel_id=1, source_target_pairs={{0,4},{4,0},{8,12},{12,8},{1,5},{5,1},{9,13},{13,9},{2,6},{6,2},{1... | collective-permute-start | bytes 1572872 | tf_op jit(solution)/shard_map/ppermute | solution.py:451
  89.3 11.1 %collective-permute-start.38 = (bf16[64,2048]{1,0:T(8,128)(2,1)S(1)}, bf16[64,2048]{1,0:T(8,128)(2,1)S(1)}, u32[]{:S(2)}, u32[]{:S(2)}) collective-permute-start(bf16[64,2048]{1,0:T(8,128)(2,1)S(1)} %add_convert_fusion.2), channel_id=1, source_target_pairs={{0,1},{1,0},{2,3},{3,2},{4,5},{5,4},{6,7},{7,6},{8,9},{9,8},{10,11... | collective-permute-start | bytes 786440 | tf_op jit(solution)/shard_map/ppermute | solution.py:448
  91.2 9.2 %collective-permute-start.32 = (bf16[64,2048]{1,0:T(8,128)(2,1)S(1)}, bf16[64,2048]{1,0:T(8,128)(2,1)S(1)}, u32[]{:S(2)}, u32[]{:S(2)}) collective-permute-start(bf16[64,2048]{1,0:T(8,128)(2,1)S(1)} %add_convert_fusion.6), channel_id=1, source_target_pairs={{0,8},{4,12},{8,0},{12,4},{1,9},{5,13},{9,1},{13,5},{2,10},{6,14},... | collective-permute-start | bytes 786440 | tf_op jit(solution)/shard_map/ppermute | solution.py:451
  95.4 10.0 %collective-permute-start.36 = (bf16[64,2048]{1,0:T(8,128)(2,1)S(1)}, bf16[64,2048]{1,0:T(8,128)(2,1)S(1)}, u32[]{:S(2)}, u32[]{:S(2)}) collective-permute-start(bf16[64,2048]{1,0:T(8,128)(2,1)S(1)} %add_convert_fusion.4), channel_id=1, source_target_pairs={{0,8},{4,12},{8,0},{12,4},{1,9},{5,13},{9,1},{13,5},{2,10},{6,14},... | collective-permute-start | bytes 786440 | tf_op jit(solution)/shard_map/ppermute | solution.py:451
  100.4 5.4 %collective-permute-start.33 = (bf16[128,2048]{1,0:T(8,128)(2,1)S(1)}, bf16[128,2048]{1,0:T(8,128)(2,1)S(1)}, u32[]{:S(2)}, u32[]{:S(2)}) collective-permute-start(bf16[128,2048]{1,0:T(8,128)(2,1)S(1)} %get-tuple-element.87), channel_id=1, source_target_pairs={{0,4},{4,0},{8,12},{12,8},{1,5},{5,1},{9,13},{13,9},{2,6},{6,2},{1... | collective-permute-start | bytes 1572872 | tf_op jit(solution)/shard_map/ppermute | solution.py:451
  100.5 15.1 %collective-permute-start.39 = (bf16[64,2048]{1,0:T(8,128)(2,1)S(1)}, bf16[64,2048]{1,0:T(8,128)(2,1)S(1)}, u32[]{:S(2)}, u32[]{:S(2)}) collective-permute-start(bf16[64,2048]{1,0:T(8,128)(2,1)S(1)} %add_convert_fusion.1), channel_id=1, source_target_pairs={{0,2},{1,3},{2,0},{3,1},{4,6},{5,7},{6,4},{7,5},{8,10},{9,11},{10,... | collective-permute-start | bytes 786440 | tf_op jit(solution)/shard_map/ppermute | solution.py:448
  105.4 13.2 %collective-permute-start.37 = (bf16[64,2048]{1,0:T(8,128)(2,1)S(1)}, bf16[64,2048]{1,0:T(8,128)(2,1)S(1)}, u32[]{:S(2)}, u32[]{:S(2)}) collective-permute-start(bf16[64,2048]{1,0:T(8,128)(2,1)S(1)} %add_convert_fusion.3), channel_id=1, source_target_pairs={{0,1},{1,0},{2,3},{3,2},{4,5},{5,4},{6,7},{7,6},{8,9},{9,8},{10,11... | collective-permute-start | bytes 786440 | tf_op jit(solution)/shard_map/ppermute | solution.py:448
  105.9 12.8 %collective-permute-start.35 = (bf16[64,2048]{1,0:T(8,128)(2,1)S(1)}, bf16[64,2048]{1,0:T(8,128)(2,1)S(1)}, u32[]{:S(2)}, u32[]{:S(2)}) collective-permute-start(bf16[64,2048]{1,0:T(8,128)(2,1)S(1)} %add_convert_fusion.5), channel_id=1, source_target_pairs={{0,8},{4,12},{8,0},{12,4},{1,9},{5,13},{9,1},{13,5},{2,10},{6,14},... | collective-permute-start | bytes 786440 | tf_op jit(solution)/shard_map/ppermute | solution.py:451
  (2 other events, 2.6 us)

commit v4 on v3

--- a/solution.py
+++ b/solution.py
@@ -695,7 +695,7 @@
     pass_on(last)
     keep[final], send[final] = expert(ready[final], keep[last])
     slots[far_plane] = [added(slots[far_plane]).astype(jnp.bfloat16)]
-    slots[final], leaving[final] = combine(final, *passed[far_plane])
+    slots[final], leaving[final] = combine(final)
     leaving[final] = [after(part, *leaving[last]) for part in leaving[final]]
     pass_on(final)
     keep[0], send[0] = expert(ready[0], keep[final], *leaving[last])

time: 120 us -> 119 us (level)
  waiting for transfers between devices: 59 us -> 57.8 us
where the time goes in v4:
time: 119 us
  waiting for transfers between devices  57.8 us (49%)
  starting transfers between devices  33.6 us (28%)
  Pallas kernels  24.3 us (20%)
  other arithmetic  1.79 us (2%)
    ppermute x17, waiting for transfers between devices, over_role(): return lax.ppermute(array, 'role', [(i, i ^ k) for i in range(role_count)])  40.5 us
    ppermute x17, starting transfers between devices, over_role(): return lax.ppermute(array, 'role', [(i, i ^ k) for i in range(role_count)])  18 us
    ppermute x23, waiting for transfers between devices, over_seq(): return lax.ppermute(array, 'seq', [(i, i ^ j) for i in range(seq_count)])  17.3 us
    ppermute x23, starting transfers between devices, over_seq(): return lax.ppermute(array, 'seq', [(i, i ^ j) for i in range(seq_count)])  15.6 us
    pallas_call x4, Pallas kernels, run_expert(): pl.pallas_call(partial(expert_kernel, len(tokens)), in_specs=[pl.BlockSpe...  13 us
    pallas_call x2, Pallas kernels, gathered_shards(): pl.pallas_call(partial(attend_kernel, seq_count, role_count, slots, parts...  5.35 us
    pallas_call x4, Pallas kernels, normed_rows(): pl.pallas_call(partial(norm_kernel, chips, *firsts), in_specs=[pl.BlockSp...  3.26 us
  transfers between devices with their start and end apart: 40, of which 21 were waited for; matrix products, arithmetic and copies ran while one was open for 2% of the time, Pallas kernels for 18%

profile of v4, /device:TPU:0, one launch (start us, length us, event | category | flops | bytes accessed | tf_op | source)
XLA Modules:
  0.0 118.9 jit_solution(15268137458211070437)
XLA Ops:
  0.5 0.8 constant_dynamic-slice_fusion
  1.3 3.7 %collective-permute-start.3 = (bf16[4,16,256]{2,1,0:T(8,128)(2,1)S(1)}, bf16[4,16,256]{2,1,0:T(8,128)(2,1)S(1)}, u32[]{:S(2)}, u32[]{:S(2)}) collective-permute-start(bf16[4,16,256]{2,1,0:T(8,128)(2,1)S(1)} %pad_maximum_fusion.3), channel_id=1, source_target_pairs={{0,2},{1,3},{2,0},{3,1},{4,6},{5,7},{6,4},{7,5},{8,10},{9,11},{10,... | collective-permute-start | bytes 98312 | tf_op jit(solution)/shard_map/ppermute | solution.py:448
  5.0 1.3 %collective-permute-start.4 = (bf16[4,16,256]{2,1,0:T(8,128)(2,1)S(1)}, bf16[4,16,256]{2,1,0:T(8,128)(2,1)S(1)}, u32[]{:S(2)}, u32[]{:S(2)}) collective-permute-start(bf16[4,16,256]{2,1,0:T(8,128)(2,1)S(1)} %pad_maximum_fusion.4), channel_id=1, source_target_pairs={{0,3},{1,2},{2,1},{3,0},{4,7},{5,6},{6,5},{7,4},{8,11},{9,10},{10,... | collective-permute-start | bytes 98312 | tf_op jit(solution)/shard_map/ppermute | solution.py:448
  6.7 1.2 %shard_map.109.refs_4_.refs_1_.proj_ref = bf16[1024,1024]{1,0:T(8,128)(2,1)S(1)} custom-call(bf16[1024,512]{1,0:T(8,128)(2,1)} %refs_0_.1, bf16[1024,512]{1,0:T(8,128)(2,1)S(1)} %collective-permute-done.1.refs_1_), custom_call_target="tpu_custom_call" | custom-call | flops 1 | bytes 1 | tf_op jit(solution)/shard_map/pallas_call | solution.py:468
  8.0 2.8 %collective-permute-done.4.refs_3_ = bf16[4,16,256]{2,1,0:T(8,128)(2,1)S(1)} collective-permute-done((bf16[4,16,256]{2,1,0:T(8,128)(2,1)S(1)}, bf16[4,16,256]{2,1,0:T(8,128)(2,1)S(1)}, u32[]{:S(2)}, u32[]{:S(2)}) %collective-permute-start.4) | collective-permute-done | bytes 32800 | tf_op jit(solution)/shard_map/ppermute | solution.py:448
  10.8 1.6 %collective-permute-start.5 = (bf16[4,64,256]{2,1,0:T(8,128)(2,1)S(1)}, bf16[4,64,256]{2,1,0:T(8,128)(2,1)S(1)}, u32[]{:S(2)}, u32[]{:S(2)}) collective-permute-start(bf16[4,64,256]{2,1,0:T(8,128)(2,1)S(1)} %shard_map.110.refs_3_), channel_id=1, source_target_pairs={{0,8},{4,12},{8,0},{12,4},{1,9},{5,13},{9,1},{13,5},{2,10},{6,14},... | collective-permute-start | bytes 393224 | tf_op jit(solution)/shard_map/ppermute | solution.py:451
  12.5 1.3 %collective-permute-start = (f32[64,16]{1,0:T(8,128)S(1)}, f32[64,16]{1,0:T(8,128)S(1)}, u32[]{:S(2)}, u32[]{:S(2)}) collective-permute-start(f32[64,16]{1,0:T(8,128)S(1)} %copy.15.route_ref), channel_id=1, source_target_pairs={{0,2},{1,3},{2,0},{3,1},{4,6},{5,7},{6,4},{7,5},{8,10},{9,11},{10,... | collective-permute-start | bytes 12296 | tf_op jit(solution)/shard_map/ppermute | solution.py:448
  13.7 2.1 %collective-permute-done.5.refs_5_ = bf16[4,64,256]{2,1,0:T(8,128)(2,1)S(1)} collective-permute-done((bf16[4,64,256]{2,1,0:T(8,128)(2,1)S(1)}, bf16[4,64,256]{2,1,0:T(8,128)(2,1)S(1)}, u32[]{:S(2)}, u32[]{:S(2)}) %collective-permute-start.5) | collective-permute-done | bytes 131104 | tf_op jit(solution)/shard_map/ppermute | solution.py:451
  16.0 1.2 %collective-permute-done.6.refs_0_ = bf16[4,64,256]{2,1,0:T(8,128)(2,1)S(1)} collective-permute-done((bf16[4,64,256]{2,1,0:T(8,128)(2,1)S(1)}, bf16[4,64,256]{2,1,0:T(8,128)(2,1)S(1)}, u32[]{:S(2)}, u32[]{:S(2)}) %collective-permute-start.6) | collective-permute-done | bytes 131104 | tf_op jit(solution)/shard_map/ppermute | solution.py:451
  17.2 2.7 %shard_map.112 = (bf16[128,1024]{1,0:T(8,128)(2,1)S(1)}, bf16[128,1024]{1,0:T(8,128)(2,1)S(1)}) custom-call(s32[3]{0:T(128)S(1)} %pad_add_fusion.at_ref, bf16[4,64,256]{2,1,0:T(8,128)(2,1)S(1)} %collective-permute-done.6.refs_0_, bf16[1024,1024]{1,0:T(8,128)(2,1)S(1)} %shard_map.109.refs_4_.refs_1_.proj_ref, bf16[4,64,1024]{2,1,0:T(8,128)(2,1)} %refs_2_.7, ...), custom_call_target="tpu_custom_call" | custom-call | flops 2000000000 | bytes 4194304 | tf_op jit(solution)/shard_map/pallas_call | solution.py:511
  20.0 1.6 %collective-permute-start.15 = (bf16[128,1024]{1,0:T(8,128)(2,1)S(1)}, bf16[128,1024]{1,0:T(8,128)(2,1)S(1)}, u32[]{:S(2)}, u32[]{:S(2)}) collective-permute-start(bf16[128,1024]{1,0:T(8,128)(2,1)S(1)} %get-tuple-element.56), channel_id=1, source_target_pairs={{0,8},{4,12},{8,0},{12,4},{1,9},{5,13},{9,1},{13,5},{2,10},{6,14},... | collective-permute-start | bytes 786440 | tf_op jit(solution)/shard_map/ppermute | solution.py:451
  21.6 2.7 %shard_map.111 = (bf16[128,1024]{1,0:T(8,128)(2,1)S(1)}, bf16[128,1024]{1,0:T(8,128)(2,1)S(1)}) custom-call(s32[3]{0:T(128)S(1)} %pad_add_fusion.at_ref, bf16[4,64,256]{2,1,0:T(8,128)(2,1)S(1)} %collective-permute-done.6.refs_0_, bf16[1024,1024]{1,0:T(8,128)(2,1)S(1)} %shard_map.109.refs_4_.refs_1_.proj_ref, bf16[4,64,1024]{2,1,0:T(8,128)(2,1)} %refs_2_.7, ...), custom_call_target="tpu_custom_call" | custom-call | flops 2000000000 | bytes 4194304 | tf_op jit(solution)/shard_map/pallas_call | solution.py:511
  24.8 1.5 %collective-permute-start.17 = (bf16[64,1024]{1,0:T(8,128)(2,1)S(1)}, bf16[64,1024]{1,0:T(8,128)(2,1)S(1)}, u32[]{:S(2)}, u32[]{:S(2)}) collective-permute-start(bf16[64,1024]{1,0:T(8,128)(2,1)S(1)} %pad_maximum_fusion), channel_id=1, source_target_pairs={{0,8},{4,12},{8,0},{12,4},{1,9},{5,13},{9,1},{13,5},{2,10},{6,14},... | collective-permute-start | bytes 393224 | tf_op jit(solution)/shard_map/ppermute | solution.py:451
  26.3 2.0 %collective-permute-done.8 = bf16[128,1024]{1,0:T(8,128)(2,1)S(1)} collective-permute-done((bf16[128,1024]{1,0:T(8,128)(2,1)S(1)}, bf16[128,1024]{1,0:T(8,128)(2,1)S(1)}, u32[]{:S(2)}, u32[]{:S(2)}) %collective-permute-start.8) | collective-permute-done | bytes 262176 | tf_op jit(solution)/shard_map/ppermute | solution.py:448
  28.4 1.5 %collective-permute-start.9 = (bf16[128,1024]{1,0:T(8,128)(2,1)S(1)}, bf16[128,1024]{1,0:T(8,128)(2,1)S(1)}, u32[]{:S(2)}, u32[]{:S(2)}) collective-permute-start(bf16[128,1024]{1,0:T(8,128)(2,1)S(1)} %add_convert_fusion.9.sent), channel_id=1, source_target_pairs={{0,2},{1,3},{2,0},{3,1},{4,6},{5,7},{6,4},{7,5},{8,10},{9,11},{10,... | collective-permute-start | bytes 786440 | tf_op jit(solution)/shard_map/ppermute | solution.py:448
  30.4 1.4 %collective-permute-start.16 = (bf16[128,1024]{1,0:T(8,128)(2,1)S(1)}, bf16[128,1024]{1,0:T(8,128)(2,1)S(1)}, u32[]{:S(2)}, u32[]{:S(2)}) collective-permute-start(bf16[128,1024]{1,0:T(8,128)(2,1)S(1)} %shard_map.115), channel_id=1, source_target_pairs={{0,1},{1,0},{2,3},{3,2},{4,5},{5,4},{6,7},{7,6},{8,9},{9,8},{10,11... | collective-permute-start | bytes 786440 | tf_op jit(solution)/shard_map/ppermute | solution.py:448
  31.8 3.1 %collective-permute-done.14.attended_ref = bf16[128,1024]{1,0:T(8,128)(2,1)S(1)} collective-permute-done((bf16[128,1024]{1,0:T(8,128)(2,1)S(1)}, bf16[128,1024]{1,0:T(8,128)(2,1)S(1)}, u32[]{:S(2)}, u32[]{:S(2)}) %collective-permute-start.14) | collective-permute-done | bytes 262176 | tf_op jit(solution)/shard_map/ppermute | solution.py:451
  35.3 7.3 %collective-permute-done.9.came_ref = bf16[128,1024]{1,0:T(8,128)(2,1)S(1)} collective-permute-done((bf16[128,1024]{1,0:T(8,128)(2,1)S(1)}, bf16[128,1024]{1,0:T(8,128)(2,1)S(1)}, u32[]{:S(2)}, u32[]{:S(2)}) %collective-permute-start.9) | collective-permute-done | bytes 262176 | tf_op jit(solution)/shard_map/ppermute | solution.py:448
  43.1 1.6 %collective-permute-start.10 = (bf16[128,1152]{1,0:T(8,128)(2,1)S(1)}, bf16[128,1152]{1,0:T(8,128)(2,1)S(1)}, u32[]{:S(2)}, u32[]{:S(2)}) collective-permute-start(bf16[128,1152]{1,0:T(8,128)(2,1)S(1)} %get-tuple-element.52), channel_id=1, source_target_pairs={{0,8},{4,12},{8,0},{12,4},{1,9},{5,13},{9,1},{13,5},{2,10},{6,14},... | collective-permute-start | bytes 884744 | tf_op jit(solution)/shard_map/ppermute | solution.py:451
  44.8 2.5 %collective-permute-start.18 = (bf16[128,1024]{1,0:T(8,128)(2,1)S(1)}, bf16[128,1024]{1,0:T(8,128)(2,1)S(1)}, u32[]{:S(2)}, u32[]{:S(2)}) collective-permute-start(bf16[128,1024]{1,0:T(8,128)(2,1)S(1)} %add_convert_fusion.8.refs_8_), channel_id=1, source_target_pairs={{0,2},{1,3},{2,0},{3,1},{4,6},{5,7},{6,4},{7,5},{8,10},{9,11},{10,... | collective-permute-start | bytes 786440 | tf_op jit(solution)/shard_map/ppermute | solution.py:448
  47.3 3.3 %collective-permute-done.11.refs_1_.refs_0_ = bf16[64,1152]{1,0:T(8,128)(2,1)S(1)} collective-permute-done((bf16[64,1152]{1,0:T(8,128)(2,1)S(1)}, bf16[64,1152]{1,0:T(8,128)(2,1)S(1)}, u32[]{:S(2)}, u32[]{:S(2)}) %collective-permute-start.11) | collective-permute-done | bytes 147488 | tf_op jit(solution)/shard_map/ppermute | solution.py:448
  50.6 1.4 %collective-permute-done.10.refs_0_.refs_2_ = bf16[128,1152]{1,0:T(8,128)(2,1)S(1)} collective-permute-done((bf16[128,1152]{1,0:T(8,128)(2,1)S(1)}, bf16[128,1152]{1,0:T(8,128)(2,1)S(1)}, u32[]{:S(2)}, u32[]{:S(2)}) %collective-permute-start.10) | collective-permute-done | bytes 294944 | tf_op jit(solution)/shard_map/ppermute | solution.py:451
  52.0 1.5 %collective-permute-start.12 = (bf16[64,1152]{1,0:T(8,128)(2,1)S(1)}, bf16[64,1152]{1,0:T(8,128)(2,1)S(1)}, u32[]{:S(2)}, u32[]{:S(2)}) collective-permute-start(bf16[64,1152]{1,0:T(8,128)(2,1)S(1)} %collective-permute-done.11.refs_1_.refs_0_), channel_id=1, source_target_pairs={{0,8},{4,12},{8,0},{12,4},{1,9},{5,13},{9,1},{13,5},{2,10},{6,14},... | collective-permute-start | bytes 442376 | tf_op jit(solution)/shard_map/ppermute | solution.py:451
  53.6 1.7 %collective-permute-start.20 = (bf16[64,1152]{1,0:T(8,128)(2,1)S(1)}, bf16[64,1152]{1,0:T(8,128)(2,1)S(1)}, u32[]{:S(2)}, u32[]{:S(2)}) collective-permute-start(bf16[64,1152]{1,0:T(8,128)(2,1)S(1)} %slice.72), channel_id=1, source_target_pairs={{0,1},{1,0},{2,3},{3,2},{4,5},{5,4},{6,7},{7,6},{8,9},{9,8},{10,11... | collective-permute-start | bytes 442376 | tf_op jit(solution)/shard_map/ppermute | solution.py:448
  55.3 1.6 %collective-permute-done.13.refs_3_.refs_0_ = bf16[64,1152]{1,0:T(8,128)(2,1)S(1)} collective-permute-done((bf16[64,1152]{1,0:T(8,128)(2,1)S(1)}, bf16[64,1152]{1,0:T(8,128)(2,1)S(1)}, u32[]{:S(2)}, u32[]{:S(2)}) %collective-permute-start.13) | collective-permute-done | bytes 147488 | tf_op jit(solution)/shard_map/ppermute | solution.py:448
  56.9 2.5 %collective-permute-done.18.refs_7_ = bf16[128,1024]{1,0:T(8,128)(2,1)S(1)} collective-permute-done((bf16[128,1024]{1,0:T(8,128)(2,1)S(1)}, bf16[128,1024]{1,0:T(8,128)(2,1)S(1)}, u32[]{:S(2)}, u32[]{:S(2)}) %collective-permute-start.18) | collective-permute-done | bytes 262176 | tf_op jit(solution)/shard_map/ppermute | solution.py:448
  60.1 1.7 %collective-permute-done.20.refs_2_ = bf16[64,1152]{1,0:T(8,128)(2,1)S(1)} collective-permute-done((bf16[64,1152]{1,0:T(8,128)(2,1)S(1)}, bf16[64,1152]{1,0:T(8,128)(2,1)S(1)}, u32[]{:S(2)}, u32[]{:S(2)}) %collective-permute-start.20) | collective-permute-done | bytes 147488 | tf_op jit(solution)/shard_map/ppermute | solution.py:448
  61.8 5.0 %collective-permute-done.21.refs_1_ = bf16[64,1024]{1,0:T(8,128)(2,1)S(1)} collective-permute-done((bf16[64,1024]{1,0:T(8,128)(2,1)S(1)}, bf16[64,1024]{1,0:T(8,128)(2,1)S(1)}, u32[]{:S(2)}, u32[]{:S(2)}) %collective-permute-start.21) | collective-permute-done | bytes 131104 | tf_op jit(solution)/shard_map/ppermute | solution.py:448
  66.7 0.8 collective-permute-start.22
  67.5 1.8 %collective-permute-start.25 = (bf16[64,1024]{1,0:T(8,128)(2,1)S(1)}, bf16[64,1024]{1,0:T(8,128)(2,1)S(1)}, u32[]{:S(2)}, u32[]{:S(2)}) collective-permute-start(bf16[64,1024]{1,0:T(8,128)(2,1)S(1)} %slice.73), channel_id=1, source_target_pairs={{0,1},{1,0},{2,3},{3,2},{4,5},{5,4},{6,7},{7,6},{8,9},{9,8},{10,11... | collective-permute-start | bytes 393224 | tf_op jit(solution)/shard_map/ppermute | solution.py:448
  69.4 2.6 %collective-permute-done.23.refs_1_ = bf16[64,1024]{1,0:T(8,128)(2,1)S(1)} collective-permute-done((bf16[64,1024]{1,0:T(8,128)(2,1)S(1)}, bf16[64,1024]{1,0:T(8,128)(2,1)S(1)}, u32[]{:S(2)}, u32[]{:S(2)}) %collective-permute-start.23) | collective-permute-done | bytes 131104 | tf_op jit(solution)/shard_map/ppermute | solution.py:448
  72.0 0.8 shard_map.117.refs_0_
  73.4 0.8 shard_map.118.refs_0_
  74.8 3.2 %shard_map.119 = (bf16[128,2048]{1,0:T(8,128)(2,1)S(1)}, bf16[128,2048]{1,0:T(8,128)(2,1)S(1)}) custom-call(s32[3]{0:T(128)S(1)} %pad_add_fusion.at_ref, bf16[128,2176]{1,0:T(8,128)(2,1)S(1)} %shard_map.117.refs_0_, bf16[128,2176]{1,0:T(8,128)(2,1)S(1)} %collective-permute-done.24.refs_1_, bf16[1,2048,768]{2,1,0:T(8,128)(2,1)S(1)} %copy-done, ...), custom_call_target="tpu_custom_call" | custom-call | flops 1 | bytes 1 | tf_op jit(solution)/shard_map/pallas_call | solution.py:402
  78.6 0.8 shard_map.121.refs_0_
  79.6 0.8 shard_map.120
  81.6 3.2 %shard_map.122 = (bf16[128,2048]{1,0:T(8,128)(2,1)S(1)}, bf16[128,2048]{1,0:T(8,128)(2,1)S(1)}) custom-call(s32[3]{0:T(128)S(1)} %pad_add_fusion.at_ref, bf16[128,2176]{1,0:T(8,128)(2,1)S(1)} %shard_map.121.refs_0_, bf16[128,2176]{1,0:T(8,128)(2,1)S(1)} %collective-permute-done.28.refs_1_, bf16[1,2048,768]{2,1,0:T(8,128)(2,1)S(1)} %copy-done, ...), custom_call_target="tpu_custom_call" | custom-call | flops 1 | bytes 1 | tf_op jit(solution)/shard_map/pallas_call | solution.py:402
  85.4 3.4 %shard_map.123 = (bf16[128,2048]{1,0:T(8,128)(2,1)S(1)}, bf16[128,2048]{1,0:T(8,128)(2,1)S(1)}) custom-call(s32[3]{0:T(128)S(1)} %pad_add_fusion.at_ref, bf16[128,2176]{1,0:T(8,128)(2,1)S(1)} %shard_map.118.refs_0_, bf16[128,2176]{1,0:T(8,128)(2,1)S(1)} %collective-permute-done.27.refs_1_, bf16[1,2048,768]{2,1,0:T(8,128)(2,1)S(1)} %copy-done, ...), custom_call_target="tpu_custom_call" | custom-call | flops 1 | bytes 1 | tf_op jit(solution)/shard_map/pallas_call | solution.py:402
  89.3 1.8 %collective-permute-start.38 = (bf16[64,2048]{1,0:T(8,128)(2,1)S(1)}, bf16[64,2048]{1,0:T(8,128)(2,1)S(1)}, u32[]{:S(2)}, u32[]{:S(2)}) collective-permute-start(bf16[64,2048]{1,0:T(8,128)(2,1)S(1)} %add_convert_fusion.2), channel_id=1, source_target_pairs={{0,1},{1,0},{2,3},{3,2},{4,5},{5,4},{6,7},{7,6},{8,9},{9,8},{10,11... | collective-permute-start | bytes 786440 | tf_op jit(solution)/shard_map/ppermute | solution.py:448
  91.2 0.9 collective-permute-start.32
  92.1 1.3 %collective-permute-start.36 = (bf16[64,2048]{1,0:T(8,128)(2,1)S(1)}, bf16[64,2048]{1,0:T(8,128)(2,1)S(1)}, u32[]{:S(2)}, u32[]{:S(2)}) collective-permute-start(bf16[64,2048]{1,0:T(8,128)(2,1)S(1)} %add_convert_fusion.4), channel_id=1, source_target_pairs={{0,8},{4,12},{8,0},{12,4},{1,9},{5,13},{9,1},{13,5},{2,10},{6,14},... | collective-permute-start | bytes 786440 | tf_op jit(solution)/shard_map/ppermute | solution.py:451
  93.4 3.2 %shard_map.124 = (bf16[128,2048]{1,0:T(8,128)(2,1)S(1)}, bf16[128,2048]{1,0:T(8,128)(2,1)S(1)}) custom-call(s32[3]{0:T(128)S(1)} %pad_add_fusion.at_ref, bf16[128,2176]{1,0:T(8,128)(2,1)S(1)} %get-tuple-element.82.refs_0_, bf16[128,2176]{1,0:T(8,128)(2,1)S(1)} %collective-permute-done.26.refs_1_, bf16[1,2048,768]{2,1,0:T(8,128)(2,1)S(1)} %copy-done, ...), custom_call_target="tpu_custom_call" | custom-call | flops 1 | bytes 1 | tf_op jit(solution)/shard_map/pallas_call | solution.py:402
  96.6 3.8 %collective-permute-done.32 = bf16[64,2048]{1,0:T(8,128)(2,1)S(1)} collective-permute-done((bf16[64,2048]{1,0:T(8,128)(2,1)S(1)}, bf16[64,2048]{1,0:T(8,128)(2,1)S(1)}, u32[]{:S(2)}, u32[]{:S(2)}) %collective-permute-start.32) | collective-permute-done | bytes 262176 | tf_op jit(solution)/shard_map/ppermute | solution.py:451
  100.7 4.3 %collective-permute-done.36 = bf16[64,2048]{1,0:T(8,128)(2,1)S(1)} collective-permute-done((bf16[64,2048]{1,0:T(8,128)(2,1)S(1)}, bf16[64,2048]{1,0:T(8,128)(2,1)S(1)}, u32[]{:S(2)}, u32[]{:S(2)}) %collective-permute-start.36) | collective-permute-done | bytes 262176 | tf_op jit(solution)/shard_map/ppermute | solution.py:451
  105.5 1.1 collective-permute-start.35
  106.6 9.1 %collective-permute-done.39 = bf16[64,2048]{1,0:T(8,128)(2,1)S(1)} collective-permute-done((bf16[64,2048]{1,0:T(8,128)(2,1)S(1)}, bf16[64,2048]{1,0:T(8,128)(2,1)S(1)}, u32[]{:S(2)}, u32[]{:S(2)}) %collective-permute-start.39) | collective-permute-done | bytes 262176 | tf_op jit(solution)/shard_map/ppermute | solution.py:448
  115.7 2.3 %collective-permute-done.37 = bf16[64,2048]{1,0:T(8,128)(2,1)S(1)} collective-permute-done((bf16[64,2048]{1,0:T(8,128)(2,1)S(1)}, bf16[64,2048]{1,0:T(8,128)(2,1)S(1)}, u32[]{:S(2)}, u32[]{:S(2)}) %collective-permute-start.37) | collective-permute-done | bytes 262176 | tf_op jit(solution)/shard_map/ppermute | solution.py:448
  118.0 0.9 fusion.2
  (91 shorter events, 9.2 us)
Async XLA Ops:
  0.0 6.3 %collective-permute-start.1 = (bf16[1024,512]{1,0:T(8,128)(2,1)}, bf16[1024,512]{1,0:T(8,128)(2,1)S(1)}, u32[]{:S(2)}, u32[]{:S(2)}) collective-permute-start(bf16[1024,512]{1,0:T(8,128)(2,1)} %refs_0_.1), channel_id=1, source_target_pairs={{0,4},{4,0},{8,12},{12,8},{1,5},{5,1},{9,13},{13,9},{2,6},{6,2},{1... | collective-permute-start | bytes 3145736 | tf_op jit(solution)/shard_map/ppermute | solution.py:451
  1.3 6.6 %collective-permute-start.3 = (bf16[4,16,256]{2,1,0:T(8,128)(2,1)S(1)}, bf16[4,16,256]{2,1,0:T(8,128)(2,1)S(1)}, u32[]{:S(2)}, u32[]{:S(2)}) collective-permute-start(bf16[4,16,256]{2,1,0:T(8,128)(2,1)S(1)} %pad_maximum_fusion.3), channel_id=1, source_target_pairs={{0,2},{1,3},{2,0},{3,1},{4,6},{5,7},{6,4},{7,5},{8,10},{9,11},{10,... | collective-permute-start | bytes 98312 | tf_op jit(solution)/shard_map/ppermute | solution.py:448
  5.0 5.8 %collective-permute-start.4 = (bf16[4,16,256]{2,1,0:T(8,128)(2,1)S(1)}, bf16[4,16,256]{2,1,0:T(8,128)(2,1)S(1)}, u32[]{:S(2)}, u32[]{:S(2)}) collective-permute-start(bf16[4,16,256]{2,1,0:T(8,128)(2,1)S(1)} %pad_maximum_fusion.4), channel_id=1, source_target_pairs={{0,3},{1,2},{2,1},{3,0},{4,7},{5,6},{6,5},{7,4},{8,11},{9,10},{10,... | collective-permute-start | bytes 98312 | tf_op jit(solution)/shard_map/ppermute | solution.py:448
  6.3 4.4 %collective-permute-start.2 = (bf16[4,16,256]{2,1,0:T(8,128)(2,1)S(1)}, bf16[4,16,256]{2,1,0:T(8,128)(2,1)S(1)}, u32[]{:S(2)}, u32[]{:S(2)}) collective-permute-start(bf16[4,16,256]{2,1,0:T(8,128)(2,1)S(1)} %pad_maximum_fusion.2), channel_id=1, source_target_pairs={{0,1},{1,0},{2,3},{3,2},{4,5},{5,4},{6,7},{7,6},{8,9},{9,8},{10,11... | collective-permute-start | bytes 98312 | tf_op jit(solution)/shard_map/ppermute | solution.py:448
  7.9 4.5 %copy-start.6 = (s32[1,64,8]{1,2,0:T(8,128)S(1)}, s32[1,64,8]{1,2,0:T(8,128)}, u32[]{:S(2)}) copy-start(s32[1,64,8]{1,2,0:T(8,128)} %param.17) | copy-start | bytes 6148
  7.9 4.4 %copy-start.7 = (f32[1,64,8]{1,2,0:T(8,128)S(1)}, f32[1,64,8]{1,2,0:T(8,128)}, u32[]{:S(2)}) copy-start(f32[1,64,8]{1,2,0:T(8,128)} %param.18) | copy-start | bytes 6148
  7.9 8.0 %copy-start.5 = (bf16[1,64,2048]{2,1,0:T(8,128)(2,1)S(1)}, bf16[1,64,2048]{2,1,0:T(8,128)(2,1)}, u32[]{:S(2)}) copy-start(bf16[1,64,2048]{2,1,0:T(8,128)(2,1)} %param.15) | copy-start | bytes 786436
  10.8 6.4 %copy-start.4 = (bf16[4,64,256]{2,1,0:T(8,128)(2,1)}, bf16[4,64,256]{2,1,0:T(8,128)(2,1)S(1)}, u32[]{:S(2)}) copy-start(bf16[4,64,256]{2,1,0:T(8,128)(2,1)S(1)} %shard_map.110.refs_3_) | copy-start | bytes 393220
  10.8 5.0 %collective-permute-start.5 = (bf16[4,64,256]{2,1,0:T(8,128)(2,1)S(1)}, bf16[4,64,256]{2,1,0:T(8,128)(2,1)S(1)}, u32[]{:S(2)}, u32[]{:S(2)}) collective-permute-start(bf16[4,64,256]{2,1,0:T(8,128)(2,1)S(1)} %shard_map.110.refs_3_), channel_id=1, source_target_pairs={{0,8},{4,12},{8,0},{12,4},{1,9},{5,13},{9,1},{13,5},{2,10},{6,14},... | collective-permute-start | bytes 393224 | tf_op jit(solution)/shard_map/ppermute | solution.py:451
  12.5 17.4 %collective-permute-start = (f32[64,16]{1,0:T(8,128)S(1)}, f32[64,16]{1,0:T(8,128)S(1)}, u32[]{:S(2)}, u32[]{:S(2)}) collective-permute-start(f32[64,16]{1,0:T(8,128)S(1)} %copy.15.route_ref), channel_id=1, source_target_pairs={{0,2},{1,3},{2,0},{3,1},{4,6},{5,7},{6,4},{7,5},{8,10},{9,11},{10,... | collective-permute-start | bytes 12296 | tf_op jit(solution)/shard_map/ppermute | solution.py:448
  13.7 2.2 %collective-permute-start.7 = (bf16[4,64,256]{2,1,0:T(8,128)(2,1)S(1)}, bf16[4,64,256]{2,1,0:T(8,128)(2,1)S(1)}, u32[]{:S(2)}, u32[]{:S(2)}) collective-permute-start(bf16[4,64,256]{2,1,0:T(8,128)(2,1)S(1)} %shard_map.110.refs_3_), channel_id=1, source_target_pairs={{0,4},{4,0},{8,12},{12,8},{1,5},{5,1},{9,13},{13,9},{2,6},{6,2},{1... | collective-permute-start | bytes 393224 | tf_op jit(solution)/shard_map/ppermute | solution.py:451
  15.8 1.3 %collective-permute-start.6 = (bf16[4,64,256]{2,1,0:T(8,128)(2,1)S(1)}, bf16[4,64,256]{2,1,0:T(8,128)(2,1)S(1)}, u32[]{:S(2)}, u32[]{:S(2)}) collective-permute-start(bf16[4,64,256]{2,1,0:T(8,128)(2,1)S(1)} %collective-permute-done.5.refs_5_), channel_id=1, source_target_pairs={{0,4},{4,0},{8,12},{12,8},{1,5},{5,1},{9,13},{13,9},{2,6},{6,2},{1... | collective-permute-start | bytes 393224 | tf_op jit(solution)/shard_map/ppermute | solution.py:451
  19.9 8.4 %collective-permute-start.8 = (bf16[128,1024]{1,0:T(8,128)(2,1)S(1)}, bf16[128,1024]{1,0:T(8,128)(2,1)S(1)}, u32[]{:S(2)}, u32[]{:S(2)}) collective-permute-start(bf16[128,1024]{1,0:T(8,128)(2,1)S(1)} %get-tuple-element.50), channel_id=1, source_target_pairs={{0,1},{1,0},{2,3},{3,2},{4,5},{5,4},{6,7},{7,6},{8,9},{9,8},{10,11... | collective-permute-start | bytes 786440 | tf_op jit(solution)/shard_map/ppermute | solution.py:448
  20.0 9.9 %collective-permute-start.15 = (bf16[128,1024]{1,0:T(8,128)(2,1)S(1)}, bf16[128,1024]{1,0:T(8,128)(2,1)S(1)}, u32[]{:S(2)}, u32[]{:S(2)}) collective-permute-start(bf16[128,1024]{1,0:T(8,128)(2,1)S(1)} %get-tuple-element.56), channel_id=1, source_target_pairs={{0,8},{4,12},{8,0},{12,4},{1,9},{5,13},{9,1},{13,5},{2,10},{6,14},... | collective-permute-start | bytes 786440 | tf_op jit(solution)/shard_map/ppermute | solution.py:451
  24.2 10.6 %collective-permute-start.14 = (bf16[128,1024]{1,0:T(8,128)(2,1)S(1)}, bf16[128,1024]{1,0:T(8,128)(2,1)S(1)}, u32[]{:S(2)}, u32[]{:S(2)}) collective-permute-start(bf16[128,1024]{1,0:T(8,128)(2,1)S(1)} %get-tuple-element.55), channel_id=1, source_target_pairs={{0,8},{4,12},{8,0},{12,4},{1,9},{5,13},{9,1},{13,5},{2,10},{6,14},... | collective-permute-start | bytes 786440 | tf_op jit(solution)/shard_map/ppermute | solution.py:451
  24.8 19.8 %collective-permute-start.17 = (bf16[64,1024]{1,0:T(8,128)(2,1)S(1)}, bf16[64,1024]{1,0:T(8,128)(2,1)S(1)}, u32[]{:S(2)}, u32[]{:S(2)}) collective-permute-start(bf16[64,1024]{1,0:T(8,128)(2,1)S(1)} %pad_maximum_fusion), channel_id=1, source_target_pairs={{0,8},{4,12},{8,0},{12,4},{1,9},{5,13},{9,1},{13,5},{2,10},{6,14},... | collective-permute-start | bytes 393224 | tf_op jit(solution)/shard_map/ppermute | solution.py:451
  28.4 14.2 %collective-permute-start.9 = (bf16[128,1024]{1,0:T(8,128)(2,1)S(1)}, bf16[128,1024]{1,0:T(8,128)(2,1)S(1)}, u32[]{:S(2)}, u32[]{:S(2)}) collective-permute-start(bf16[128,1024]{1,0:T(8,128)(2,1)S(1)} %add_convert_fusion.9.sent), channel_id=1, source_target_pairs={{0,2},{1,3},{2,0},{3,1},{4,6},{5,7},{6,4},{7,5},{8,10},{9,11},{10,... | collective-permute-start | bytes 786440 | tf_op jit(solution)/shard_map/ppermute | solution.py:448
  30.4 14.3 %collective-permute-start.16 = (bf16[128,1024]{1,0:T(8,128)(2,1)S(1)}, bf16[128,1024]{1,0:T(8,128)(2,1)S(1)}, u32[]{:S(2)}, u32[]{:S(2)}) collective-permute-start(bf16[128,1024]{1,0:T(8,128)(2,1)S(1)} %shard_map.115), channel_id=1, source_target_pairs={{0,1},{1,0},{2,3},{3,2},{4,5},{5,4},{6,7},{7,6},{8,9},{9,8},{10,11... | collective-permute-start | bytes 786440 | tf_op jit(solution)/shard_map/ppermute | solution.py:448
  42.6 16.8 %copy-start = (bf16[1,2048,768]{2,1,0:T(8,128)(2,1)S(1)}, bf16[1,2048,768]{2,1,0:T(8,128)(2,1)}, u32[]{:S(2)}) copy-start(bf16[1,2048,768]{2,1,0:T(8,128)(2,1)} %refs_2_.11) | copy-start | bytes 9437188
  42.6 16.8 %copy-start.1 = (bf16[1,2048,768]{2,1,0:T(8,128)(2,1)S(1)}, bf16[1,2048,768]{2,1,0:T(8,128)(2,1)}, u32[]{:S(2)}) copy-start(bf16[1,2048,768]{2,1,0:T(8,128)(2,1)} %refs_3_.7) | copy-start | bytes 9437188
  42.6 16.8 %copy-start.2 = (bf16[1,768,2048]{2,1,0:T(8,128)(2,1)S(1)}, bf16[1,768,2048]{2,1,0:T(8,128)(2,1)}, u32[]{:S(2)}) copy-start(bf16[1,768,2048]{2,1,0:T(8,128)(2,1)} %refs_4_.9) | copy-start | bytes 9437188
  43.0 7.6 %collective-permute-start.11 = (bf16[64,1152]{1,0:T(8,128)(2,1)S(1)}, bf16[64,1152]{1,0:T(8,128)(2,1)S(1)}, u32[]{:S(2)}, u32[]{:S(2)}) collective-permute-start(bf16[64,1152]{1,0:T(8,128)(2,1)S(1)} %get-tuple-element.53.refs_0_), channel_id=1, source_target_pairs={{0,1},{1,0},{2,3},{3,2},{4,5},{5,4},{6,7},{7,6},{8,9},{9,8},{10,11... | collective-permute-start | bytes 442376 | tf_op jit(solution)/shard_map/ppermute | solution.py:448
  43.1 8.9 %collective-permute-start.10 = (bf16[128,1152]{1,0:T(8,128)(2,1)S(1)}, bf16[128,1152]{1,0:T(8,128)(2,1)S(1)}, u32[]{:S(2)}, u32[]{:S(2)}) collective-permute-start(bf16[128,1152]{1,0:T(8,128)(2,1)S(1)} %get-tuple-element.52), channel_id=1, source_target_pairs={{0,8},{4,12},{8,0},{12,4},{1,9},{5,13},{9,1},{13,5},{2,10},{6,14},... | collective-permute-start | bytes 884744 | tf_op jit(solution)/shard_map/ppermute | solution.py:451
  44.8 14.6 %collective-permute-start.18 = (bf16[128,1024]{1,0:T(8,128)(2,1)S(1)}, bf16[128,1024]{1,0:T(8,128)(2,1)S(1)}, u32[]{:S(2)}, u32[]{:S(2)}) collective-permute-start(bf16[128,1024]{1,0:T(8,128)(2,1)S(1)} %add_convert_fusion.8.refs_8_), channel_id=1, source_target_pairs={{0,2},{1,3},{2,0},{3,1},{4,6},{5,7},{6,4},{7,5},{8,10},{9,11},{10,... | collective-permute-start | bytes 786440 | tf_op jit(solution)/shard_map/ppermute | solution.py:448
  47.2 9.7 %collective-permute-start.13 = (bf16[64,1152]{1,0:T(8,128)(2,1)S(1)}, bf16[64,1152]{1,0:T(8,128)(2,1)S(1)}, u32[]{:S(2)}, u32[]{:S(2)}) collective-permute-start(bf16[64,1152]{1,0:T(8,128)(2,1)S(1)} %get-tuple-element.51.refs_0_), channel_id=1, source_target_pairs={{0,1},{1,0},{2,3},{3,2},{4,5},{5,4},{6,7},{7,6},{8,9},{9,8},{10,11... | collective-permute-start | bytes 442376 | tf_op jit(solution)/shard_map/ppermute | solution.py:448
  52.0 7.3 %collective-permute-start.12 = (bf16[64,1152]{1,0:T(8,128)(2,1)S(1)}, bf16[64,1152]{1,0:T(8,128)(2,1)S(1)}, u32[]{:S(2)}, u32[]{:S(2)}) collective-permute-start(bf16[64,1152]{1,0:T(8,128)(2,1)S(1)} %collective-permute-done.11.refs_1_.refs_0_), channel_id=1, source_target_pairs={{0,8},{4,12},{8,0},{12,4},{1,9},{5,13},{9,1},{13,5},{2,10},{6,14},... | collective-permute-start | bytes 442376 | tf_op jit(solution)/shard_map/ppermute | solution.py:451
  53.5 18.4 %copy-start.3 = (f32[2048]{0:T(1024)S(1)}, f32[2048]{0:T(1024)}, u32[]{:S(2)}) copy-start(f32[2048]{0:T(1024)} %param.16) | copy-start | bytes 24580
  53.6 8.2 %collective-permute-start.20 = (bf16[64,1152]{1,0:T(8,128)(2,1)S(1)}, bf16[64,1152]{1,0:T(8,128)(2,1)S(1)}, u32[]{:S(2)}, u32[]{:S(2)}) collective-permute-start(bf16[64,1152]{1,0:T(8,128)(2,1)S(1)} %slice.72), channel_id=1, source_target_pairs={{0,1},{1,0},{2,3},{3,2},{4,5},{5,4},{6,7},{7,6},{8,9},{9,8},{10,11... | collective-permute-start | bytes 442376 | tf_op jit(solution)/shard_map/ppermute | solution.py:448
  59.5 7.3 %collective-permute-start.19 = (bf16[128,1024]{1,0:T(8,128)(2,1)S(1)}, bf16[128,1024]{1,0:T(8,128)(2,1)S(1)}, u32[]{:S(2)}, u32[]{:S(2)}) collective-permute-start(bf16[128,1024]{1,0:T(8,128)(2,1)S(1)} %get-tuple-element.60), channel_id=1, source_target_pairs={{0,8},{4,12},{8,0},{12,4},{1,9},{5,13},{9,1},{13,5},{2,10},{6,14},... | collective-permute-start | bytes 786440 | tf_op jit(solution)/shard_map/ppermute | solution.py:451
  61.8 5.0 %collective-permute-start.21 = (bf16[64,1024]{1,0:T(8,128)(2,1)S(1)}, bf16[64,1024]{1,0:T(8,128)(2,1)S(1)}, u32[]{:S(2)}, u32[]{:S(2)}) collective-permute-start(bf16[64,1024]{1,0:T(8,128)(2,1)S(1)} %get-tuple-element.62.refs_1_), channel_id=1, source_target_pairs={{0,1},{1,0},{2,3},{3,2},{4,5},{5,4},{6,7},{7,6},{8,9},{9,8},{10,11... | collective-permute-start | bytes 393224 | tf_op jit(solution)/shard_map/ppermute | solution.py:448
  66.7 5.2 %collective-permute-start.23 = (bf16[64,1024]{1,0:T(8,128)(2,1)S(1)}, bf16[64,1024]{1,0:T(8,128)(2,1)S(1)}, u32[]{:S(2)}, u32[]{:S(2)}) collective-permute-start(bf16[64,1024]{1,0:T(8,128)(2,1)S(1)} %get-tuple-element.64.refs_1_), channel_id=1, source_target_pairs={{0,1},{1,0},{2,3},{3,2},{4,5},{5,4},{6,7},{7,6},{8,9},{9,8},{10,11... | collective-permute-start | bytes 393224 | tf_op jit(solution)/shard_map/ppermute | solution.py:448
  66.7 5.2 %collective-permute-start.22 = (bf16[64,1024]{1,0:T(8,128)(2,1)S(1)}, bf16[64,1024]{1,0:T(8,128)(2,1)S(1)}, u32[]{:S(2)}, u32[]{:S(2)}) collective-permute-start(bf16[64,1024]{1,0:T(8,128)(2,1)S(1)} %collective-permute-done.21.refs_1_), channel_id=1, source_target_pairs={{0,8},{4,12},{8,0},{12,4},{1,9},{5,13},{9,1},{13,5},{2,10},{6,14},... | collective-permute-start | bytes 393224 | tf_op jit(solution)/shard_map/ppermute | solution.py:451
  67.5 5.8 %collective-permute-start.25 = (bf16[64,1024]{1,0:T(8,128)(2,1)S(1)}, bf16[64,1024]{1,0:T(8,128)(2,1)S(1)}, u32[]{:S(2)}, u32[]{:S(2)}) collective-permute-start(bf16[64,1024]{1,0:T(8,128)(2,1)S(1)} %slice.73), channel_id=1, source_target_pairs={{0,1},{1,0},{2,3},{3,2},{4,5},{5,4},{6,7},{7,6},{8,9},{9,8},{10,11... | collective-permute-start | bytes 393224 | tf_op jit(solution)/shard_map/ppermute | solution.py:448
  72.8 2.0 %collective-permute-start.24 = (bf16[128,2176]{1,0:T(8,128)(2,1)S(1)}, bf16[128,2176]{1,0:T(8,128)(2,1)S(1)}, u32[]{:S(2)}, u32[]{:S(2)}) collective-permute-start(bf16[128,2176]{1,0:T(8,128)(2,1)S(1)} %shard_map.117.refs_0_), channel_id=1, source_target_pairs={{0,4},{4,0},{8,12},{12,8},{1,5},{5,1},{9,13},{13,9},{2,6},{6,2},{1... | collective-permute-start | bytes 1671176 | tf_op jit(solution)/shard_map/ppermute | solution.py:451
  78.0 2.4 %collective-permute-start.29 = (bf16[128,2048]{1,0:T(8,128)(2,1)S(1)}, bf16[128,2048]{1,0:T(8,128)(2,1)S(1)}, u32[]{:S(2)}, u32[]{:S(2)}) collective-permute-start(bf16[128,2048]{1,0:T(8,128)(2,1)S(1)} %get-tuple-element.72), channel_id=1, source_target_pairs={{0,4},{4,0},{8,12},{12,8},{1,5},{5,1},{9,13},{13,9},{2,6},{6,2},{1... | collective-permute-start | bytes 1572872 | tf_op jit(solution)/shard_map/ppermute | solution.py:451
  78.2 7.2 %collective-permute-start.27 = (bf16[128,2176]{1,0:T(8,128)(2,1)S(1)}, bf16[128,2176]{1,0:T(8,128)(2,1)S(1)}, u32[]{:S(2)}, u32[]{:S(2)}) collective-permute-start(bf16[128,2176]{1,0:T(8,128)(2,1)S(1)} %shard_map.118.refs_0_), channel_id=1, source_target_pairs={{0,4},{4,0},{8,12},{12,8},{1,5},{5,1},{9,13},{13,9},{2,6},{6,2},{1... | collective-permute-start | bytes 1671176 | tf_op jit(solution)/shard_map/ppermute | solution.py:451
  79.4 2.2 %collective-permute-start.28 = (bf16[128,2176]{1,0:T(8,128)(2,1)S(1)}, bf16[128,2176]{1,0:T(8,128)(2,1)S(1)}, u32[]{:S(2)}, u32[]{:S(2)}) collective-permute-start(bf16[128,2176]{1,0:T(8,128)(2,1)S(1)} %shard_map.121.refs_0_), channel_id=1, source_target_pairs={{0,4},{4,0},{8,12},{12,8},{1,5},{5,1},{9,13},{13,9},{2,6},{6,2},{1... | collective-permute-start | bytes 1671176 | tf_op jit(solution)/shard_map/ppermute | solution.py:451
  80.5 8.6 %collective-permute-start.31 = (bf16[64,2048]{1,0:T(8,128)(2,1)S(1)}, bf16[64,2048]{1,0:T(8,128)(2,1)S(1)}, u32[]{:S(2)}, u32[]{:S(2)}) collective-permute-start(bf16[64,2048]{1,0:T(8,128)(2,1)S(1)} %add_convert_fusion.7), channel_id=1, source_target_pairs={{0,8},{4,12},{8,0},{12,4},{1,9},{5,13},{9,1},{13,5},{2,10},{6,14},... | collective-permute-start | bytes 786440 | tf_op jit(solution)/shard_map/ppermute | solution.py:451
  84.8 6.3 %collective-permute-start.30 = (bf16[128,2048]{1,0:T(8,128)(2,1)S(1)}, bf16[128,2048]{1,0:T(8,128)(2,1)S(1)}, u32[]{:S(2)}, u32[]{:S(2)}) collective-permute-start(bf16[128,2048]{1,0:T(8,128)(2,1)S(1)} %get-tuple-element.80), channel_id=1, source_target_pairs={{0,4},{4,0},{8,12},{12,8},{1,5},{5,1},{9,13},{13,9},{2,6},{6,2},{1... | collective-permute-start | bytes 1572872 | tf_op jit(solution)/shard_map/ppermute | solution.py:451
  85.0 8.4 %collective-permute-start.26 = (bf16[128,2176]{1,0:T(8,128)(2,1)S(1)}, bf16[128,2176]{1,0:T(8,128)(2,1)S(1)}, u32[]{:S(2)}, u32[]{:S(2)}) collective-permute-start(bf16[128,2176]{1,0:T(8,128)(2,1)S(1)} %get-tuple-element.82.refs_0_), channel_id=1, source_target_pairs={{0,4},{4,0},{8,12},{12,8},{1,5},{5,1},{9,13},{13,9},{2,6},{6,2},{1... | collective-permute-start | bytes 1671176 | tf_op jit(solution)/shard_map/ppermute | solution.py:451
  88.8 3.3 %collective-permute-start.34 = (bf16[128,2048]{1,0:T(8,128)(2,1)S(1)}, bf16[128,2048]{1,0:T(8,128)(2,1)S(1)}, u32[]{:S(2)}, u32[]{:S(2)}) collective-permute-start(bf16[128,2048]{1,0:T(8,128)(2,1)S(1)} %get-tuple-element.87), channel_id=1, source_target_pairs={{0,4},{4,0},{8,12},{12,8},{1,5},{5,1},{9,13},{13,9},{2,6},{6,2},{1... | collective-permute-start | bytes 1572872 | tf_op jit(solution)/shard_map/ppermute | solution.py:451
  89.3 11.2 %collective-permute-start.38 = (bf16[64,2048]{1,0:T(8,128)(2,1)S(1)}, bf16[64,2048]{1,0:T(8,128)(2,1)S(1)}, u32[]{:S(2)}, u32[]{:S(2)}) collective-permute-start(bf16[64,2048]{1,0:T(8,128)(2,1)S(1)} %add_convert_fusion.2), channel_id=1, source_target_pairs={{0,1},{1,0},{2,3},{3,2},{4,5},{5,4},{6,7},{7,6},{8,9},{9,8},{10,11... | collective-permute-start | bytes 786440 | tf_op jit(solution)/shard_map/ppermute | solution.py:448
  91.2 9.2 %collective-permute-start.32 = (bf16[64,2048]{1,0:T(8,128)(2,1)S(1)}, bf16[64,2048]{1,0:T(8,128)(2,1)S(1)}, u32[]{:S(2)}, u32[]{:S(2)}) collective-permute-start(bf16[64,2048]{1,0:T(8,128)(2,1)S(1)} %add_convert_fusion.6), channel_id=1, source_target_pairs={{0,8},{4,12},{8,0},{12,4},{1,9},{5,13},{9,1},{13,5},{2,10},{6,14},... | collective-permute-start | bytes 786440 | tf_op jit(solution)/shard_map/ppermute | solution.py:451
  92.1 12.9 %collective-permute-start.36 = (bf16[64,2048]{1,0:T(8,128)(2,1)S(1)}, bf16[64,2048]{1,0:T(8,128)(2,1)S(1)}, u32[]{:S(2)}, u32[]{:S(2)}) collective-permute-start(bf16[64,2048]{1,0:T(8,128)(2,1)S(1)} %add_convert_fusion.4), channel_id=1, source_target_pairs={{0,8},{4,12},{8,0},{12,4},{1,9},{5,13},{9,1},{13,5},{2,10},{6,14},... | collective-permute-start | bytes 786440 | tf_op jit(solution)/shard_map/ppermute | solution.py:451
  100.4 5.0 %collective-permute-start.33 = (bf16[128,2048]{1,0:T(8,128)(2,1)S(1)}, bf16[128,2048]{1,0:T(8,128)(2,1)S(1)}, u32[]{:S(2)}, u32[]{:S(2)}) collective-permute-start(bf16[128,2048]{1,0:T(8,128)(2,1)S(1)} %get-tuple-element.86), channel_id=1, source_target_pairs={{0,4},{4,0},{8,12},{12,8},{1,5},{5,1},{9,13},{13,9},{2,6},{6,2},{1... | collective-permute-start | bytes 1572872 | tf_op jit(solution)/shard_map/ppermute | solution.py:451
  100.6 15.1 %collective-permute-start.39 = (bf16[64,2048]{1,0:T(8,128)(2,1)S(1)}, bf16[64,2048]{1,0:T(8,128)(2,1)S(1)}, u32[]{:S(2)}, u32[]{:S(2)}) collective-permute-start(bf16[64,2048]{1,0:T(8,128)(2,1)S(1)} %add_convert_fusion.1), channel_id=1, source_target_pairs={{0,2},{1,3},{2,0},{3,1},{4,6},{5,7},{6,4},{7,5},{8,10},{9,11},{10,... | collective-permute-start | bytes 786440 | tf_op jit(solution)/shard_map/ppermute | solution.py:448
  105.1 12.8 %collective-permute-start.37 = (bf16[64,2048]{1,0:T(8,128)(2,1)S(1)}, bf16[64,2048]{1,0:T(8,128)(2,1)S(1)}, u32[]{:S(2)}, u32[]{:S(2)}) collective-permute-start(bf16[64,2048]{1,0:T(8,128)(2,1)S(1)} %add_convert_fusion.3), channel_id=1, source_target_pairs={{0,1},{1,0},{2,3},{3,2},{4,5},{5,4},{6,7},{7,6},{8,9},{9,8},{10,11... | collective-permute-start | bytes 786440 | tf_op jit(solution)/shard_map/ppermute | solution.py:448
  105.5 12.4 %collective-permute-start.35 = (bf16[64,2048]{1,0:T(8,128)(2,1)S(1)}, bf16[64,2048]{1,0:T(8,128)(2,1)S(1)}, u32[]{:S(2)}, u32[]{:S(2)}) collective-permute-start(bf16[64,2048]{1,0:T(8,128)(2,1)S(1)} %add_convert_fusion.5), channel_id=1, source_target_pairs={{0,8},{4,12},{8,0},{12,4},{1,9},{5,13},{9,1},{13,5},{2,10},{6,14},... | collective-permute-start | bytes 786440 | tf_op jit(solution)/shard_map/ppermute | solution.py:451
  (2 other events, 2.6 us)
